TPU v7x, 128 devices: a whole 4x4x4 slice. The times are simulated.
128 devices in a mesh: row: 8 (over x, core), col: 8 (over z_lo, y), batch: 2 (over z_hi).
Axes of the slice: x: 4, y: 4, z: 4 (z_hi: 2, z_lo: 2; z = z_hi * 2 + z_lo), core: 2. Of those that a mesh axis runs over, the one named last changes fastest.
Arguments:
- syndromes: int32 [512, 1024], P(('batch', 'row'), 'col'), parts along dimension 0, may hold values from 0 to 65535
- embedding: bfloat16 [64, 16], replicated, may hold values from -1.5 to 1.5
- kernel_first: bfloat16 [3, 3, 64, 64], replicated, may hold values from -0.25 to 0.25
- kernel_second: bfloat16 [3, 3, 128, 64], replicated, may hold values from -0.25 to 0.25
- kernel_bottom: bfloat16 [3, 3, 256, 128], replicated, may hold values from -0.1875 to 0.1875
- kernel_return: bfloat16 [3, 3, 128, 256], replicated, may hold values from -0.125 to 0.125
- kernel_final: bfloat16 [3, 3, 64, 128], replicated, may hold values from -0.1875 to 0.1875
- readout: bfloat16 [2, 64], replicated, may hold values from -0.75 to 0.75
- cotangent: bfloat16 [2, 512, 1024], P(None, ('batch', 'row'), 'col'), parts along dimension 1, may hold values from -6 to 6
Outputs:
- logits: float32 [2, 512, 1024], P(None, ('batch', 'row'), 'col'), parts along dimension 1
- feature_grad: bfloat16 [64, 512, 1024], P(None, ('batch', 'row'), 'col'), parts along dimension 1
- embedding_grad: float32 [128, 16], P('batch'), parts along dimension 0
- first_grad: float32 [6, 3, 64, 64], P('batch'), parts along dimension 0
- second_grad: float32 [6, 3, 128, 64], P('batch'), parts along dimension 0
- bottom_grad: float32 [6, 3, 256, 128], P('batch'), parts along dimension 0
- return_grad: float32 [6, 3, 128, 256], P('batch'), parts along dimension 0
- final_grad: float32 [6, 3, 64, 128], P('batch'), parts along dimension 0
- readout_grad: float32 [4, 64], P('batch'), parts along dimension 0
There are 2 independent parts, one for each index of `batch`. A program takes and returns all parts, laid end to end along the dimension named above; an argument that names none is the same for every part. Nothing has to cross between parts.
All inputs are finite; a program needn't handle non-finite values.
Results may differ from a plain program's by a relative error of at most 0.038.
Values may be sent and summed in bfloat16 or wider, within the bound.
A program may use at most 64 MiB of HBM per device.

v0:
```python
import functools

import jax
import jax.numpy as jnp
import numpy as np
from jax import lax
from jax.experimental import pallas as pl
from jax.experimental.pallas import tpu as pltpu
from jax.sharding import PartitionSpec as P

BF, F32 = jnp.bfloat16, jnp.float32
MESH = pl.DeviceIdType.MESH

DEEP, WIDE = 8, 32
CELLS = DEEP * WIDE

ROWS = 6144
HALF = ROWS // 2
PART = HALF // 2
CHUNK = PART // 4
SUB = CHUNK // 4
LEAF = SUB // 2

AT_RETURN, AT_BOTTOM, AT_FINAL, AT_SECOND, AT_FIRST, AT_READ = 0, 2304, 4608, 5184, 5824, 6080


def ranged(values, start, size, unit=16):
    return values.at[pl.ds(pl.multiple_of(start, unit), size), :]


def shift_table():
    table = {}
    for dr in (-1, 0, 1):
        for dc in (-1, 0, 1):
            m = np.zeros((CELLS, CELLS), np.float32)
            for r in range(DEEP):
                for q in range(WIDE):
                    if 0 <= r + dr < DEEP and 0 <= q + dc < WIDE:
                        m[(r + dr) * WIDE + q + dc, r * WIDE + q] = 1
            table[dr, dc] = m
    return table


def gather_tables():
    blocks, where = [], {}

    def put(name, m):
        where[name] = len(blocks)
        blocks.append(m)

    for b in range(4):
        for name, r in (("up", 0), ("down", DEEP - 1)):
            m = np.zeros((CELLS, 128), np.float32)
            for q in range(WIDE):
                m[r * WIDE + q, b * WIDE + q] = 1
            put((name, b), m)
    for p in (4, 2, 1):
        for a in range(p):
            for name, q, base, corners in (("left", 0, 0, (64, 66)), ("right", WIDE - 1, 32, (65, 67))):
                m = np.zeros((CELLS, 128), np.float32)
                for r in range(DEEP):
                    m[r * WIDE + q, base + a * DEEP + r] = 1
                if a == 0:
                    m[q, corners[0]] = 1
                if a == p - 1:
                    m[(DEEP - 1) * WIDE + q, corners[1]] = 1
                put((name, p, a), m)
    return np.concatenate(blocks), where


def halo_tables():
    blocks, where = [], {}
    for p in (4, 2, 1):
        for ea in range(p + 2):
            for eb in range(p + 2):
                dr, dc = (ea > p) - (ea < 1), (eb > p) - (eb < 1)
                if (dr, dc) == (0, 0):
                    continue
                sa, sb = (ea - 1) % p, (eb - 1) % p
                m = np.zeros((3, 128, CELLS), np.float32)
                for r in range(DEEP):
                    for q in range(WIDE):
                        rr, qq = r + dr, q + dc
                        row_in, col_in = 0 <= rr < DEEP, 0 <= qq < WIDE
                        if row_in and col_in:
                            continue
                        if col_in:
                            tile, lane = (0 if rr < 0 else 1), sb * WIDE + qq
                        elif row_in:
                            tile, lane = 2, (32 if qq < 0 else 0) + sa * DEEP + rr
                        else:
                            tile, lane = 2, {(-1, -1): 67, (-1, 1): 66, (1, -1): 65, (1, 1): 64}[dr, dc]
                        m[tile, lane, r * WIDE + q] = 1
                used = []
                for tile in range(3):
                    if m[tile].any():
                        used.append((tile, len(blocks)))
                        blocks.append(m[tile])
                where[p, ea, eb] = used
    return np.concatenate(blocks), where


def spread_table():
    m = np.zeros((512, 512), np.float32)
    for r in range(4):
        for w in range(128):
            m[r * 128 + w, (w % 4) * 128 + r * WIDE + w // 4] = 1
    return m


SHIFTS = shift_table()
SHIFT_AT = {key: n for n, key in enumerate(SHIFTS)}
SHIFT_ALL = np.concatenate(list(SHIFTS.values()))
GATHER_ALL, GATHER_AT = gather_tables()
HALO_ALL, HALO_AT = halo_tables()
SPREAD = spread_table()

UNDER = (((0,), (1, 2)), ((0, 1), (2,)))
OVER = ((2,), (1, 2), (0, 1), (0,))
BASE = (0, 1, 1, 2)


def mm(a, b):
    return jnp.dot(a, b, preferred_element_type=F32)


def nt(a, b):
    return lax.dot_general(a, b, (((1,), (1,)), ((), ())), preferred_element_type=F32)


def logistic(z):
    return 0.5 + 0.5 * jnp.tanh(0.5 * z)


def activated(v):
    stored = v.astype(BF)
    z = stored.astype(F32)
    return stored, (z * logistic(z)).astype(BF)


def sloped(incoming, stored):
    z = stored.astype(F32)
    s = logistic(z)
    return (incoming * (s * (1.0 + z * (1.0 - s)))).astype(BF)


def remote(src, dst, send, recv, target):
    return pltpu.make_async_remote_copy(
        src_ref=src, dst_ref=dst, send_sem=send, recv_sem=recv, device_id=target, device_id_type=MESH
    )


SIDES = ((-1, 0), (1, 0), (0, -1), (0, 1), (-1, -1), (-1, 1), (1, -1), (1, 1))
SLOT = {(-1, 0): 0, (1, 0): 1, (0, -1): 2, (0, 1): 3, (-1, -1): 4, (-1, 1): 5, (1, -1): 6, (1, 1): 7}


def net_kernel(counts, *refs):
    it = iter(refs)

    def take(n):
        return [next(it) for _ in range(n)]

    syn, emb, k1, k2, k3, k4, k5, rdo, cot, cS, cG, cT, cU, cV = take(14)
    logits_ref, fg_ref, g_ref = take(3)
    xb, e0, z0, z1, f1, e1, z2, f2, e2, z3, e3, z4, e4, z5, f5, t5, t4, t3, t2, t1, fg, cp = take(22)
    w0, w1, w1b, w2, w2b, w3, w3b, w4, w4b, w5, w5b, r4, r4t = take(13)
    halos = [take(2) for _ in range(10)]
    sends, recvs = take(2)

    n_row, n_col = counts
    row, col = lax.axis_index("row"), lax.axis_index("col")
    there = {
        (-1, 0): row > 0,
        (1, 0): row < n_row - 1,
        (0, -1): col > 0,
        (0, 1): col < n_col - 1,
    }
    for dr in (-1, 1):
        for dc in (-1, 1):
            there[dr, dc] = jnp.logical_and(there[dr, 0], there[0, dc])

    def place(dr, dc):
        return {"row": (row + dr + n_row) % n_row, "col": (col + dc + n_col) % n_col}

    barrier = pltpu.get_barrier_semaphore()
    for side in SIDES:
        pl.semaphore_signal(barrier, inc=1, device_id=place(*side), device_id_type=MESH)
    pl.semaphore_wait(barrier, len(SIDES))

    def shift(dr, dc):
        n = SHIFT_AT[dr, dc]
        return cS[n * CELLS : (n + 1) * CELLS, :]

    def gather(*name):
        n = GATHER_AT[name]
        return cG[n * CELLS : (n + 1) * CELLS, :]

    lane = lax.broadcasted_iota(jnp.int32, (1, 128), 1)

    def begin(n, p, width, ref):
        out, into = halos[n]

        def phase(a, b):
            start = ((a + 1) * (p + 2) + b + 1) * width
            return ref[start : start + width, :]

        out[0] = sum(mm(phase(0, b), gather("up", b)) for b in range(p)).astype(BF)
        out[1] = sum(mm(phase(p - 1, b), gather("down", b)) for b in range(p)).astype(BF)
        out[2] = sum(
            mm(phase(a, 0), gather("left", p, a)) + mm(phase(a, p - 1), gather("right", p, a)) for a in range(p)
        ).astype(BF)
        copies = []
        for k, (dr, dc) in enumerate(SIDES):
            src = out.at[(0 if dr < 0 else 1) if dc == 0 else 2]
            slot = SLOT[-dr, -dc]
            copies.append(remote(src, into.at[slot], sends.at[n, slot], recvs.at[n, slot], place(dr, dc)))
        for copy in copies:
            copy.start()
        return copies

    def end(n, p, width, ref, copies):
        into = halos[n][1]
        for copy in copies:
            copy.wait()

        def got(side, low=0, high=128):
            keep = jnp.logical_and(jnp.logical_and(lane >= low, lane < high), there[side])
            return jnp.where(keep, into[SLOT[side]].astype(F32), 0.0)

        third = got((0, 1), 0, 32) + got((0, -1), 32, 64)
        for k, side in enumerate(((1, 1), (1, -1), (-1, 1), (-1, -1))):
            third = third + got(side, 64 + k, 65 + k)
        tiles = [got((-1, 0)).astype(BF), got((1, 0)).astype(BF), third.astype(BF)]
        for ea in range(p + 2):
            for eb in range(p + 2):
                dr, dc = (ea > p) - (ea < 1), (eb > p) - (eb < 1)
                if (dr, dc) == (0, 0):
                    continue
                start = (((ea - 1) % p + 1) * (p + 2) + (eb - 1) % p + 1) * width
                moved = mm(ref[start : start + width, :], shift(dr, dc))
                for tile, block in HALO_AT[p, ea, eb]:
                    moved = moved + mm(tiles[tile], cT[block * 128 : (block + 1) * 128, :])
                start = (ea * (p + 2) + eb) * width
                ref[start : start + width, :] = moved.astype(BF)

    bit = lax.broadcasted_iota(jnp.int32, (16, 1), 0)
    groups = []
    for a in range(4):
        for t in range(2):
            line = [(syn[16 * t + 4 * r + a : 16 * t + 4 * r + a + 1, :] >> bit) & 1 for r in range(4)]
            groups.append(jnp.concatenate(line, axis=1))
    bits = jnp.concatenate(groups, axis=0).astype(F32).astype(BF)
    phased = mm(bits, cU[...]).astype(BF)
    for a in range(4):
        for t in range(2):
            for b in range(4):
                start = ((a + 1) * 6 + b + 1) * 16
                xb[start : start + 16, t * 128 : (t + 1) * 128] = phased[(a * 2 + t) * 16 : (a * 2 + t + 1) * 16, b * 128 : (b + 1) * 128]
    copies = begin(0, 4, 16, xb)

    eye = shift(0, 0)
    repeat = (lax.broadcasted_iota(jnp.int32, (16, 96), 1) % 16 == lax.broadcasted_iota(jnp.int32, (16, 96), 0)).astype(F32).astype(BF)
    tiled = mm(emb[...], repeat)
    own = lax.broadcasted_iota(jnp.int32, (64, 96), 1) // 16
    for j in range(6):
        w0[j * 64 : (j + 1) * 64, :] = jnp.where(own == j, tiled, 0.0).astype(BF)
    for ta in range(3):
        for i in range(2):
            w1[i * 64 : (i + 1) * 64, ta * 256 : (ta + 1) * 256] = sum(
                mm(k1[ta, tb], eye[(tb + i) * 64 : (tb + i + 1) * 64, :]) for tb in range(3)
            ).astype(BF)
            w2[i * 128 : (i + 1) * 128, ta * 256 : (ta + 1) * 256] = sum(
                mm(k2[ta, tb], eye[(tb + i) * 64 : (tb + i + 1) * 64, :]) for tb in range(3)
            ).astype(BF)
            blank = [jnp.zeros((64, 64), BF)]
            line = [k1[2 - ta, 2 - tb] for tb in range(3)]
            line = line + blank if i == 0 else blank + line
            w1b[i * 64 : (i + 1) * 64, ta * 256 : (ta + 1) * 256] = nt(eye[:64, :64], jnp.concatenate(line, axis=0)).astype(BF)
            blank = [jnp.zeros((128, 64), BF)]
            line = [k2[2 - ta, 2 - tb] for tb in range(3)]
            line = line + blank if i == 0 else blank + line
            w2b[i * 64 : (i + 1) * 64, ta * 512 : (ta + 1) * 512] = nt(eye[:64, :64], jnp.concatenate(line, axis=0)).astype(BF)
    for t in range(9):
        w3[:, t * 128 : (t + 1) * 128] = k3[t // 3, t % 3]
        w3b[:, t * 256 : (t + 1) * 256] = nt(eye[:128, :128], k3[2 - t // 3, 2 - t % 3]).astype(BF)

    def added(k, rows, cols):
        return sum(k[ta, tb].astype(F32) for ta in rows for tb in cols).astype(BF)

    for pa in range(2):
        for pb in range(2):
            for s in range(2):
                for u in range(2):
                    block = added(k4, UNDER[pa][s], UNDER[pb][u])
                    w4[(pa * 2 + pb) * 128 : (pa * 2 + pb + 1) * 128, (s * 2 + u) * 256 : (s * 2 + u + 1) * 256] = block
                    at = OVER.index(UNDER[pa][s]) * 4 + OVER.index(UNDER[pb][u])
                    w4b[:, at * 128 : (at + 1) * 128] = nt(eye, block).astype(BF)
                    start = pa * 128 + (1 - pb) * 64
                    w5[start : start + 64, (s * 2 + u) * 128 : (s * 2 + u + 1) * 128] = added(k5, UNDER[pa][s], UNDER[pb][u])
    for ea in range(4):
        for pair in range(2):
            stack = jnp.concatenate([added(k5, OVER[ea], OVER[2 * pair + i]) for i in range(2)], axis=0)
            at = ea * 2 + pair
            w5b[:, at * 128 : (at + 1) * 128] = nt(eye[:128, :128], stack).astype(BF)

    repeat = (lax.broadcasted_iota(jnp.int32, (64, 256), 1) % 64 == lax.broadcasted_iota(jnp.int32, (64, 256), 0)).astype(F32).astype(BF)
    tiled = mm(rdo[...], repeat)
    tiled = jnp.concatenate([tiled, jnp.zeros((2, 256), F32)] * 4, axis=0)
    own = lax.broadcasted_iota(jnp.int32, (16, 256), 1) // 64 == lax.broadcasted_iota(jnp.int32, (16, 256), 0) // 4
    r4[...] = jnp.where(own, tiled, 0.0).astype(BF)
    r4t[...] = nt(eye, r4[...]).astype(BF)

    wide = cot[...].astype(F32)
    groups = []
    for a in range(4):
        for t in range(2):
            line = jnp.concatenate([wide[:, 16 * t + 4 * r + a, :] for r in range(4)], axis=1)
            groups.append(jnp.concatenate([line, jnp.zeros((6, 512), F32)], axis=0))
    phased = mm(jnp.concatenate(groups, axis=0).astype(BF), cU[...])
    for a in range(4):
        for t in range(2):
            start = (a * 2 + t) * 8
            pieces = [phased[start : start + 4, b * 128 : (b + 1) * 128] for b in range(4)]
            cp[a * 16 : (a + 1) * 16, t * 128 : (t + 1) * 128] = jnp.concatenate(pieces, axis=0).astype(BF)

    end(0, 4, 16, xb, copies)

    for ea in range(6):
        stored, active = activated(mm(w0[...], xb[ea * 96 : (ea + 1) * 96, :]))
        e0[ea * 384 : (ea + 1) * 384, :] = active
        if 1 <= ea <= 4:
            z0[(ea - 1) * 256 : ea * 256, :] = stored[64:320, :]

    for a in range(4):
        for pair in range(2):
            v = sum(
                mm(w1[:, ta * 256 : (ta + 1) * 256], e0[((a + ta) * 6 + 2 * pair) * 64 : ((a + ta) * 6 + 2 * pair + 4) * 64, :])
                for ta in range(3)
            )
            start = (a * 4 + 2 * pair) * 64
            z1[start : start + 128, :], f1[start : start + 128, :] = activated(v)

    def pooled(ref, side, width, a, b):
        spots = [((2 * a + i) * side + 2 * b + j) * width for i in range(2) for j in range(2)]
        return (sum(ref[s : s + width, :].astype(F32) for s in spots) * 0.25).astype(BF)

    for a in range(2):
        for b in range(2):
            start = ((a + 1) * 4 + b + 1) * 64
            e1[start : start + 64, :] = pooled(f1, 4, 64, a, b)
    end(1, 2, 64, e1, begin(1, 2, 64, e1))

    for a in range(2):
        v = sum(mm(w2[:, ta * 256 : (ta + 1) * 256], e1[(a + ta) * 256 : (a + ta + 1) * 256, :]) for ta in range(3))
        z2[a * 256 : (a + 1) * 256, :], f2[a * 256 : (a + 1) * 256, :] = activated(v)
    e2[4 * 128 : 5 * 128, :] = pooled(f2, 2, 128, 0, 0)
    end(2, 1, 128, e2, begin(2, 1, 128, e2))

    z3[...], e3[4 * 256 : 5 * 256, :] = activated(mm(w3[...], e2[...]))
    end(3, 1, 256, e3, begin(3, 1, 256, e3))

    for a in range(2):
        for b in range(2):
            n = a * 2 + b
            v = sum(
                mm(w4[n * 128 : (n + 1) * 128, s * 512 : (s + 1) * 512], e3[((a + s) * 3 + b) * 256 : ((a + s) * 3 + b + 2) * 256, :])
                for s in range(2)
            )
            v = v + f2[n * 128 : (n + 1) * 128, :].astype(F32)
            start = ((a + 1) * 4 + b + 1) * 128
            z4[n * 128 : (n + 1) * 128, :], e4[start : start + 128, :] = activated(v)
    end(4, 2, 128, e4, begin(4, 2, 128, e4))

    RUNS = ((0, 1, 64, 64), (1, 2, 0, 128), (3, 1, 0, 64))
    for a in range(4):
        for b, many, first, size in RUNS:
            base = (a % 2) * 128 + first
            v = sum(
                mm(w5[base : base + size, s * 256 : (s + 1) * 256], e4[((BASE[a] + s) * 4 + BASE[b]) * 128 : ((BASE[a] + s) * 4 + BASE[b] + 2) * 128, :])
                for s in range(2)
            )
            start = (a * 4 + b) * 64
            v = v + f1[start : start + size, :].astype(F32)
            z5[start : start + size, :], f5[start : start + size, :] = activated(v)

    for a in range(4):
        back = mm(r4t[...], cp[a * 16 : (a + 1) * 16, :])
        start = ((a + 1) * 6 + 1) * 64
        t5[start : start + 256, :] = sloped(back, z5[a * 256 : (a + 1) * 256, :])
    copies = begin(5, 4, 64, t5)

    groups = []
    total = jnp.zeros((16, 256), F32)
    for a in range(4):
        here = f5[a * 256 : (a + 1) * 256, :]
        value = mm(r4[...], here)
        total = total + nt(cp[a * 16 : (a + 1) * 16, :], here)
        for t in range(2):
            groups.append(jnp.concatenate([value[b * 4 : (b + 1) * 4, t * 128 : (t + 1) * 128] for b in range(4)], axis=1))
    value = jnp.concatenate(groups, axis=0)
    laid = 0.0
    for _ in range(3):
        piece = value.astype(BF)
        laid = laid + mm(piece, cV[...])
        value = value - piece.astype(F32)
    for a in range(4):
        for t in range(2):
            for r in range(4):
                h = 16 * t + 4 * r + a
                logits_ref[:, h * 128 : (h + 1) * 128] = laid[(a * 2 + t) * 4 : (a * 2 + t + 1) * 4, r * 128 : (r + 1) * 128]
    total = sum(total[b * 4 : (b + 1) * 4, b * 64 : (b + 1) * 64] for b in range(4))
    g_ref[AT_READ : AT_READ + 64, :] = jnp.zeros((64, 128), F32)
    g_ref[AT_READ : AT_READ + 4, 0:64] = total

    sums = {}
    for a in range(4):
        for s in range(2):
            for b, many, first, size in RUNS:
                start = ((BASE[a] + s) * 4 + BASE[b]) * 128
                t_start = ((a + 1) * 6 + b + 1) * 64
                product = nt(t5[t_start : t_start + size, :], e4[start : start + 256, :])
                for m in range(many):
                    key = (a % 2, s, (b + m) % 2)
                    block = product[m * 64 : (m + 1) * 64, :]
                    sums[key] = sums[key] + block if key in sums else block

    def reads(parity, tap):
        return 0 if tap in UNDER[parity][0] else 1

    for ta in range(3):
        rowed = [sums[0, reads(0, ta), pb] + sums[1, reads(1, ta), pb] for pb in range(2)]
        for tb in range(3):
            value = sum(rowed[pb][:, reads(pb, tb) * 128 : (reads(pb, tb) + 1) * 128] for pb in range(2))
            start = AT_FINAL + (ta * 3 + tb) * 64
            g_ref[start : start + 64, :] = value

    end(5, 4, 64, t5, copies)
    for a in range(2):
        for b in range(2):
            v = sum(
                mm(w5b[:, m * 256 : (m + 1) * 256], t5[((2 * a + m) * 6 + 2 * b) * 64 : ((2 * a + m) * 6 + 2 * b + 4) * 64, :])
                for m in range(4)
            )
            start = ((a + 1) * 4 + b + 1) * 128
            n = a * 2 + b
            t4[start : start + 128, :] = sloped(v, z4[n * 128 : (n + 1) * 128, :])
    copies = begin(6, 2, 128, t4)

    for b in range(2):
        for u in range(2):
            parts = {}
            for a in range(2):
                for s in range(2):
                    start = ((a + 1) * 4 + b + 1) * 128
                    from_ = ((a + s) * 3 + b + u) * 256
                    parts[a, s] = nt(t4[start : start + 128, :], e3[from_ : from_ + 256, :])
            for ta in range(3):
                value = parts[0, reads(0, ta)] + parts[1, reads(1, ta)]
                for tb in UNDER[b][u]:
                    for half in range(2):
                        start = AT_RETURN + ((ta * 3 + tb) * 2 + half) * 128
                        piece = value[:, half * 128 : (half + 1) * 128]
                        g_ref[start : start + 128, :] = piece if b == 0 else g_ref[start : start + 128, :] + piece

    end(6, 2, 128, t4, copies)
    v = sum(mm(w4b[:, m * 512 : (m + 1) * 512], t4[m * 512 : (m + 1) * 512, :]) for m in range(4))
    t3[4 * 256 : 5 * 256, :] = sloped(v, z3[...])
    copies = begin(7, 1, 256, t3)
    for t in range(9):
        g_ref[AT_BOTTOM + t * 256 : AT_BOTTOM + (t + 1) * 256, :] = nt(t3[4 * 256 : 5 * 256, :], e2[t * 128 : (t + 1) * 128, :])
    end(7, 1, 256, t3, copies)

    through = mm(w3b[...], t3[...]) * 0.25
    for a in range(2):
        for b in range(2):
            n = a * 2 + b
            start = ((a + 1) * 4 + b + 1) * 128
            t2[start : start + 128, :] = sloped(t4[start : start + 128, :].astype(F32) + through, z2[n * 128 : (n + 1) * 128, :])
    copies = begin(8, 2, 128, t2)
    ends = []
    for ta in range(3):
        product = 0.0
        for a in range(2):
            start = ((a + 1) * 4 + 1) * 128
            product = product + nt(t2[start : start + 256, :], e1[(a + ta) * 256 : (a + ta + 1) * 256, :])
        value = product[0:128, 0:192] + product[128:256, 64:256]
        g_ref[AT_SECOND + ta * 128 : AT_SECOND + (ta + 1) * 128, :] = value[:, 0:128]
        ends.append(value[:, 128:192])
    g_ref[AT_SECOND + 384 : AT_SECOND + 512, :] = jnp.concatenate(ends[:2], axis=1)
    g_ref[AT_SECOND + 512 : AT_SECOND + 640, 0:64] = ends[2]
    end(8, 2, 128, t2, copies)

    for a in range(2):
        v = sum(mm(w2b[:, ta * 512 : (ta + 1) * 512], t2[(a + ta) * 512 : (a + ta + 1) * 512, :]) for ta in range(3)) * 0.25
        for b in range(2):
            for i in range(2):
                for j in range(2):
                    fa, fb = 2 * a + i, 2 * b + j
                    start = ((fa + 1) * 6 + fb + 1) * 64
                    n = (fa * 4 + fb) * 64
                    t1[start : start + 64, :] = sloped(t5[start : start + 64, :].astype(F32) + v[b * 64 : (b + 1) * 64, :], z1[n : n + 64, :])
    copies = begin(9, 4, 64, t1)
    for ta in range(3):
        product = 0.0
        for a in range(4):
            for pair in range(2):
                start = ((a + 1) * 6 + 2 * pair + 1) * 64
                from_ = ((a + ta) * 6 + 2 * pair) * 64
                product = product + nt(t1[start : start + 128, :], e0[from_ : from_ + 256, :])
        value = product[0:64, 0:192] + product[64:128, 64:256]
        g_ref[AT_FIRST + ta * 64 : AT_FIRST + (ta + 1) * 64, :] = value[:, 0:128]
        if ta < 2:
            g_ref[AT_SECOND + 512 + ta * 64 : AT_SECOND + 512 + (ta + 1) * 64, 64:128] = value[:, 128:192]
        else:
            g_ref[AT_FIRST + 192 : AT_FIRST + 256, 64:128] = value[:, 128:192]
    end(9, 4, 64, t1, copies)

    total = jnp.zeros((256, 64), F32)
    for a in range(4):
        for pair in range(2):
            v = sum(
                mm(w1b[:, ta * 256 : (ta + 1) * 256], t1[((a + ta) * 6 + 2 * pair) * 64 : ((a + ta) * 6 + 2 * pair + 4) * 64, :])
                for ta in range(3)
            )
            start = (a * 4 + 2 * pair) * 64
            fg[start : start + 128, :] = sloped(v, z0[start : start + 128, :])
        start = ((a + 1) * 6 + 1) * 16
        total = total + nt(fg[a * 256 : (a + 1) * 256, :], xb[start : start + 64, :])
    total = sum(total[b * 64 : (b + 1) * 64, b * 16 : (b + 1) * 16] for b in range(4))
    g_ref[AT_FIRST + 192 : AT_FIRST + 256, 0:16] = total
    g_ref[AT_FIRST + 192 : AT_FIRST + 256, 16:64] = jnp.zeros((64, 48), F32)

    for a in range(4):
        for t in range(2):
            line = jnp.concatenate([fg[(a * 4 + b) * 64 : (a * 4 + b + 1) * 64, t * 128 : (t + 1) * 128] for b in range(4)], axis=1)
            laid = mm(line, cV[...]).astype(BF)
            for r in range(4):
                h = 16 * t + 4 * r + a
                fg_ref[:, h * 128 : (h + 1) * 128] = laid[:, r * 128 : (r + 1) * 128]


LEVELS = ((4, 16), (2, 64), (1, 128), (1, 256), (2, 128), (4, 64), (2, 128), (1, 256), (2, 128), (4, 64))


def run_net(counts, *args):
    tables = [jnp.asarray(t, BF) for t in (SHIFT_ALL, GATHER_ALL, HALO_ALL, SPREAD, SPREAD.T)]
    blocks = [16 * 36, 64 * 36, 1024, 1024, 1024, 64 * 16, 512, 512, 128 * 9, 256, 256 * 9, 512, 128 * 16, 1024, 1024]
    blocks += [64 * 36, 128 * 16, 256 * 9, 128 * 16, 64 * 36, 1024, 64]
    weights = [(384, 96), (128, 768), (128, 768), (256, 768), (128, 1536), (256, 1152), (128, 2304), (512, 1024), (256, 2048), (256, 512), (128, 1024), (16, 256), (256, 16)]
    scratch = [pltpu.VMEM((n, CELLS), BF) for n in blocks] + [pltpu.VMEM(s, BF) for s in weights]
    for _, width in LEVELS:
        scratch += [pltpu.VMEM((3, width, 128), BF), pltpu.VMEM((8, width, 128), BF)]
    scratch += [pltpu.SemaphoreType.DMA((10, 8)), pltpu.SemaphoreType.DMA((10, 8))]
    vmem = pl.BlockSpec(memory_space=pltpu.VMEM)
    return pl.pallas_call(
        functools.partial(net_kernel, counts),
        out_shape=(
            jax.ShapeDtypeStruct((4, 4096), F32),
            jax.ShapeDtypeStruct((64, 4096), BF),
            jax.ShapeDtypeStruct((ROWS, 128), F32),
        ),
        in_specs=[vmem] * 14,
        out_specs=(vmem, vmem, vmem),
        scratch_shapes=scratch,
        compiler_params=pltpu.CompilerParams(collective_id=1, has_side_effects=True, vmem_limit_bytes=56 * 2**20),
    )(*args, *tables)


def unlaid(g):
    by_return = g[AT_RETURN : AT_RETURN + 2304].reshape(3, 3, 2, 128, 128).transpose(0, 1, 3, 2, 4).reshape(3, 3, 128, 256)
    by_bottom = g[AT_BOTTOM : AT_BOTTOM + 2304].reshape(3, 3, 256, 128)
    by_final = g[AT_FINAL : AT_FINAL + 576].reshape(3, 3, 64, 128)
    wide = g[AT_SECOND : AT_SECOND + 384].reshape(3, 128, 2, 64).transpose(0, 2, 1, 3)
    two = g[AT_SECOND + 384 : AT_SECOND + 512].reshape(128, 2, 64).transpose(1, 0, 2)
    one = g[AT_SECOND + 512 : AT_SECOND + 640]
    last = jnp.concatenate([two, one[None, :, :64]], axis=0)
    by_second = jnp.concatenate([wide, last[:, None]], axis=1)
    wide = g[AT_FIRST : AT_FIRST + 192].reshape(3, 64, 2, 64).transpose(0, 2, 1, 3)
    tail = g[AT_FIRST + 192 : AT_FIRST + 256]
    last = jnp.concatenate([one[:, 64:].reshape(2, 64, 64), tail[None, :, 64:]], axis=0)
    by_first = jnp.concatenate([wide, last[:, None]], axis=1)
    return tail[:, :16], by_first, by_second, by_bottom, by_return, by_final, g[AT_READ : AT_READ + 2, :64]


def places():
    row, col = lax.axis_index("row"), lax.axis_index("col")
    return row // 2, row % 2, col % 4, col // 4


def peer(axis, d):
    x, core, y, z = places()
    if axis == "core":
        return {"row": x * 2 + 1 - core}
    if axis == "z":
        return {"col": (1 - z) * 4 + y}
    if axis == "x":
        return {"row": (x + d) % 4 * 2 + core}
    return {"col": z * 4 + (y + d) % 4}


def sum_kernel(x_ref, o_ref, s1, r1, h1, s2, r2, h2, s3, r3, h3, s4, r4, g, ss1, rs1, ss2, rs2, ss3, rs3, ss4, rs4):
    x, core, y, z = places()
    barrier = pltpu.get_barrier_semaphore()
    hops = [("core", 1), ("z", 1)] + [(axis, d) for axis in "xy" for d in (1, 2, 3)]
    for axis, d in hops:
        pl.semaphore_signal(barrier, inc=1, device_id=peer(axis, d), device_id_type=pl.DeviceIdType.MESH)
    pl.semaphore_wait(barrier, len(hops))

    def span(start, size, unit=16):
        return pl.ds(pl.multiple_of(start, unit), size)

    bf, f32 = jnp.bfloat16, jnp.float32
    s1[...] = x_ref[span((1 - core) * HALF, HALF), :].astype(bf)
    first = remote(s1, r1, ss1.at[0], rs1.at[0], peer("core", 1))
    first.start()
    first.wait()
    h1[...] = x_ref[span(core * HALF, HALF), :] + r1[...].astype(f32)

    s2[...] = h1[...].astype(bf)
    copies = []
    for part, axis, me in ((0, "x", x), (1, "y", y)):
        for d in (1, 2, 3):
            copies.append(remote(s2.at[span(part * PART + (me + d) % 4 * CHUNK, CHUNK), :], r2.at[part, d - 1], ss2.at[part, d - 1], rs2.at[part, d - 1], peer(axis, d)))
    for copy in copies:
        copy.start()
    for copy in copies:
        copy.wait()
    for part, me in ((0, x), (1, y)):
        total = h1[span(part * PART + me * CHUNK, CHUNK), :]
        for d in range(3):
            total = total + r2[part, d].astype(f32)
        h2[part] = total

    s3[...] = h2[...].astype(bf)
    copies = []
    for part, axis, me in ((0, "y", y), (1, "x", x)):
        for d in (1, 2, 3):
            copies.append(remote(s3.at[part, span((me + d) % 4 * SUB, SUB), :], r3.at[part, d - 1], ss3.at[part, d - 1], rs3.at[part, d - 1], peer(axis, d)))
    for copy in copies:
        copy.start()
    for copy in copies:
        copy.wait()
    for part, me in ((0, y), (1, x)):
        total = h2[part, span(me * SUB, SUB), :]
        for d in range(3):
            total = total + r3[part, d].astype(f32)
        h3[part] = total

    s4[...] = h3[:, span((1 - z) * LEAF, LEAF), :].astype(bf)
    fourth = remote(s4, r4, ss4.at[0], rs4.at[0], peer("z", 1))
    fourth.start()
    fourth.wait()

    base = [core * HALF + x * CHUNK + y * SUB, core * HALF + PART + y * CHUNK + x * SUB]
    for part in (0, 1):
        g[span(base[part] + z * LEAF, LEAF), :] = (h3[part, span(z * LEAF, LEAF), :] + r4[part].astype(f32)).astype(bf)

    def spread(jobs, send, recv):
        copies = []
        for k, (start, size, axis, d) in enumerate(jobs):
            here = g.at[span(start, size), :]
            copies.append(remote(here, here, send.at[k], recv.at[k], peer(axis, d)))
        for copy in copies:
            copy.start()
        for copy in copies:
            copy.wait()

    spread([(base[part] + z * LEAF, LEAF, "z", 1) for part in (0, 1)], ss4.at[pl.ds(1, 2)], rs4.at[pl.ds(1, 2)])
    spread([(base[part], SUB, axis, d) for part, axis in ((0, "y"), (1, "x")) for d in (1, 2, 3)], ss3.at[2], rs3.at[2])
    wide = [core * HALF + x * CHUNK, core * HALF + PART + y * CHUNK]
    spread([(wide[part], CHUNK, axis, d) for part, axis in ((0, "x"), (1, "y")) for d in (1, 2, 3)], ss2.at[2], rs2.at[2])
    spread([(core * HALF, HALF, "core", 1)], ss1.at[pl.ds(1, 1)], rs1.at[pl.ds(1, 1)])
    o_ref[...] = g[...].astype(f32)


def all_sum(values):
    bf, f32 = jnp.bfloat16, jnp.float32
    return pl.pallas_call(
        sum_kernel,
        out_shape=jax.ShapeDtypeStruct((ROWS, 128), f32),
        in_specs=[pl.BlockSpec(memory_space=pltpu.VMEM)],
        out_specs=pl.BlockSpec(memory_space=pltpu.VMEM),
        scratch_shapes=[
            pltpu.VMEM((HALF, 128), bf),
            pltpu.VMEM((HALF, 128), bf),
            pltpu.VMEM((HALF, 128), f32),
            pltpu.VMEM((HALF, 128), bf),
            pltpu.VMEM((2, 3, CHUNK, 128), bf),
            pltpu.VMEM((2, CHUNK, 128), f32),
            pltpu.VMEM((2, CHUNK, 128), bf),
            pltpu.VMEM((2, 3, SUB, 128), bf),
            pltpu.VMEM((2, SUB, 128), f32),
            pltpu.VMEM((2, LEAF, 128), bf),
            pltpu.VMEM((2, LEAF, 128), bf),
            pltpu.VMEM((ROWS, 128), bf),
        ]
        + [pltpu.SemaphoreType.DMA(n) for n in ((2,), (2,), (3, 6), (3, 6), (3, 6), (3, 6), (3,), (3,))],
        compiler_params=pltpu.CompilerParams(collective_id=0, has_side_effects=True, vmem_limit_bytes=48 * 2**20),
    )(values)


def on_device(counts, *args):
    logits, features, grads = run_net(counts, *args)
    grads = unlaid(all_sum(grads))
    return (logits[:2].reshape(2, 32, 128), features.reshape(64, 32, 128)) + grads


def solution(mesh):
    counts = (mesh.shape["row"], mesh.shape["col"])
    cells = P(None, ("batch", "row"), "col")
    in_specs = (P(("batch", "row"), "col"),) + (P(),) * 7 + (cells,)
    out_specs = (cells, cells, P("batch", None)) + (P("batch", None, None, None),) * 5 + (P("batch", None),)
    return jax.shard_map(
        functools.partial(on_device, counts), mesh=mesh, in_specs=in_specs, out_specs=out_specs, check_vma=False
    )
```

profile of v0, /device:TPU:1, one launch (start us, length us, event | category | flops | bytes accessed | tf_op | source)
XLA Modules:
  0.0 136.7 jit_solution(11659059412126323248)
XLA Ops:
  0.6 1.4 %copy.31.refs_1_ = bf16[64,16]{1,0:T(8,128)(2,1)} copy(bf16[64,16]{0,1:T(8,128)(2,1)} %param.15) | data formatting | bytes 4096 | tf_op args[1]
  2.0 1.8 %copy.32.refs_3_ = bf16[3,3,128,64]{3,2,1,0:T(8,128)(2,1)} copy(bf16[3,3,128,64]{2,3,1,0:T(8,128)(2,1)} %param.17) | data formatting | bytes 294912 | tf_op args[3]
  3.8 81.7 %shard_map.205 = (f32[4,4096]{1,0:T(4,128)}, bf16[64,4096]{1,0:T(8,128)(2,1)}, f32[6144,128]{1,0:T(8,128)}) custom-call(s32[32,128]{1,0:T(8,128)} %refs_0_.1, bf16[64,16]{1,0:T(8,128)(2,1)} %copy.31.refs_1_, bf16[3,3,64,64]{3,2,1,0:T(8,128)(2,1)} %refs_2_.1, bf16[3,3,128,64]{3,2,1,0:T(8,128)(2,1)} %copy.32.refs_3_, bf16[3,3,256,128]{3,2,1,0:T(8,128)(2,1)} %refs_4_.1, ...), custom_call_target="tpu_custom_call" | custom-call | tf_op jit(solution)/shard_map/pallas_call | solution.py:555
  85.6 0.9 slice_bitcast_fusion.2
  86.4 0.6 copy.51
  87.0 1.9 %copy.43 = bf16[8,8,32,128]{3,2,1,0:T(8,128)(2,1)} copy(bf16[8,8,32,128]{3,1,2,0:T(8,128)(2,1)} %bitcast.41) | data formatting | bytes 1048576
  89.0 36.6 %shard_map.206 = f32[6144,128]{1,0:T(8,128)S(1)} custom-call(f32[6144,128]{1,0:T(8,128)} %get-tuple-element.14.x_ref), custom_call_target="tpu_custom_call" | custom-call | tf_op jit(solution)/shard_map/pallas_call | solution.py:678
  125.5 0.6 slice.53
  126.1 0.7 slice_bitcast_fusion.1
  126.8 0.7 copy.39
  127.5 0.1 copy.35
  127.6 0.7 copy.50
  128.3 0.2 reshape.50
  128.5 0.1 slice_bitcast_fusion
  128.5 0.1 copy.37
  128.6 0.8 maximum_bitcast_fusion.1
  129.4 0.7 pad_maximum_fusion.1
  130.1 0.9 maximum_bitcast_fusion
  131.1 0.8 copy.34
  131.9 1.0 reshape.52
  132.9 0.1 pad_maximum_fusion
  133.0 0.7 copy.40
  133.7 0.7 slice.52
  134.5 1.2 fusion
  135.6 1.1 copy.48
  (5 shorter events, 0.0 us)
where the time goes:
time: 137 us
  Pallas kernels  118 us (86%)
  local copies, waits for them, and re-layouts  15.2 us (11%)
  other arithmetic  2.53 us (2%)
    pallas_call x1, Pallas kernels, run_net(): pl.pallas_call(functools.partial(net_kernel, counts), out_shape=(jax.Shap...  81.7 us
    pallas_call x1, Pallas kernels, all_sum(): pl.pallas_call(sum_kernel, out_shape=jax.ShapeDtypeStruct((ROWS, 128), f3...  36.6 us
    unnamed x7, local copies, waits for them, and re-layouts  7.99 us

commit v1 on v0

v1 whole, which is shorter than its diff:
```python
import functools

import jax
import jax.numpy as jnp
import numpy as np
from jax import lax
from jax.experimental import pallas as pl
from jax.experimental.pallas import tpu as pltpu
from jax.sharding import PartitionSpec as P

BF, F32 = jnp.bfloat16, jnp.float32
MESH = pl.DeviceIdType.MESH

DEEP, WIDE = 8, 32
CELLS = DEEP * WIDE

ROWS = 6144
PARTS = ((0, 2048, "row"), (2048, 3072, "col"), (5120, 1024, "row"))
AT_RETURN, AT_FINAL, AT_BOTTOM, AT_SECOND, AT_FIRST, AT_READ = 0, 2304, 2880, 5184, 5760, 6080


def ranged(values, start, size):
    return values.at[pl.ds(pl.multiple_of(start, 16), size), :]


def bounds(p):
    side = max(DEEP * p, 16)
    left = 2 * WIDE * p
    return WIDE * p, left, left + side, left + 2 * side


def shift_table():
    table = {}
    for dr in (-1, 0, 1):
        for dc in (-1, 0, 1):
            m = np.zeros((CELLS, CELLS), np.float32)
            for r in range(DEEP):
                for q in range(WIDE):
                    if 0 <= r + dr < DEEP and 0 <= q + dc < WIDE:
                        m[(r + dr) * WIDE + q + dc, r * WIDE + q] = 1
            table[dr, dc] = m
    return table


def pick_table():
    m = np.zeros((112, CELLS), np.float32)
    for q in range(WIDE):
        m[q, q] = 1
        m[32 + q, (DEEP - 1) * WIDE + q] = 1
    for r in range(DEEP):
        m[64 + r, r * WIDE] = 1
        m[80 + r, r * WIDE + WIDE - 1] = 1
    for k, cell in enumerate((0, WIDE - 1, CELLS - WIDE, CELLS - 1)):
        m[96 + k, cell] = 1
    return m


CORNERS = {(-1, -1): 3, (-1, 1): 2, (1, -1): 1, (1, 1): 0}


def halo_tables():
    blocks, where = [], {}
    for p in (4, 2, 1):
        for ea in range(p + 2):
            for eb in range(p + 2):
                dr, dc = (ea > p) - (ea < 1), (eb > p) - (eb < 1)
                if (dr, dc) == (0, 0):
                    continue
                sa, sb = (ea - 1) % p, (eb - 1) % p
                down, left, right, corner = bounds(p)
                m = np.zeros((384, CELLS), np.float32)
                for r in range(DEEP):
                    for q in range(WIDE):
                        rr, qq = r + dr, q + dc
                        row_in, col_in = 0 <= rr < DEEP, 0 <= qq < WIDE
                        if row_in and col_in:
                            continue
                        if col_in:
                            spot = (0 if rr < 0 else down) + sb * WIDE + qq
                        elif row_in:
                            spot = (left if qq < 0 else right) + sa * DEEP + rr
                        else:
                            spot = corner + CORNERS[dr, dc]
                        m[spot, r * WIDE + q] = 1
                used = []
                for tile in range(3):
                    block = m[tile * 128 : (tile + 1) * 128]
                    if block.any():
                        used.append((tile, len(blocks)))
                        blocks.append(block)
                where[p, ea, eb] = used
    return np.concatenate(blocks), where


def spread_table():
    m = np.zeros((512, 512), np.float32)
    for r in range(4):
        for w in range(128):
            m[r * 128 + w, (w % 4) * 128 + r * WIDE + w // 4] = 1
    return m


SHIFTS = shift_table()
SHIFT_AT = {key: n for n, key in enumerate(SHIFTS)}
SHIFT_ALL = np.concatenate(list(SHIFTS.values()))
PICK = pick_table()
HALO_ALL, HALO_AT = halo_tables()
SPREAD = spread_table()

EYE = SHIFT_AT[0, 0] * CELLS

UNDER = (((0,), (1, 2)), ((0, 1), (2,)))
OVER = ((2,), (1, 2), (0, 1), (0,))
BASE = (0, 1, 1, 2)


def mm(a, b):
    return jnp.dot(a, b, preferred_element_type=F32)


def nt(a, b):
    return lax.dot_general(a, b, (((1,), (1,)), ((), ())), preferred_element_type=F32)


def logistic(z):
    return 0.5 + 0.5 * jnp.tanh(0.5 * z)


def activated(v):
    stored = v.astype(BF)
    z = stored.astype(F32)
    return stored, (z * logistic(z)).astype(BF)


def sloped(incoming, stored):
    z = stored.astype(F32)
    s = logistic(z)
    return (incoming * (s * (1.0 + z * (1.0 - s)))).astype(BF)


def remote(src, dst, send, recv, target):
    return pltpu.make_async_remote_copy(
        src_ref=src, dst_ref=dst, send_sem=send, recv_sem=recv, device_id=target, device_id_type=MESH
    )


SIDES = ((-1, 0), (1, 0), (0, -1), (0, 1), (-1, -1), (-1, 1), (1, -1), (1, 1))


def net_kernel(counts, *refs):
    it = iter(refs)

    def take(n):
        return [next(it) for _ in range(n)]

    syn, embt, k1, k2t, k3, k4, k5, rdo, cot, cS, cQ, cT, cU = take(13)
    logits_ref, features_ref, grads_ref = take(3)
    xb, e0, z0, z1, f1, e1, z2, f2, e2, z3, e3, z4, e4, z5, f5, t5, t4, t3, t2, t1, fg, cp = take(22)
    w0, w1, w1b, w2, w2b, w3, w3b, w4, w4b, w5, w5b, r4, r4t = take(13)
    halos = [take(2) for _ in range(10)]
    sends, recvs = take(2)
    g_ref, whole, tall = take(3)
    stages = [take(5) for _ in PARTS]
    sum_sends, sum_recvs = take(2)

    n_row, n_col = counts
    row, col = lax.axis_index("row"), lax.axis_index("col")
    there = {
        (-1, 0): row > 0,
        (1, 0): row < n_row - 1,
        (0, -1): col > 0,
        (0, 1): col < n_col - 1,
    }
    for dr in (-1, 1):
        for dc in (-1, 1):
            there[dr, dc] = jnp.logical_and(there[dr, 0], there[0, dc])

    def place(dr, dc):
        return {"row": (row + dr + n_row) % n_row, "col": (col + dc + n_col) % n_col}

    partners = [(d, 0) for d in range(1, n_row)] + [(0, d) for d in range(1, n_col)] + list(SIDES[4:])
    barrier = pltpu.get_barrier_semaphore()
    for partner in partners:
        pl.semaphore_signal(barrier, inc=1, device_id=place(*partner), device_id_type=MESH)

    def shift(dr, dc):
        n = SHIFT_AT[dr, dc]
        return cS[n * CELLS : (n + 1) * CELLS, :]

    lane = lax.broadcasted_iota(jnp.int32, (1, 128), 1)
    sixteen = lax.broadcasted_iota(jnp.int32, (16, 1), 0)

    def begin(n, p, width, ref, ahead=None):
        out, into = halos[n]
        down, left, right, corner = bounds(p)
        picked = {}
        for a in range(p):
            for b in range(p):
                if a in (0, p - 1) or b in (0, p - 1):
                    start = ((a + 1) * (p + 2) + b + 1) * width
                    picked[a, b] = nt(cQ[...], ref[start : start + width, :])
        for b in range(p):
            out[b * WIDE : (b + 1) * WIDE, 0:width] = picked[0, b][0:32].astype(BF)
            out[down + b * WIDE : down + (b + 1) * WIDE, 0:width] = picked[p - 1, b][32:64].astype(BF)
        for base, at, b in ((left, 64, 0), (right, 80, p - 1)):
            if p == 1:
                out[base : base + 16, 0:width] = picked[0, 0][at : at + 16].astype(BF)
            else:
                side = jnp.concatenate([picked[a, b][at : at + 8] for a in range(p)], axis=0)
                out[base : base + DEEP * p, 0:width] = side.astype(BF)
        ends = 0.0
        for k, spot in enumerate(((0, 0), (0, p - 1), (p - 1, 0), (p - 1, p - 1))):
            ends = ends + jnp.where(sixteen == k, picked[spot][96:112], 0.0)
        out[corner : corner + 16, 0:width] = ends.astype(BF)

        size = {(-1, 0): (0, down, down), (1, 0): (down, left, 0), (0, -1): (left, right, right), (0, 1): (right, corner, left)}
        copies = []
        for k, (dr, dc) in enumerate(SIDES):
            if (dr, dc) in size:
                start, stop, target = size[dr, dc]
            else:
                start, stop = corner, corner + 16
                target = corner + 16 * (1 + CORNERS[-dr, -dc])
            copies.append(
                remote(out.at[start:stop], into.at[target : target + stop - start], sends.at[n, k], recvs.at[n, k], place(dr, dc))
            )
        if ahead is not None:
            ahead()
        for copy in copies:
            copy.start()
        return copies

    def end(n, p, width, ref, copies):
        into = halos[n][1]
        down, left, right, corner = bounds(p)
        for copy in copies:
            copy.wait()
        ends = 0.0
        for side, k in CORNERS.items():
            tile = into[corner + 16 * (k + 1) : corner + 16 * (k + 2), 0:width].astype(F32)
            ends = ends + jnp.where(jnp.logical_and(sixteen == k, there[side]), tile, 0.0)
        into[corner : corner + 16, 0:width] = ends.astype(BF)
        tiles = []
        for tile in range(-(-(corner + 16) // 128)):
            at = lane + tile * 128
            keep = jnp.logical_and(at >= corner, at < corner + 16)
            for low, high, side in ((0, down, (-1, 0)), (down, left, (1, 0)), (left, right, (0, -1)), (right, corner, (0, 1))):
                keep = jnp.logical_or(keep, jnp.logical_and(jnp.logical_and(at >= low, at < high), there[side]))
            turned = nt(cS[EYE : EYE + width, 0:width], into[tile * 128 : (tile + 1) * 128, 0:width])
            tiles.append(jnp.where(keep, turned, 0.0).astype(BF))
        for ea in range(p + 2):
            for eb in range(p + 2):
                dr, dc = (ea > p) - (ea < 1), (eb > p) - (eb < 1)
                if (dr, dc) == (0, 0):
                    continue
                start = (((ea - 1) % p + 1) * (p + 2) + (eb - 1) % p + 1) * width
                moved = mm(ref[start : start + width, :], shift(dr, dc))
                for tile, block in HALO_AT[p, ea, eb]:
                    moved = moved + mm(tiles[tile], cT[block * 128 : (block + 1) * 128, :])
                start = (ea * (p + 2) + eb) * width
                ref[start : start + width, :] = moved.astype(BF)

    ways = {"row": (row, n_row, lambda d: place(d, 0)), "col": (col, n_col, lambda d: place(0, d))}
    flying = {}

    def sum_step(part, step):
        start, size, first = PARTS[part]
        s1, r1, h1, s2, r2 = stages[part]
        me1, n1, to1 = ways[first]
        me2, n2, to2 = ways["col" if first == "row" else "row"]
        c1, c2 = size // n1, size // n1 // n2
        for copy in flying.pop(part, ()):
            copy.wait()
        if step == 4:
            return
        if step == 0:
            s1[...] = g_ref[start : start + size, :].astype(BF)
        elif step == 1:
            total = g_ref[pl.ds(pl.multiple_of(start + me1 * c1, 16), c1), :]
            for d in range(n1 - 1):
                total = total + r1[d].astype(F32)
            h1[...] = total
            s2[...] = total.astype(BF)
        elif step == 2:
            total = h1[pl.ds(pl.multiple_of(me2 * c2, 16), c2), :]
            for d in range(n2 - 1):
                total = total + r2[d].astype(F32)
            whole[pl.ds(pl.multiple_of(start + me1 * c1 + me2 * c2, 16), c2), :] = total.astype(BF)
        copies = []
        for d in range(1, n1 if step in (0, 3) else n2):
            if step == 0:
                src, dst, to = ranged(s1, (me1 + d) % n1 * c1, c1), r1.at[d - 1], to1
            elif step == 1:
                src, dst, to = ranged(s2, (me2 + d) % n2 * c2, c2), r2.at[d - 1], to2
            elif step == 2:
                src = dst = ranged(whole, start + me1 * c1 + me2 * c2, c2)
                to = to2
            else:
                src = dst = ranged(whole, start + me1 * c1, c1)
                to = to1
            copies.append(remote(src, dst, sum_sends.at[part, step, d], sum_recvs.at[part, step, d], to(d)))
        for copy in copies:
            copy.start()
        flying[part] = copies

    bit = lax.broadcasted_iota(jnp.int32, (16, 1), 0)
    groups = []
    for a in range(4):
        for t in range(2):
            line = [(syn[16 * t + 4 * r + a : 16 * t + 4 * r + a + 1, :] >> bit) & 1 for r in range(4)]
            groups.append(jnp.concatenate(line, axis=1))
    bits = jnp.concatenate(groups, axis=0).astype(F32).astype(BF)
    phased = mm(bits, cU[...]).astype(BF)
    for a in range(4):
        for t in range(2):
            for b in range(4):
                start = ((a + 1) * 6 + b + 1) * 16
                xb[start : start + 16, t * 128 : (t + 1) * 128] = phased[(a * 2 + t) * 16 : (a * 2 + t + 1) * 16, b * 128 : (b + 1) * 128]
    copies = begin(0, 4, 16, xb, lambda: pl.semaphore_wait(barrier, len(partners)))

    eye = shift(0, 0)

    def beside(blocks, i, blank):
        return jnp.concatenate(blocks + [blank] if i == 0 else [blank] + blocks, axis=0)

    def added(k, rows, cols):
        return sum(k[ta, tb].astype(F32) for ta in rows for tb in cols).astype(BF)

    def arrange_first():
        repeat = (lax.broadcasted_iota(jnp.int32, (16, 96), 1) % 16 == lax.broadcasted_iota(jnp.int32, (16, 96), 0)).astype(F32).astype(BF)
        tiled = mm(nt(eye[:64, :64], embt[...]).astype(BF), repeat)
        own = lax.broadcasted_iota(jnp.int32, (64, 96), 1) // 16
        for j in range(6):
            w0[j * 64 : (j + 1) * 64, :] = jnp.where(own == j, tiled, 0.0).astype(BF)
        for ta in range(3):
            for i in range(2):
                w1[i * 64 : (i + 1) * 64, ta * 256 : (ta + 1) * 256] = sum(
                    mm(k1[ta, tb], eye[(tb + i) * 64 : (tb + i + 1) * 64, :]) for tb in range(3)
                ).astype(BF)

    def arrange_second():
        blank, empty = jnp.zeros((64, 128), BF), jnp.zeros((64, 64), BF)
        for ta in range(3):
            for i in range(2):
                line = beside([k2t[ta, tb] for tb in range(3)], i, blank)
                w2[i * 128 : (i + 1) * 128, ta * 256 : (ta + 1) * 256] = nt(eye[:128, :128], line).astype(BF)
                for tb in range(3):
                    w2b[i * 64 : (i + 1) * 64, ta * 512 + (tb + i) * 128 : ta * 512 + (tb + i + 1) * 128] = k2t[2 - ta, 2 - tb]
                hole = ta * 512 + (384 if i == 0 else 0)
                w2b[i * 64 : (i + 1) * 64, hole : hole + 128] = blank
                line = beside([k1[2 - ta, 2 - tb] for tb in range(3)], i, empty)
                w1b[i * 64 : (i + 1) * 64, ta * 256 : (ta + 1) * 256] = nt(eye[:64, :64], line).astype(BF)

    def arrange_bottom():
        for t in range(9):
            w3[:, t * 128 : (t + 1) * 128] = k3[t // 3, t % 3]
            w3b[:, t * 256 : (t + 1) * 256] = nt(eye[:128, :128], k3[2 - t // 3, 2 - t % 3]).astype(BF)

    def arrange_return():
        for pa in range(2):
            for pb in range(2):
                for s in range(2):
                    for u in range(2):
                        block = added(k4, UNDER[pa][s], UNDER[pb][u])
                        w4[(pa * 2 + pb) * 128 : (pa * 2 + pb + 1) * 128, (s * 2 + u) * 256 : (s * 2 + u + 1) * 256] = block
                        at = OVER.index(UNDER[pa][s]) * 4 + OVER.index(UNDER[pb][u])
                        w4b[:, at * 128 : (at + 1) * 128] = nt(eye, block).astype(BF)

    def arrange_final():
        for pa in range(2):
            for pb in range(2):
                for s in range(2):
                    for u in range(2):
                        start = pa * 128 + (1 - pb) * 64
                        w5[start : start + 64, (s * 2 + u) * 128 : (s * 2 + u + 1) * 128] = added(k5, UNDER[pa][s], UNDER[pb][u])
        for ea in range(4):
            for pair in range(2):
                stack = jnp.concatenate([added(k5, OVER[ea], OVER[2 * pair + i]) for i in range(2)], axis=0)
                at = ea * 2 + pair
                w5b[:, at * 128 : (at + 1) * 128] = nt(eye[:128, :128], stack).astype(BF)

    def arrange_readout():
        repeat = (lax.broadcasted_iota(jnp.int32, (64, 256), 1) % 64 == lax.broadcasted_iota(jnp.int32, (64, 256), 0)).astype(F32).astype(BF)
        tiled = mm(rdo[...], repeat)
        tiled = jnp.concatenate([tiled, jnp.zeros((2, 256), F32)] * 4, axis=0)
        own = lax.broadcasted_iota(jnp.int32, (16, 256), 1) // 64 == lax.broadcasted_iota(jnp.int32, (16, 256), 0) // 4
        r4[...] = jnp.where(own, tiled, 0.0).astype(BF)
        r4t[...] = nt(eye, r4[...]).astype(BF)

        wide = cot[...].astype(F32)
        groups = []
        for a in range(4):
            for t in range(2):
                line = jnp.concatenate([wide[:, 16 * t + 4 * r + a, :] for r in range(4)], axis=1)
                groups.append(jnp.concatenate([line, jnp.zeros((6, 512), F32)], axis=0))
        phased = mm(jnp.concatenate(groups, axis=0).astype(BF), cU[...])
        for a in range(4):
            for t in range(2):
                start = (a * 2 + t) * 8
                pieces = [phased[start : start + 4, b * 128 : (b + 1) * 128] for b in range(4)]
                cp[a * 16 : (a + 1) * 16, t * 128 : (t + 1) * 128] = jnp.concatenate(pieces, axis=0).astype(BF)

    arrange_first()
    arrange_readout()
    end(0, 4, 16, xb, copies)

    for ea in range(6):
        stored, active = activated(mm(w0[...], xb[ea * 96 : (ea + 1) * 96, :]))
        e0[ea * 384 : (ea + 1) * 384, :] = active
        if 1 <= ea <= 4:
            z0[(ea - 1) * 256 : ea * 256, :] = stored[64:320, :]

    for a in range(4):
        for pair in range(2):
            v = sum(
                mm(w1[:, ta * 256 : (ta + 1) * 256], e0[((a + ta) * 6 + 2 * pair) * 64 : ((a + ta) * 6 + 2 * pair + 4) * 64, :])
                for ta in range(3)
            )
            start = (a * 4 + 2 * pair) * 64
            z1[start : start + 128, :], f1[start : start + 128, :] = activated(v)

    def pooled(ref, side, width, a, b):
        spots = [((2 * a + i) * side + 2 * b + j) * width for i in range(2) for j in range(2)]
        return (sum(ref[s : s + width, :].astype(F32) for s in spots) * 0.25).astype(BF)

    for a in range(2):
        for b in range(2):
            start = ((a + 1) * 4 + b + 1) * 64
            e1[start : start + 64, :] = pooled(f1, 4, 64, a, b)
    copies = begin(1, 2, 64, e1)
    arrange_second()
    end(1, 2, 64, e1, copies)

    for a in range(2):
        v = sum(mm(w2[:, ta * 256 : (ta + 1) * 256], e1[(a + ta) * 256 : (a + ta + 1) * 256, :]) for ta in range(3))
        z2[a * 256 : (a + 1) * 256, :], f2[a * 256 : (a + 1) * 256, :] = activated(v)
    e2[4 * 128 : 5 * 128, :] = pooled(f2, 2, 128, 0, 0)
    copies = begin(2, 1, 128, e2)
    arrange_bottom()
    end(2, 1, 128, e2, copies)

    z3[...], e3[4 * 256 : 5 * 256, :] = activated(mm(w3[...], e2[...]))
    copies = begin(3, 1, 256, e3)
    arrange_return()
    end(3, 1, 256, e3, copies)

    for a in range(2):
        for b in range(2):
            n = a * 2 + b
            v = sum(
                mm(w4[n * 128 : (n + 1) * 128, s * 512 : (s + 1) * 512], e3[((a + s) * 3 + b) * 256 : ((a + s) * 3 + b + 2) * 256, :])
                for s in range(2)
            )
            v = v + f2[n * 128 : (n + 1) * 128, :].astype(F32)
            start = ((a + 1) * 4 + b + 1) * 128
            z4[n * 128 : (n + 1) * 128, :], e4[start : start + 128, :] = activated(v)
    copies = begin(4, 2, 128, e4)
    arrange_final()
    end(4, 2, 128, e4, copies)

    RUNS = ((0, 1, 64, 64), (1, 2, 0, 128), (3, 1, 0, 64))
    for a in range(4):
        for b, many, first, size in RUNS:
            base = (a % 2) * 128 + first
            v = sum(
                mm(w5[base : base + size, s * 256 : (s + 1) * 256], e4[((BASE[a] + s) * 4 + BASE[b]) * 128 : ((BASE[a] + s) * 4 + BASE[b] + 2) * 128, :])
                for s in range(2)
            )
            start = (a * 4 + b) * 64
            v = v + f1[start : start + size, :].astype(F32)
            z5[start : start + size, :], f5[start : start + size, :] = activated(v)

    for a in range(4):
        back = mm(r4t[...], cp[a * 16 : (a + 1) * 16, :])
        start = ((a + 1) * 6 + 1) * 64
        t5[start : start + 256, :] = sloped(back, z5[a * 256 : (a + 1) * 256, :])
    copies = begin(5, 4, 64, t5)

    groups = []
    total = jnp.zeros((16, 256), F32)
    for a in range(4):
        here = f5[a * 256 : (a + 1) * 256, :]
        value = mm(r4[...], here)
        total = total + nt(cp[a * 16 : (a + 1) * 16, :], here)
        for t in range(2):
            groups.append(jnp.concatenate([value[b * 4 : (b + 1) * 4, t * 128 : (t + 1) * 128] for b in range(4)], axis=1))
    value = jnp.concatenate(groups, axis=0)
    laid = 0.0
    for _ in range(3):
        piece = value.astype(BF)
        laid = laid + nt(piece, cU[...])
        value = value - piece.astype(F32)
    for a in range(4):
        for t in range(2):
            for r in range(4):
                h = 16 * t + 4 * r + a
                logits_ref[:, h : h + 1, :] = laid[(a * 2 + t) * 4 : (a * 2 + t) * 4 + 2, r * 128 : (r + 1) * 128].reshape(2, 1, 128)
    total = sum(total[b * 4 : (b + 1) * 4, b * 64 : (b + 1) * 64] for b in range(4))
    g_ref[AT_READ:ROWS, :] = jnp.zeros((ROWS - AT_READ, 128), F32)
    g_ref[AT_READ : AT_READ + 4, 0:64] = total

    sums = {}
    for a in range(4):
        for s in range(2):
            for b, many, first, size in RUNS:
                start = ((BASE[a] + s) * 4 + BASE[b]) * 128
                t_start = ((a + 1) * 6 + b + 1) * 64
                product = nt(t5[t_start : t_start + size, :], e4[start : start + 256, :])
                for m in range(many):
                    key = (a % 2, s, (b + m) % 2)
                    block = product[m * 64 : (m + 1) * 64, :]
                    sums[key] = sums[key] + block if key in sums else block

    def reads(parity, tap):
        return 0 if tap in UNDER[parity][0] else 1

    for ta in range(3):
        rowed = [sums[0, reads(0, ta), pb] + sums[1, reads(1, ta), pb] for pb in range(2)]
        for tb in range(3):
            value = sum(rowed[pb][:, reads(pb, tb) * 128 : (reads(pb, tb) + 1) * 128] for pb in range(2))
            start = AT_FINAL + (ta * 3 + tb) * 64
            g_ref[start : start + 64, :] = value

    end(5, 4, 64, t5, copies)
    for a in range(2):
        for b in range(2):
            v = sum(
                mm(w5b[:, m * 256 : (m + 1) * 256], t5[((2 * a + m) * 6 + 2 * b) * 64 : ((2 * a + m) * 6 + 2 * b + 4) * 64, :])
                for m in range(4)
            )
            start = ((a + 1) * 4 + b + 1) * 128
            n = a * 2 + b
            t4[start : start + 128, :] = sloped(v, z4[n * 128 : (n + 1) * 128, :])
    copies = begin(6, 2, 128, t4)

    for b in range(2):
        for u in range(2):
            parts = {}
            for a in range(2):
                for s in range(2):
                    start = ((a + 1) * 4 + b + 1) * 128
                    from_ = ((a + s) * 3 + b + u) * 256
                    parts[a, s] = nt(t4[start : start + 128, :], e3[from_ : from_ + 256, :])
            for ta in range(3):
                value = parts[0, reads(0, ta)] + parts[1, reads(1, ta)]
                for tb in UNDER[b][u]:
                    for half in range(2):
                        start = AT_RETURN + ((ta * 3 + tb) * 2 + half) * 128
                        piece = value[:, half * 128 : (half + 1) * 128]
                        g_ref[start : start + 128, :] = piece if b == 0 else g_ref[start : start + 128, :] + piece

    sum_step(0, 0)
    end(6, 2, 128, t4, copies)
    v = sum(mm(w4b[:, m * 512 : (m + 1) * 512], t4[m * 512 : (m + 1) * 512, :]) for m in range(4))
    t3[4 * 256 : 5 * 256, :] = sloped(v, z3[...])
    copies = begin(7, 1, 256, t3)
    for t in range(9):
        g_ref[AT_BOTTOM + t * 256 : AT_BOTTOM + (t + 1) * 256, :] = nt(t3[4 * 256 : 5 * 256, :], e2[t * 128 : (t + 1) * 128, :])
    sum_step(1, 0)
    end(7, 1, 256, t3, copies)

    through = mm(w3b[...], t3[...]) * 0.25
    for a in range(2):
        for b in range(2):
            n = a * 2 + b
            start = ((a + 1) * 4 + b + 1) * 128
            t2[start : start + 128, :] = sloped(t4[start : start + 128, :].astype(F32) + through, z2[n * 128 : (n + 1) * 128, :])
    copies = begin(8, 2, 128, t2)
    for ta in range(3):
        product = 0.0
        for a in range(2):
            start = ((a + 1) * 4 + 1) * 128
            product = product + nt(e1[(a + ta) * 256 : (a + ta + 1) * 256, :], t2[start : start + 256, :])
        g_ref[AT_SECOND + ta * 192 : AT_SECOND + (ta + 1) * 192, :] = product[0:192, 0:128] + product[64:256, 128:256]
    sum_step(0, 1)
    end(8, 2, 128, t2, copies)

    for a in range(2):
        v = sum(mm(w2b[:, ta * 512 : (ta + 1) * 512], t2[(a + ta) * 512 : (a + ta + 1) * 512, :]) for ta in range(3)) * 0.25
        for b in range(2):
            for i in range(2):
                for j in range(2):
                    fa, fb = 2 * a + i, 2 * b + j
                    start = ((fa + 1) * 6 + fb + 1) * 64
                    n = (fa * 4 + fb) * 64
                    t1[start : start + 64, :] = sloped(t5[start : start + 64, :].astype(F32) + v[b * 64 : (b + 1) * 64, :], z1[n : n + 64, :])
    copies = begin(9, 4, 64, t1)
    for ta in range(3):
        product = 0.0
        for a in range(4):
            for pair in range(2):
                start = ((a + 1) * 6 + 2 * pair + 1) * 64
                from_ = ((a + ta) * 6 + 2 * pair) * 64
                product = product + nt(t1[start : start + 128, :], e0[from_ : from_ + 256, :])
        value = product[0:64, 0:192] + product[64:128, 64:256]
        g_ref[AT_FIRST + ta * 64 : AT_FIRST + (ta + 1) * 64, :] = value[:, 0:128]
        start = AT_FIRST + (192 if ta < 2 else 256)
        g_ref[start : start + 64, ta % 2 * 64 : ta % 2 * 64 + 64] = value[:, 128:192]
    sum_step(1, 1)
    sum_step(0, 2)
    end(9, 4, 64, t1, copies)

    total = jnp.zeros((64, 256), F32)
    for a in range(4):
        for pair in range(2):
            v = sum(
                mm(w1b[:, ta * 256 : (ta + 1) * 256], t1[((a + ta) * 6 + 2 * pair) * 64 : ((a + ta) * 6 + 2 * pair + 4) * 64, :])
                for ta in range(3)
            )
            start = (a * 4 + 2 * pair) * 64
            fg[start : start + 128, :] = sloped(v, z0[start : start + 128, :])
        start = ((a + 1) * 6 + 1) * 16
        total = total + nt(xb[start : start + 64, :], fg[a * 256 : (a + 1) * 256, :])
    total = sum(total[b * 16 : (b + 1) * 16, b * 64 : (b + 1) * 64] for b in range(4))
    g_ref[AT_FIRST + 256 : AT_FIRST + 272, 64:128] = total
    g_ref[AT_FIRST + 272 : AT_FIRST + 320, 64:128] = jnp.zeros((48, 64), F32)

    def lay(a):
        for t in range(2):
            line = jnp.concatenate([fg[(a * 4 + b) * 64 : (a * 4 + b + 1) * 64, t * 128 : (t + 1) * 128] for b in range(4)], axis=1)
            laid = nt(line, cU[...])
            for r in range(4):
                tall[:, 16 * t + 4 * r + a, :] = laid[:, r * 128 : (r + 1) * 128]

    sum_step(2, 0)
    sum_step(0, 3)
    sum_step(1, 2)
    lay(0)
    lay(1)
    sum_step(2, 1)
    sum_step(1, 3)
    lay(2)
    lay(3)
    sum_step(2, 2)
    features_ref[...] = tall[...].astype(BF)
    sum_step(2, 3)
    for part in range(3):
        sum_step(part, 4)
    grads_ref[...] = whole[...]


LEVELS = ((4, 16), (2, 64), (1, 128), (1, 256), (2, 128), (4, 64), (2, 128), (1, 256), (2, 128), (4, 64))


def run_net(counts, *args):
    syn, emb, k1, k2, *rest = args
    args = (syn, emb.T, k1, k2.transpose(0, 1, 3, 2), *rest)
    tables = [jnp.asarray(t, BF) for t in (SHIFT_ALL, PICK, HALO_ALL, SPREAD)]
    blocks = [16 * 36, 64 * 36, 1024, 1024, 1024, 64 * 16, 512, 512, 128 * 9, 256, 256 * 9, 512, 128 * 16, 1024, 1024]
    blocks += [64 * 36, 128 * 16, 256 * 9, 128 * 16, 64 * 36, 1024, 64]
    weights = [(384, 96), (128, 768), (128, 768), (256, 768), (128, 1536), (256, 1152), (128, 2304), (512, 1024), (256, 2048), (256, 512), (128, 1024), (16, 256), (256, 16)]
    scratch = [pltpu.VMEM((n, CELLS), BF) for n in blocks] + [pltpu.VMEM(s, BF) for s in weights]
    for p, width in LEVELS:
        out = bounds(p)[3] + 16
        into = max(out + 64, -(-out // 128) * 128)
        scratch += [pltpu.VMEM((rows, max(width, 128)), BF) for rows in (out, into)]
    scratch += [pltpu.SemaphoreType.DMA((10, 8)), pltpu.SemaphoreType.DMA((10, 8))]
    scratch += [pltpu.VMEM((ROWS, 128), F32), pltpu.VMEM((ROWS, 128), BF), pltpu.VMEM((64, 32, 128), F32)]
    n_row, n_col = counts
    most = max(n_row, n_col)
    for _, size, first in PARTS:
        n1, n2 = (n_row, n_col) if first == "row" else (n_col, n_row)
        c1, c2 = size // n1, size // n1 // n2
        scratch += [
            pltpu.VMEM((size, 128), BF),
            pltpu.VMEM((n1 - 1, c1, 128), BF),
            pltpu.VMEM((c1, 128), F32),
            pltpu.VMEM((c1, 128), BF),
            pltpu.VMEM((n2 - 1, c2, 128), BF),
        ]
    scratch += [pltpu.SemaphoreType.DMA((len(PARTS), 4, most)), pltpu.SemaphoreType.DMA((len(PARTS), 4, most))]
    vmem = pl.BlockSpec(memory_space=pltpu.VMEM)
    return pl.pallas_call(
        functools.partial(net_kernel, counts),
        out_shape=(
            jax.ShapeDtypeStruct((2, 32, 128), F32),
            jax.ShapeDtypeStruct((64, 32, 128), BF),
            jax.ShapeDtypeStruct((ROWS, 128), BF),
        ),
        in_specs=[vmem] * 13,
        out_specs=(vmem, vmem, vmem),
        scratch_shapes=scratch,
        compiler_params=pltpu.CompilerParams(collective_id=1, has_side_effects=True, vmem_limit_bytes=56 * 2**20),
    )(*args, *tables)


def out_kernel(logits, features, g, o_logits, o_features, o_embed, o_first, o_second, o_bottom, o_return, o_final, o_read):
    o_logits[...] = logits[...]
    o_features[...] = features[...]
    for t in range(9):
        ta, tb = t // 3, t % 3
        for half in range(2):
            start = AT_RETURN + (t * 2 + half) * 128
            o_return[ta, tb, :, half * 128 : (half + 1) * 128] = g[start : start + 128, :].astype(F32)
        o_final[ta, tb] = g[AT_FINAL + t * 64 : AT_FINAL + (t + 1) * 64, :].astype(F32)
        o_bottom[ta, tb] = g[AT_BOTTOM + t * 256 : AT_BOTTOM + (t + 1) * 256, :].astype(F32)
        o_second[ta, tb] = g[AT_SECOND + t * 64 : AT_SECOND + (t + 1) * 64, :].astype(F32)
        start, low = (AT_FIRST + ta * 64, tb * 64) if tb < 2 else (AT_FIRST + (192 if ta < 2 else 256), ta % 2 * 64)
        o_first[ta, tb] = g[start : start + 64, low : low + 64].astype(F32)
    o_embed[...] = g[AT_FIRST + 256 : AT_FIRST + 272, 64:128].astype(F32)
    o_read[...] = g[AT_READ : AT_READ + 16, 0:64].astype(F32)[0:2]


def write_out(logits, features, g):
    shapes = [(2, 32, 128), (64, 32, 128), (16, 64), (3, 3, 64, 64), (3, 3, 64, 128), (3, 3, 256, 128), (3, 3, 128, 256), (3, 3, 64, 128), (2, 64)]
    vmem = pl.BlockSpec(memory_space=pltpu.VMEM)
    outs = pl.pallas_call(
        out_kernel,
        out_shape=tuple(jax.ShapeDtypeStruct(s, BF if n == 1 else F32) for n, s in enumerate(shapes)),
        in_specs=[vmem] * 3,
        out_specs=(vmem,) * 9,
        compiler_params=pltpu.CompilerParams(vmem_limit_bytes=32 * 2**20),
    )(logits, features, g)
    outs = list(outs)
    outs[2] = outs[2].T
    outs[4] = outs[4].transpose(0, 1, 3, 2)
    return tuple(outs)


def on_device(counts, *args):
    return write_out(*run_net(counts, *args))


def solution(mesh):
    counts = (mesh.shape["row"], mesh.shape["col"])
    cells = P(None, ("batch", "row"), "col")
    in_specs = (P(("batch", "row"), "col"),) + (P(),) * 7 + (cells,)
    out_specs = (cells, cells, P("batch", None)) + (P("batch", None, None, None),) * 5 + (P("batch", None),)
    return jax.shard_map(
        functools.partial(on_device, counts), mesh=mesh, in_specs=in_specs, out_specs=out_specs, check_vma=False
    )
```

time: 137 us -> 114 us (0.83)
  local copies, waits for them, and re-layouts: 15.2 us -> 3.2 us
  Pallas kernels: 118 us -> 109 us
  other arithmetic: 2.53 us -> 0 us
    pallas_call x1, Pallas kernels: 36.6 us -> 1.93 us  [write_out(): pl.pallas_call(out_kernel, out_shape=tuple((jax.ShapeDtypeStruct(s, BF if...]
    pallas_call x1, Pallas kernels: 81.7 us -> 108 us  [run_net(): pl.pallas_call(functools.partial(net_kernel, counts), out_shape=(jax.Shap...]
    unnamed x7 -> x6, local copies, waits for them, and re-layouts: 7.99 us -> 3.2 us
    slice x9 -> x0, local copies, waits for them, and re-layouts: 3.39 us -> none  [the longest x1 1.16 us: unlaid(): g[AT_RETURN:AT_RETURN + 2304].reshape(3, 3, 2, 128, 128)]
    reshape x5 -> x0, local copies, waits for them, and re-layouts: 2.98 us -> none  [the longest x1 1.11 us: unlaid(): g[AT_RETURN:AT_RETURN + 2304].reshape(3, 3, 2, 128, 128)]
    broadcast_in_dim x2 -> x0, other arithmetic: 1.69 us -> none  [the longest x1 0.9 us: unlaid(): by_second = jnp.concatenate([wide, last[:, None]], axis=1)]
where the time goes in v1:
time: 114 us; the launch traced here: 113 us
  Pallas kernels  109 us (96%)
  local copies, waits for them, and re-layouts  3.2 us (3%)
    pallas_call x1, Pallas kernels, run_net(): pl.pallas_call(functools.partial(net_kernel, counts), out_shape=(jax.Shap...  108 us
    unnamed x6, local copies, waits for them, and re-layouts  3.2 us

profile of v1, /device:TPU:1, one launch (start us, length us, event | category | flops | bytes accessed | tf_op | source)
XLA Modules:
  0.0 113.3 jit_solution(5031719906637350337)
XLA Ops:
  0.6 107.5 %shard_map.196 = (f32[2,32,128]{2,1,0:T(8,128)}, bf16[64,32,128]{2,1,0:T(8,128)(2,1)}, bf16[6144,128]{1,0:T(8,128)(2,1)}) custom-call(s32[32,128]{1,0:T(8,128)} %refs_0_.1, bf16[16,64]{1,0:T(8,128)(2,1)} %bitcast.5, bf16[3,3,64,64]{3,2,1,0:T(8,128)(2,1)} %refs_2_.1, bf16[3,3,64,128]{3,2,1,0:T(8,128)(2,1)} %bitcast.4, bf16[3,3,256,128]{3,2,1,0:T(8,128)(2,1)} %refs_4_.1, ...), custom_call_target="tpu_custom_call" | custom-call | tf_op jit(solution)/shard_map/pallas_call | solution.py:673
  108.2 0.0 copy-start
  108.2 1.4 %copy-done = bf16[6144,128]{1,0:T(8,128)(2,1)S(1)} copy-done((bf16[6144,128]{1,0:T(8,128)(2,1)S(1)}, bf16[6144,128]{1,0:T(8,128)(2,1)}, u32[]{:S(2)}) %copy-start) | copy-done | bytes 1572888
  109.6 0.0 copy-start.1
  109.6 1.0 copy-done.1
  110.6 0.0 copy-start.2
  110.6 0.8 copy-done.2
  111.4 1.9 %shard_map.197 = (f32[2,32,128]{2,1,0:T(8,128)}, bf16[64,32,128]{2,1,0:T(8,128)(2,1)}, f32[16,64]{1,0:T(8,128)}, f32[3,3,64,64]{3,2,1,0:T(8,128)}, f32[3,3,64,12...) custom-call(f32[2,32,128]{2,1,0:T(8,128)S(1)} %copy-done.2, ...), custom_call_target="tpu_custom_call" | custom-call | tf_op jit(solution)/shard_map/pallas_call | solution.py:707
Async XLA Ops:
  108.2 1.4 %copy-start = (bf16[6144,128]{1,0:T(8,128)(2,1)S(1)}, bf16[6144,128]{1,0:T(8,128)(2,1)}, u32[]{:S(2)}) copy-start(bf16[6144,128]{1,0:T(8,128)(2,1)} %get-tuple-element.23.g) | copy-start | bytes 4718596
  109.6 1.0 copy-start.1
  110.6 0.8 copy-start.2

commit v2 on v1

--- a/solution.py
+++ b/solution.py
@@ -15,7 +15,7 @@
 CELLS = DEEP * WIDE
 
 ROWS = 6144
-PARTS = ((0, 2048, "row"), (2048, 3072, "col"), (5120, 1024, "row"))
+PARTS = ((0, 1024, "row"), (1024, 1024, "col"), (2048, 1024, "row"), (3072, 2048, "col"), (5120, 1024, "row"))
 AT_RETURN, AT_FINAL, AT_BOTTOM, AT_SECOND, AT_FIRST, AT_READ = 0, 2304, 2880, 5184, 5760, 6080
 
 
@@ -154,14 +154,14 @@
         return [next(it) for _ in range(n)]
 
     syn, embt, k1, k2t, k3, k4, k5, rdo, cot, cS, cQ, cT, cU = take(13)
-    logits_ref, features_ref, grads_ref = take(3)
+    logits_ref, features_ref, embed_ref, grads_ref = take(4)
     xb, e0, z0, z1, f1, e1, z2, f2, e2, z3, e3, z4, e4, z5, f5, t5, t4, t3, t2, t1, fg, cp = take(22)
     w0, w1, w1b, w2, w2b, w3, w3b, w4, w4b, w5, w5b, r4, r4t = take(13)
     halos = [take(2) for _ in range(10)]
     sends, recvs = take(2)
     g_ref, whole, tall = take(3)
     stages = [take(5) for _ in PARTS]
-    sum_sends, sum_recvs = take(2)
+    sum_sends, sum_recvs, embed_row, embed_col, embed_sends, embed_recvs = take(6)
 
     n_row, n_col = counts
     row, col = lax.axis_index("row"), lax.axis_index("col")
@@ -303,6 +303,23 @@
             copy.start()
         flying[part] = copies
 
+    def embed_step(step, value=None):
+        if step > 0:
+            for copy in flying.pop("embed"):
+                copy.wait()
+            slots = embed_row if step == 1 else embed_col
+            value = sum(slots[d] for d in range(slots.shape[0]))
+        if step == 2:
+            return value
+        slots, (me, count, to) = (embed_row, ways["row"]) if step == 0 else (embed_col, ways["col"])
+        slots[me] = value
+        copies = [
+            remote(slots.at[me], slots.at[me], embed_sends.at[step, d], embed_recvs.at[step, d], to(d)) for d in range(1, count)
+        ]
+        for copy in copies:
+            copy.start()
+        flying["embed"] = copies
+
     bit = lax.broadcasted_iota(jnp.int32, (16, 1), 0)
     groups = []
     for a in range(4):
@@ -550,13 +567,15 @@
                         g_ref[start : start + 128, :] = piece if b == 0 else g_ref[start : start + 128, :] + piece
 
     sum_step(0, 0)
+    sum_step(1, 0)
     end(6, 2, 128, t4, copies)
     v = sum(mm(w4b[:, m * 512 : (m + 1) * 512], t4[m * 512 : (m + 1) * 512, :]) for m in range(4))
     t3[4 * 256 : 5 * 256, :] = sloped(v, z3[...])
     copies = begin(7, 1, 256, t3)
     for t in range(9):
         g_ref[AT_BOTTOM + t * 256 : AT_BOTTOM + (t + 1) * 256, :] = nt(t3[4 * 256 : 5 * 256, :], e2[t * 128 : (t + 1) * 128, :])
-    sum_step(1, 0)
+    sum_step(2, 0)
+    sum_step(3, 0)
     end(7, 1, 256, t3, copies)
 
     through = mm(w3b[...], t3[...]) * 0.25
@@ -573,6 +592,7 @@
             product = product + nt(e1[(a + ta) * 256 : (a + ta + 1) * 256, :], t2[start : start + 256, :])
         g_ref[AT_SECOND + ta * 192 : AT_SECOND + (ta + 1) * 192, :] = product[0:192, 0:128] + product[64:256, 128:256]
     sum_step(0, 1)
+    sum_step(1, 1)
     end(8, 2, 128, t2, copies)
 
     for a in range(2):
@@ -596,8 +616,12 @@
         g_ref[AT_FIRST + ta * 64 : AT_FIRST + (ta + 1) * 64, :] = value[:, 0:128]
         start = AT_FIRST + (192 if ta < 2 else 256)
         g_ref[start : start + 64, ta % 2 * 64 : ta % 2 * 64 + 64] = value[:, 128:192]
-    sum_step(1, 1)
+    g_ref[AT_FIRST + 256 : AT_FIRST + 320, 64:128] = jnp.zeros((64, 64), F32)
+    sum_step(4, 0)
+    sum_step(2, 1)
+    sum_step(3, 1)
     sum_step(0, 2)
+    sum_step(1, 2)
     end(9, 4, 64, t1, copies)
 
     total = jnp.zeros((64, 256), F32)
@@ -612,8 +636,7 @@
         start = ((a + 1) * 6 + 1) * 16
         total = total + nt(xb[start : start + 64, :], fg[a * 256 : (a + 1) * 256, :])
     total = sum(total[b * 16 : (b + 1) * 16, b * 64 : (b + 1) * 64] for b in range(4))
-    g_ref[AT_FIRST + 256 : AT_FIRST + 272, 64:128] = total
-    g_ref[AT_FIRST + 272 : AT_FIRST + 320, 64:128] = jnp.zeros((48, 64), F32)
+    embed_step(0, total)
 
     def lay(a):
         for t in range(2):
@@ -622,19 +645,23 @@
             for r in range(4):
                 tall[:, 16 * t + 4 * r + a, :] = laid[:, r * 128 : (r + 1) * 128]
 
-    sum_step(2, 0)
+    sum_step(4, 1)
+    sum_step(2, 2)
+    sum_step(3, 2)
     sum_step(0, 3)
-    sum_step(1, 2)
+    sum_step(1, 3)
     lay(0)
     lay(1)
-    sum_step(2, 1)
-    sum_step(1, 3)
+    embed_step(1)
+    sum_step(4, 2)
+    sum_step(2, 3)
+    sum_step(3, 3)
     lay(2)
     lay(3)
-    sum_step(2, 2)
     features_ref[...] = tall[...].astype(BF)
-    sum_step(2, 3)
-    for part in range(3):
+    sum_step(4, 3)
+    embed_ref[...] = embed_step(2)
+    for part in range(len(PARTS)):
         sum_step(part, 4)
     grads_ref[...] = whole[...]
 
@@ -669,22 +696,25 @@
             pltpu.VMEM((n2 - 1, c2, 128), BF),
         ]
     scratch += [pltpu.SemaphoreType.DMA((len(PARTS), 4, most)), pltpu.SemaphoreType.DMA((len(PARTS), 4, most))]
+    scratch += [pltpu.VMEM((n_row, 16, 64), F32), pltpu.VMEM((n_col, 16, 64), F32)]
+    scratch += [pltpu.SemaphoreType.DMA((2, most)), pltpu.SemaphoreType.DMA((2, most))]
     vmem = pl.BlockSpec(memory_space=pltpu.VMEM)
     return pl.pallas_call(
         functools.partial(net_kernel, counts),
         out_shape=(
             jax.ShapeDtypeStruct((2, 32, 128), F32),
             jax.ShapeDtypeStruct((64, 32, 128), BF),
+            jax.ShapeDtypeStruct((16, 64), F32),
             jax.ShapeDtypeStruct((ROWS, 128), BF),
         ),
         in_specs=[vmem] * 13,
-        out_specs=(vmem, vmem, vmem),
+        out_specs=(vmem,) * 4,
         scratch_shapes=scratch,
         compiler_params=pltpu.CompilerParams(collective_id=1, has_side_effects=True, vmem_limit_bytes=56 * 2**20),
     )(*args, *tables)
 
 
-def out_kernel(logits, features, g, o_logits, o_features, o_embed, o_first, o_second, o_bottom, o_return, o_final, o_read):
+def out_kernel(logits, features, embed, g, o_logits, o_features, o_embed, o_first, o_second, o_bottom, o_return, o_final, o_read):
     o_logits[...] = logits[...]
     o_features[...] = features[...]
     for t in range(9):
@@ -697,20 +727,20 @@
         o_second[ta, tb] = g[AT_SECOND + t * 64 : AT_SECOND + (t + 1) * 64, :].astype(F32)
         start, low = (AT_FIRST + ta * 64, tb * 64) if tb < 2 else (AT_FIRST + (192 if ta < 2 else 256), ta % 2 * 64)
         o_first[ta, tb] = g[start : start + 64, low : low + 64].astype(F32)
-    o_embed[...] = g[AT_FIRST + 256 : AT_FIRST + 272, 64:128].astype(F32)
+    o_embed[...] = embed[...]
     o_read[...] = g[AT_READ : AT_READ + 16, 0:64].astype(F32)[0:2]
 
 
-def write_out(logits, features, g):
+def write_out(logits, features, embed, g):
     shapes = [(2, 32, 128), (64, 32, 128), (16, 64), (3, 3, 64, 64), (3, 3, 64, 128), (3, 3, 256, 128), (3, 3, 128, 256), (3, 3, 64, 128), (2, 64)]
     vmem = pl.BlockSpec(memory_space=pltpu.VMEM)
     outs = pl.pallas_call(
         out_kernel,
         out_shape=tuple(jax.ShapeDtypeStruct(s, BF if n == 1 else F32) for n, s in enumerate(shapes)),
-        in_specs=[vmem] * 3,
+        in_specs=[vmem] * 4,
         out_specs=(vmem,) * 9,
         compiler_params=pltpu.CompilerParams(vmem_limit_bytes=32 * 2**20),
-    )(logits, features, g)
+    )(logits, features, embed, g)
     outs = list(outs)
     outs[2] = outs[2].T
     outs[4] = outs[4].transpose(0, 1, 3, 2)

time: 114 us -> 102 us (0.89)
  the two profiles are of different devices: /device:TPU:1 before, /device:TPU:65 now
where the time goes in v2:
time: 102 us
  Pallas kernels  97 us (95%)
  local copies, waits for them, and re-layouts  3.9 us (4%)
    pallas_call x1, Pallas kernels, run_net(): pl.pallas_call(functools.partial(net_kernel, counts), out_shape=(jax.Shap...  95.1 us
    unnamed x8, local copies, waits for them, and re-layouts  3.9 us

profile of v2, /device:TPU:65, one launch (start us, length us, event | category | flops | bytes accessed | tf_op | source)
XLA Modules:
  0.0 101.5 jit_solution(3070365875428365519)
XLA Ops:
  0.6 95.1 %shard_map.196 = (f32[2,32,128]{2,1,0:T(8,128)}, bf16[64,32,128]{2,1,0:T(8,128)(2,1)}, f32[16,64]{1,0:T(8,128)}, bf16[6144,128]{1,0:T(8,128)(2,1)}) custom-call(s32[32,128]{1,0:T(8,128)} %refs_0_.1, bf16[16,64]{1,0:T(8,128)(2,1)} %bitcast.5, bf16[3,3,64,64]{3,2,1,0:T(8,128)(2,1)} %refs_2_.1, bf16[3,3,64,128]{3,2,1,0:T(8,128)(2,1)} %bitcast.4, ...), custom_call_target="tpu_custom_call" | custom-call | tf_op jit(solution)/shard_map/pallas_call | solution.py:702
  95.7 0.0 copy-start
  95.7 1.4 %copy-done = bf16[6144,128]{1,0:T(8,128)(2,1)S(1)} copy-done((bf16[6144,128]{1,0:T(8,128)(2,1)S(1)}, bf16[6144,128]{1,0:T(8,128)(2,1)}, u32[]{:S(2)}) %copy-start) | copy-done | bytes 1572888
  97.1 0.0 copy-start.1
  97.1 1.0 %copy-done.1 = bf16[64,32,128]{2,1,0:T(8,128)(2,1)S(1)} copy-done((bf16[64,32,128]{2,1,0:T(8,128)(2,1)S(1)}, bf16[64,32,128]{2,1,0:T(8,128)(2,1)}, u32[]{:S(2)}) %copy-start.1) | copy-done | bytes 524312
  98.2 0.0 copy-start.2
  98.2 0.8 copy-done.2
  98.9 0.0 copy-start.3
  98.9 0.7 copy-done.3
  99.6 1.9 %shard_map.197 = (f32[2,32,128]{2,1,0:T(8,128)}, bf16[64,32,128]{2,1,0:T(8,128)(2,1)}, f32[16,64]{1,0:T(8,128)}, f32[3,3,64,64]{3,2,1,0:T(8,128)}, f32[3,3,64,12...) custom-call(f32[2,32,128]{2,1,0:T(8,128)S(1)} %copy-done.2, ...), custom_call_target="tpu_custom_call" | custom-call | tf_op jit(solution)/shard_map/pallas_call | solution.py:737
Async XLA Ops:
  95.7 1.4 %copy-start = (bf16[6144,128]{1,0:T(8,128)(2,1)S(1)}, bf16[6144,128]{1,0:T(8,128)(2,1)}, u32[]{:S(2)}) copy-start(bf16[6144,128]{1,0:T(8,128)(2,1)} %get-tuple-element.25.g) | copy-start | bytes 4718596
  97.1 1.0 %copy-start.1 = (bf16[64,32,128]{2,1,0:T(8,128)(2,1)S(1)}, bf16[64,32,128]{2,1,0:T(8,128)(2,1)}, u32[]{:S(2)}) copy-start(bf16[64,32,128]{2,1,0:T(8,128)(2,1)} %get-tuple-element.23.features) | copy-start | bytes 1572868
  98.2 0.8 copy-start.2
  98.9 0.7 copy-start.3

commit v3 on v2

v3 whole, which is shorter than its diff:
```python
import functools

import jax
import jax.numpy as jnp
import numpy as np
from jax import lax
from jax.experimental import pallas as pl
from jax.experimental.pallas import tpu as pltpu
from jax.sharding import PartitionSpec as P

BF, F32 = jnp.bfloat16, jnp.float32
MESH = pl.DeviceIdType.MESH

DEEP, WIDE = 8, 32
CELLS = DEEP * WIDE
EXT = CELLS + 128

ROWS = 6144
PARTS = ((0, 1024, "row"), (1024, 1024, "col"), (2048, 1024, "row"), (3072, 2048, "col"), (5120, 1024, "row"))
AT_RETURN, AT_FINAL, AT_BOTTOM, AT_SECOND, AT_FIRST, AT_READ = 0, 2304, 2880, 5184, 5760, 6080


def ranged(values, start, size):
    return values.at[pl.ds(pl.multiple_of(start, 16), size), :]


def bounds(depth):
    left = 2 * WIDE * depth
    return WIDE * depth, left, left + 16, left + 32


def lane_of(r, q, depth):
    if not (-depth <= r < DEEP + depth and -depth <= q < WIDE + depth):
        return None
    row_in, col_in = 0 <= r < DEEP, 0 <= q < WIDE
    down, left, right, corner = bounds(depth)
    if row_in and col_in:
        return r * WIDE + q
    i = r + depth if r < 0 else r - DEEP
    j = q + depth if q < 0 else q - WIDE
    if col_in:
        return CELLS + (0 if r < 0 else down) + i * WIDE + q
    if row_in:
        return CELLS + (left if q < 0 else right) + j * DEEP + r
    return CELLS + corner + CORNERS[(-1 if r < 0 else 1, -1 if q < 0 else 1)] * depth * depth + i * depth + j


def shift_tables(depth, size):
    tables = []
    for dr in (-1, 0, 1):
        for dc in (-1, 0, 1):
            m = np.zeros((size, EXT), np.float32)
            for r in range(-1, DEEP + 1):
                for q in range(-1, WIDE + 1):
                    source = lane_of(r + dr, q + dc, depth)
                    if source is not None:
                        m[source, lane_of(r, q, 1)] = 1
            tables.append(m)
    return np.concatenate(tables)


def pick_table(depth):
    down, left, right, corner = bounds(depth)
    m = np.zeros((corner + 16, CELLS), np.float32)
    for i in range(depth):
        for q in range(WIDE):
            m[i * WIDE + q, i * WIDE + q] = 1
            m[down + i * WIDE + q, (DEEP - depth + i) * WIDE + q] = 1
        for r in range(DEEP):
            m[left + i * DEEP + r, r * WIDE + i] = 1
            m[right + i * DEEP + r, r * WIDE + WIDE - depth + i] = 1
        for j in range(depth):
            for k, (r, q) in enumerate(((0, 0), (0, WIDE - depth), (DEEP - depth, 0), (DEEP - depth, WIDE - depth))):
                m[corner + k * depth * depth + i * depth + j, (r + i) * WIDE + q + j] = 1
    return m


CORNERS = {(-1, -1): 3, (-1, 1): 2, (1, -1): 1, (1, 1): 0}


def spread_table():
    m = np.zeros((512, 512), np.float32)
    for r in range(4):
        for w in range(128):
            m[r * 128 + w, (w % 4) * 128 + r * WIDE + w // 4] = 1
    return m


SHIFT = shift_tables(1, EXT)
SHIFT_FAR = shift_tables(2, 512)
PICK, PICK_FAR = pick_table(1), pick_table(2)
SPREAD = spread_table()

UNDER = (((0,), (1, 2)), ((0, 1), (2,)))
OVER = ((2,), (1, 2), (0, 1), (0,))
BASE = (0, 1, 1, 2)


def mm(a, b):
    return jnp.dot(a, b, preferred_element_type=F32)


def nt(a, b):
    return lax.dot_general(a, b, (((1,), (1,)), ((), ())), preferred_element_type=F32)


def logistic(z):
    return 0.5 + 0.5 * jnp.tanh(0.5 * z)


def activated(v):
    stored = v.astype(BF)
    z = stored.astype(F32)
    return stored, (z * logistic(z)).astype(BF)


def sloped(incoming, stored):
    z = stored.astype(F32)
    s = logistic(z)
    return (incoming * (s * (1.0 + z * (1.0 - s)))).astype(BF)


def remote(src, dst, send, recv, target):
    return pltpu.make_async_remote_copy(
        src_ref=src, dst_ref=dst, send_sem=send, recv_sem=recv, device_id=target, device_id_type=MESH
    )


SIDES = ((-1, 0), (1, 0), (0, -1), (0, 1), (-1, -1), (-1, 1), (1, -1), (1, 1))


def net_kernel(counts, *refs):
    it = iter(refs)

    def take(n):
        return [next(it) for _ in range(n)]

    syn, embt, k1, k2t, k3, k4, k5, rdo, cot, eye, cQ, cQ2, cU, cS_hbm, cF_hbm = take(15)
    logits_ref, features_ref, embed_ref, grads_ref = take(4)
    xb, e0, z0, z1, f1, e1, z2, f2, e2, z3, e3, z4, e4, z5, f5, t5, t4, t3, t2, t1, fg, cp = take(22)
    w0, w1, w1b, w2, w2b, w3, w3b, w4, w4b, w5, w5b, r4, r4t = take(13)
    halos = [take(2) for _ in WIDTHS]
    cS, cF, far, loads = take(4)
    sends, recvs = take(2)
    g_ref, whole, tall = take(3)
    stages = [take(5) for _ in PARTS]
    sum_sends, sum_recvs, embed_row, embed_col, embed_sends, embed_recvs = take(6)

    n_row, n_col = counts
    row, col = lax.axis_index("row"), lax.axis_index("col")
    there = {
        (-1, 0): row > 0,
        (1, 0): row < n_row - 1,
        (0, -1): col > 0,
        (0, 1): col < n_col - 1,
    }
    for dr in (-1, 1):
        for dc in (-1, 1):
            there[dr, dc] = jnp.logical_and(there[dr, 0], there[0, dc])

    def place(dr, dc):
        return {"row": (row + dr + n_row) % n_row, "col": (col + dc + n_col) % n_col}

    load_near = pltpu.make_async_copy(cS_hbm, cS, loads.at[0])
    load_far = pltpu.make_async_copy(cF_hbm, cF, loads.at[1])
    load_near.start()
    load_far.start()

    partners = [(d, 0) for d in range(1, n_row)] + [(0, d) for d in range(1, n_col)] + list(SIDES[4:])
    barrier = pltpu.get_barrier_semaphore()
    for partner in partners:
        pl.semaphore_signal(barrier, inc=1, device_id=place(*partner), device_id_type=MESH)

    lane = lax.broadcasted_iota(jnp.int32, (1, 128), 1)
    sixteen = lax.broadcasted_iota(jnp.int32, (16, 1), 0)

    def inside(depth):
        down, left, right, corner = bounds(depth)
        spans = [(0, down, (-1, 0)), (down, left, (1, 0)), (left, left + DEEP * depth, (0, -1)), (right, right + DEEP * depth, (0, 1))]
        spans += [(corner + k * depth * depth, corner + (k + 1) * depth * depth, side) for side, k in CORNERS.items()]
        masks = []
        for tile in range(depth):
            at = lane + tile * 128
            keep = lane < 0
            for low, high, side in spans:
                keep = jnp.logical_or(keep, jnp.logical_and(jnp.logical_and(at >= low, at < high), there[side]))
            masks.append(keep)
        return masks

    near_masks, far_masks = inside(1), inside(2)

    def fenced(v):
        return jnp.concatenate([v[:, :CELLS], jnp.where(near_masks[0], v[:, CELLS:], 0.0)], axis=1)

    def begin(n, depth, pieces, ahead=None):
        out, into = halos[n]
        down, left, right, corner = bounds(depth)
        pick = (cQ if depth == 1 else cQ2)[...]
        start = 0
        for piece in pieces:
            out[:, start : start + piece.shape[0]] = nt(pick, piece).astype(BF)
            start += piece.shape[0]
        size = {(-1, 0): (0, down, down), (1, 0): (down, left, 0), (0, -1): (left, right, right), (0, 1): (right, corner, left)}
        copies = []
        for k, (dr, dc) in enumerate(SIDES):
            if (dr, dc) in size:
                low, high, target = size[dr, dc]
            else:
                low, high = corner, corner + 16
                target = 128 * depth + 16 * CORNERS[-dr, -dc]
            copies.append(
                remote(out.at[low:high], into.at[target : target + high - low], sends.at[n, k], recvs.at[n, k], place(dr, dc))
            )
        if ahead is not None:
            ahead()
        for copy in copies:
            copy.start()
        return copies

    def end(n, depth, copies):
        into = halos[n][1]
        corner = bounds(depth)[3]
        for copy in copies:
            copy.wait()
        ends = 0.0
        for k in range(4):
            tile = into[128 * depth + 16 * k : 128 * depth + 16 * (k + 1), :].astype(F32)
            ends = ends + jnp.where(sixteen // (depth * depth) == k, tile, 0.0)
        into[corner : corner + 16, :] = ends.astype(BF)

    def ring(n, depth, start, width):
        into = halos[n][1]
        tiles = []
        for tile, keep in enumerate(near_masks if depth == 1 else far_masks):
            turned = nt(eye[0:width, 0:width], into[tile * 128 : (tile + 1) * 128, start : start + width])
            tiles.append(jnp.where(keep, turned, 0.0).astype(BF))
        return tiles

    def extend(p, width, ref, size):
        for ea in range(p + 2):
            for eb in range(p + 2):
                dr, dc = (ea > p) - (ea < 1), (eb > p) - (eb < 1)
                if (dr, dc) == (0, 0):
                    continue
                start = (((ea - 1) % p + 1) * (p + 2) + (eb - 1) % p + 1) * width
                at = (dr * 3 + dc + 4) * EXT
                moved = mm(ref[start : start + width, :], cS[at : at + EXT, 0:size])
                start = (ea * (p + 2) + eb) * width
                ref[start : start + width, 0:size] = moved.astype(BF)

    ways = {"row": (row, n_row, lambda d: place(d, 0)), "col": (col, n_col, lambda d: place(0, d))}
    flying = {}

    def sum_step(part, step):
        start, size, first = PARTS[part]
        s1, r1, h1, s2, r2 = stages[part]
        me1, n1, to1 = ways[first]
        me2, n2, to2 = ways["col" if first == "row" else "row"]
        c1, c2 = size // n1, size // n1 // n2
        for copy in flying.pop(part, ()):
            copy.wait()
        if step == 4:
            return
        if step == 0:
            s1[...] = g_ref[start : start + size, :].astype(BF)
        elif step == 1:
            total = g_ref[pl.ds(pl.multiple_of(start + me1 * c1, 16), c1), :]
            for d in range(n1 - 1):
                total = total + r1[d].astype(F32)
            h1[...] = total
            s2[...] = total.astype(BF)
        elif step == 2:
            total = h1[pl.ds(pl.multiple_of(me2 * c2, 16), c2), :]
            for d in range(n2 - 1):
                total = total + r2[d].astype(F32)
            whole[pl.ds(pl.multiple_of(start + me1 * c1 + me2 * c2, 16), c2), :] = total.astype(BF)
        copies = []
        for d in range(1, n1 if step in (0, 3) else n2):
            if step == 0:
                src, dst, to = ranged(s1, (me1 + d) % n1 * c1, c1), r1.at[d - 1], to1
            elif step == 1:
                src, dst, to = ranged(s2, (me2 + d) % n2 * c2, c2), r2.at[d - 1], to2
            elif step == 2:
                src = dst = ranged(whole, start + me1 * c1 + me2 * c2, c2)
                to = to2
            else:
                src = dst = ranged(whole, start + me1 * c1, c1)
                to = to1
            copies.append(remote(src, dst, sum_sends.at[part, step, d], sum_recvs.at[part, step, d], to(d)))
        for copy in copies:
            copy.start()
        flying[part] = copies

    def embed_step(step, value=None):
        if step > 0:
            for copy in flying.pop("embed"):
                copy.wait()
            slots = embed_row if step == 1 else embed_col
            value = sum(slots[d] for d in range(slots.shape[0]))
        if step == 2:
            return value
        slots, (me, count, to) = (embed_row, ways["row"]) if step == 0 else (embed_col, ways["col"])
        slots[me] = value
        copies = [
            remote(slots.at[me], slots.at[me], embed_sends.at[step, d], embed_recvs.at[step, d], to(d)) for d in range(1, count)
        ]
        for copy in copies:
            copy.start()
        flying["embed"] = copies

    bit = lax.broadcasted_iota(jnp.int32, (16, 1), 0)
    groups = []
    for a in range(4):
        for t in range(2):
            line = [(syn[16 * t + 4 * r + a : 16 * t + 4 * r + a + 1, :] >> bit) & 1 for r in range(4)]
            groups.append(jnp.concatenate(line, axis=1))
    bits = jnp.concatenate(groups, axis=0).astype(F32).astype(BF)
    phased = mm(bits, cU[...]).astype(BF)
    for a in range(4):
        for t in range(2):
            for b in range(4):
                start = ((a + 1) * 6 + b + 1) * 16
                xb[start : start + 16, t * 128 : (t + 1) * 128] = phased[(a * 2 + t) * 16 : (a * 2 + t + 1) * 16, b * 128 : (b + 1) * 128]
    wide = cot[...].astype(F32)
    groups = []
    for a in range(4):
        for t in range(2):
            line = jnp.concatenate([wide[:, 16 * t + 4 * r + a, :] for r in range(4)], axis=1)
            groups.append(jnp.concatenate([line, jnp.zeros((6, 512), F32)], axis=0))
    phased = mm(jnp.concatenate(groups, axis=0).astype(BF), cU[...])
    for a in range(4):
        for t in range(2):
            start = (a * 2 + t) * 8
            pieces = [phased[start : start + 4, b * 128 : (b + 1) * 128] for b in range(4)]
            cp[a * 16 : (a + 1) * 16, t * 128 : (t + 1) * 128] = jnp.concatenate(pieces, axis=0).astype(BF)

    inner = [((a + 1) * 6 + 1) * 16 for a in range(4)]
    pieces = [jnp.concatenate([xb[i : i + 64, 0:CELLS] for i in inner], axis=0), cp[:, 0:CELLS]]
    copies = begin(0, 1, pieces, lambda: pl.semaphore_wait(barrier, len(partners)))

    def beside(blocks, i, blank):
        return jnp.concatenate(blocks + [blank] if i == 0 else [blank] + blocks, axis=0)

    def added(k, rows, cols):
        return sum(k[ta, tb].astype(F32) for ta in rows for tb in cols).astype(BF)

    def arrange_first():
        repeat = (lax.broadcasted_iota(jnp.int32, (16, 96), 1) % 16 == lax.broadcasted_iota(jnp.int32, (16, 96), 0)).astype(F32).astype(BF)
        tiled = mm(nt(eye[:64, :64], embt[...]).astype(BF), repeat)
        own = lax.broadcasted_iota(jnp.int32, (64, 96), 1) // 16
        for j in range(6):
            w0[j * 64 : (j + 1) * 64, :] = jnp.where(own == j, tiled, 0.0).astype(BF)
        for ta in range(3):
            for i in range(2):
                w1[i * 64 : (i + 1) * 64, ta * 256 : (ta + 1) * 256] = sum(
                    mm(k1[ta, tb], eye[(tb + i) * 64 : (tb + i + 1) * 64, :]) for tb in range(3)
                ).astype(BF)

    def arrange_second():
        blank, empty = jnp.zeros((64, 128), BF), jnp.zeros((64, 64), BF)
        for ta in range(3):
            for i in range(2):
                line = beside([k2t[ta, tb] for tb in range(3)], i, blank)
                w2[i * 128 : (i + 1) * 128, ta * 256 : (ta + 1) * 256] = nt(eye[:128, :128], line).astype(BF)
                for tb in range(3):
                    w2b[i * 64 : (i + 1) * 64, ta * 512 + (tb + i) * 128 : ta * 512 + (tb + i + 1) * 128] = k2t[2 - ta, 2 - tb]
                hole = ta * 512 + (384 if i == 0 else 0)
                w2b[i * 64 : (i + 1) * 64, hole : hole + 128] = blank
                line = beside([k1[2 - ta, 2 - tb] for tb in range(3)], i, empty)
                w1b[i * 64 : (i + 1) * 64, ta * 256 : (ta + 1) * 256] = nt(eye[:64, :64], line).astype(BF)

    def arrange_bottom():
        for t in range(9):
            w3[:, t * 128 : (t + 1) * 128] = k3[t // 3, t % 3]
            w3b[:, t * 256 : (t + 1) * 256] = nt(eye[:128, :128], k3[2 - t // 3, 2 - t % 3]).astype(BF)

    def arrange_return():
        for pa in range(2):
            for pb in range(2):
                for s in range(2):
                    for u in range(2):
                        block = added(k4, UNDER[pa][s], UNDER[pb][u])
                        w4[(pa * 2 + pb) * 128 : (pa * 2 + pb + 1) * 128, (s * 2 + u) * 256 : (s * 2 + u + 1) * 256] = block
                        at = OVER.index(UNDER[pa][s]) * 4 + OVER.index(UNDER[pb][u])
                        w4b[:, at * 128 : (at + 1) * 128] = nt(eye[...], block).astype(BF)

    def arrange_final():
        for pa in range(2):
            for pb in range(2):
                for s in range(2):
                    for u in range(2):
                        start = pa * 128 + (1 - pb) * 64
                        w5[start : start + 64, (s * 2 + u) * 128 : (s * 2 + u + 1) * 128] = added(k5, UNDER[pa][s], UNDER[pb][u])
        for ea in range(4):
            for pair in range(2):
                stack = jnp.concatenate([added(k5, OVER[ea], OVER[2 * pair + i]) for i in range(2)], axis=0)
                at = ea * 2 + pair
                w5b[:, at * 128 : (at + 1) * 128] = nt(eye[:128, :128], stack).astype(BF)

    def arrange_readout():
        repeat = (lax.broadcasted_iota(jnp.int32, (64, 256), 1) % 64 == lax.broadcasted_iota(jnp.int32, (64, 256), 0)).astype(F32).astype(BF)
        tiled = mm(rdo[...], repeat)
        tiled = jnp.concatenate([tiled, jnp.zeros((2, 256), F32)] * 4, axis=0)
        own = lax.broadcasted_iota(jnp.int32, (16, 256), 1) // 64 == lax.broadcasted_iota(jnp.int32, (16, 256), 0) // 4
        r4[...] = jnp.where(own, tiled, 0.0).astype(BF)
        r4t[...] = nt(eye[...], r4[...]).astype(BF)

    arrange_first()
    arrange_readout()
    load_near.wait()
    end(0, 1, copies)
    (tile,) = ring(0, 1, 0, 256)
    for a in range(4):
        xb[inner[a] : inner[a] + 64, CELLS:EXT] = tile[a * 64 : (a + 1) * 64, :]
    cp[:, CELLS:EXT] = ring(0, 1, 256, 64)[0]
    extend(4, 16, xb, EXT)

    for ea in range(6):
        stored, active = activated(mm(w0[...], xb[ea * 96 : (ea + 1) * 96, :]))
        e0[ea * 384 : (ea + 1) * 384, :] = active
        if 1 <= ea <= 4:
            z0[(ea - 1) * 256 : ea * 256, :] = stored[64:320, 0:CELLS]

    for a in range(4):
        for pair in range(2):
            v = sum(
                mm(w1[:, ta * 256 : (ta + 1) * 256], e0[((a + ta) * 6 + 2 * pair) * 64 : ((a + ta) * 6 + 2 * pair + 4) * 64, :])
                for ta in range(3)
            )
            start = (a * 4 + 2 * pair) * 64
            z1[start : start + 128, :], f1[start : start + 128, :] = activated(fenced(v))

    def pooled(ref, side, width, a, b, size):
        spots = [((2 * a + i) * side + 2 * b + j) * width for i in range(2) for j in range(2)]
        return (sum(ref[s : s + width, 0:size].astype(F32) for s in spots) * 0.25).astype(BF)

    for a in range(2):
        for b in range(2):
            start = ((a + 1) * 4 + b + 1) * 64
            e1[start : start + 64, :] = pooled(f1, 4, 64, a, b, EXT)
    extend(2, 64, e1, CELLS)
    arrange_second()

    for a in range(2):
        v = sum(mm(w2[:, ta * 256 : (ta + 1) * 256], e1[(a + ta) * 256 : (a + ta + 1) * 256, 0:CELLS]) for ta in range(3))
        z2[a * 256 : (a + 1) * 256, 0:CELLS], f2[a * 256 : (a + 1) * 256, 0:CELLS] = activated(v)
    e2[4 * 128 : 5 * 128, 0:CELLS] = pooled(f2, 2, 128, 0, 0, CELLS)
    copies = begin(1, 1, [e2[4 * 128 : 5 * 128, 0:CELLS]])
    later = begin(2, 1, [z2[0:256, 0:CELLS], z2[256:512, 0:CELLS]])
    arrange_bottom()
    arrange_final()
    end(1, 1, copies)
    e2[4 * 128 : 5 * 128, CELLS:EXT] = ring(1, 1, 0, 128)[0]
    extend(1, 128, e2, CELLS)

    z3[...], e3[4 * 256 : 5 * 256, 0:CELLS] = activated(mm(w3[...], e2[:, 0:CELLS]))
    copies = begin(3, 1, [e3[4 * 256 : 5 * 256, 0:CELLS]])
    arrange_return()
    end(2, 1, later)
    for a in range(2):
        z2[a * 256 : (a + 1) * 256, CELLS:EXT] = ring(2, 1, a * 256, 256)[0]
        f2[a * 256 : (a + 1) * 256, CELLS:EXT] = activated(z2[a * 256 : (a + 1) * 256, CELLS:EXT])[1]
    end(3, 1, copies)
    e3[4 * 256 : 5 * 256, CELLS:EXT] = ring(3, 1, 0, 256)[0]
    extend(1, 256, e3, EXT)

    for a in range(2):
        for b in range(2):
            n = a * 2 + b
            v = sum(
                mm(w4[n * 128 : (n + 1) * 128, s * 512 : (s + 1) * 512], e3[((a + s) * 3 + b) * 256 : ((a + s) * 3 + b + 2) * 256, :])
                for s in range(2)
            )
            v = v + f2[n * 128 : (n + 1) * 128, :].astype(F32)
            start = ((a + 1) * 4 + b + 1) * 128
            z4[n * 128 : (n + 1) * 128, :], e4[start : start + 128, :] = activated(fenced(v))
    extend(2, 128, e4, EXT)

    RUNS = ((0, 1, 64, 64), (1, 2, 0, 128), (3, 1, 0, 64))
    for a in range(4):
        for b, many, first, size in RUNS:
            base = (a % 2) * 128 + first
            v = sum(
                mm(w5[base : base + size, s * 256 : (s + 1) * 256], e4[((BASE[a] + s) * 4 + BASE[b]) * 128 : ((BASE[a] + s) * 4 + BASE[b] + 2) * 128, :])
                for s in range(2)
            )
            start = (a * 4 + b) * 64
            v = v + f1[start : start + size, :].astype(F32)
            z5[start : start + size, :] = v.astype(BF)

    for a in range(4):
        back = mm(r4t[...], cp[a * 16 : (a + 1) * 16, :])
        start = ((a + 1) * 6 + 1) * 64
        t5[start : start + 256, :] = sloped(back, z5[a * 256 : (a + 1) * 256, :])
    extend(4, 64, t5, CELLS)
    for a in range(2):
        for b in range(2):
            v = sum(
                mm(w5b[:, m * 256 : (m + 1) * 256], t5[((2 * a + m) * 6 + 2 * b) * 64 : ((2 * a + m) * 6 + 2 * b + 4) * 64, 0:CELLS])
                for m in range(4)
            )
            start = ((a + 1) * 4 + b + 1) * 128
            n = a * 2 + b
            t4[start : start + 128, 0:CELLS] = sloped(v, z4[n * 128 : (n + 1) * 128, 0:CELLS])
    copies = begin(4, 1, [t4[((a + 1) * 4 + 1) * 128 : ((a + 1) * 4 + 3) * 128, 0:CELLS] for a in range(2)])

    sums = {}
    for a in range(4):
        for s in range(2):
            for b, many, first, size in RUNS:
                start = ((BASE[a] + s) * 4 + BASE[b]) * 128
                t_start = ((a + 1) * 6 + b + 1) * 64
                product = nt(t5[t_start : t_start + size, 0:CELLS], e4[start : start + 256, 0:CELLS])
                for m in range(many):
                    key = (a % 2, s, (b + m) % 2)
                    block = product[m * 64 : (m + 1) * 64, :]
                    sums[key] = sums[key] + block if key in sums else block

    def reads(parity, tap):
        return 0 if tap in UNDER[parity][0] else 1

    for ta in range(3):
        rowed = [sums[0, reads(0, ta), pb] + sums[1, reads(1, ta), pb] for pb in range(2)]
        for tb in range(3):
            value = sum(rowed[pb][:, reads(pb, tb) * 128 : (reads(pb, tb) + 1) * 128] for pb in range(2))
            start = AT_FINAL + (ta * 3 + tb) * 64
            g_ref[start : start + 64, :] = value

    for b in range(2):
        for u in range(2):
            parts = {}
            for a in range(2):
                for s in range(2):
                    start = ((a + 1) * 4 + b + 1) * 128
                    from_ = ((a + s) * 3 + b + u) * 256
                    parts[a, s] = nt(t4[start : start + 128, 0:CELLS], e3[from_ : from_ + 256, 0:CELLS])
            for ta in range(3):
                value = parts[0, reads(0, ta)] + parts[1, reads(1, ta)]
                for tb in UNDER[b][u]:
                    for half in range(2):
                        start = AT_RETURN + ((ta * 3 + tb) * 2 + half) * 128
                        piece = value[:, half * 128 : (half + 1) * 128]
                        g_ref[start : start + 128, :] = piece if b == 0 else g_ref[start : start + 128, :] + piece

    sum_step(0, 0)
    sum_step(1, 0)
    total = jnp.zeros((16, 256), F32)
    for a in range(4):
        f5[a * 256 : (a + 1) * 256, :] = activated(z5[a * 256 : (a + 1) * 256, 0:CELLS])[1]
        total = total + nt(cp[a * 16 : (a + 1) * 16, 0:CELLS], f5[a * 256 : (a + 1) * 256, :])
    total = sum(total[b * 4 : (b + 1) * 4, b * 64 : (b + 1) * 64] for b in range(4))
    g_ref[AT_READ:ROWS, :] = jnp.zeros((ROWS - AT_READ, 128), F32)
    g_ref[AT_READ : AT_READ + 4, 0:64] = total

    end(4, 1, copies)
    for a in range(2):
        start = ((a + 1) * 4 + 1) * 128
        t4[start : start + 256, CELLS:EXT] = ring(4, 1, a * 256, 256)[0]
    extend(2, 128, t4, CELLS)
    v = sum(mm(w4b[:, m * 512 : (m + 1) * 512], t4[m * 512 : (m + 1) * 512, 0:CELLS]) for m in range(4))
    far[:, 0:CELLS] = sloped(v, z3[...])
    copies = begin(5, 2, [far[:, 0:CELLS]])
    for t in range(9):
        g_ref[AT_BOTTOM + t * 256 : AT_BOTTOM + (t + 1) * 256, :] = nt(far[:, 0:CELLS], e2[t * 128 : (t + 1) * 128, 0:CELLS])
    sum_step(2, 0)
    sum_step(3, 0)
    groups = []
    for a in range(4):
        here = f5[a * 256 : (a + 1) * 256, :]
        value = mm(r4[...], here)
        for t in range(2):
            groups.append(jnp.concatenate([value[b * 4 : (b + 1) * 4, t * 128 : (t + 1) * 128] for b in range(4)], axis=1))
    value = jnp.concatenate(groups, axis=0)
    laid = 0.0
    for _ in range(3):
        piece = value.astype(BF)
        laid = laid + nt(piece, cU[...])
        value = value - piece.astype(F32)
    for a in range(4):
        for t in range(2):
            for r in range(4):
                h = 16 * t + 4 * r + a
                logits_ref[:, h : h + 1, :] = laid[(a * 2 + t) * 4 : (a * 2 + t) * 4 + 2, r * 128 : (r + 1) * 128].reshape(2, 1, 128)
    load_far.wait()
    end(5, 2, copies)
    far[:, 256:384], far[:, 384:512] = ring(5, 2, 0, 256)
    for n in range(9):
        t3[n * 256 : (n + 1) * 256, :] = mm(far[...], cF[n * 512 : (n + 1) * 512, :]).astype(BF)

    through = mm(w3b[...], t3[...]) * 0.25
    for a in range(2):
        for b in range(2):
            n = a * 2 + b
            start = ((a + 1) * 4 + b + 1) * 128
            v = fenced(t4[start : start + 128, :].astype(F32) + through)
            t2[start : start + 128, :] = sloped(v, z2[n * 128 : (n + 1) * 128, :])
    for ta in range(3):
        product = 0.0
        for a in range(2):
            start = ((a + 1) * 4 + 1) * 128
            product = product + nt(e1[(a + ta) * 256 : (a + ta + 1) * 256, 0:CELLS], t2[start : start + 256, 0:CELLS])
        g_ref[AT_SECOND + ta * 192 : AT_SECOND + (ta + 1) * 192, :] = product[0:192, 0:128] + product[64:256, 128:256]
    sum_step(0, 1)
    sum_step(1, 1)
    extend(2, 128, t2, EXT)

    for a in range(2):
        v = sum(mm(w2b[:, ta * 512 : (ta + 1) * 512], t2[(a + ta) * 512 : (a + ta + 1) * 512, :]) for ta in range(3)) * 0.25
        for b in range(2):
            for i in range(2):
                for j in range(2):
                    fa, fb = 2 * a + i, 2 * b + j
                    start = ((fa + 1) * 6 + fb + 1) * 64
                    n = (fa * 4 + fb) * 64
                    t1[start : start + 64, :] = sloped(fenced(t5[start : start + 64, :].astype(F32) + v[b * 64 : (b + 1) * 64, :]), z1[n : n + 64, :])
    for ta in range(3):
        product = 0.0
        for a in range(4):
            for pair in range(2):
                start = ((a + 1) * 6 + 2 * pair + 1) * 64
                from_ = ((a + ta) * 6 + 2 * pair) * 64
                product = product + nt(t1[start : start + 128, 0:CELLS], e0[from_ : from_ + 256, 0:CELLS])
        value = product[0:64, 0:192] + product[64:128, 64:256]
        g_ref[AT_FIRST + ta * 64 : AT_FIRST + (ta + 1) * 64, :] = value[:, 0:128]
        start = AT_FIRST + (192 if ta < 2 else 256)
        g_ref[start : start + 64, ta % 2 * 64 : ta % 2 * 64 + 64] = value[:, 128:192]
    g_ref[AT_FIRST + 256 : AT_FIRST + 320, 64:128] = jnp.zeros((64, 64), F32)
    sum_step(4, 0)
    extend(4, 64, t1, CELLS)

    total = jnp.zeros((64, 256), F32)
    for a in range(4):
        for pair in range(2):
            v = sum(
                mm(w1b[:, ta * 256 : (ta + 1) * 256], t1[((a + ta) * 6 + 2 * pair) * 64 : ((a + ta) * 6 + 2 * pair + 4) * 64, 0:CELLS])
                for ta in range(3)
            )
            start = (a * 4 + 2 * pair) * 64
            fg[start : start + 128, :] = sloped(v, z0[start : start + 128, :])
        start = ((a + 1) * 6 + 1) * 16
        total = total + nt(xb[start : start + 64, 0:CELLS], fg[a * 256 : (a + 1) * 256, :])
    total = sum(total[b * 16 : (b + 1) * 16, b * 64 : (b + 1) * 64] for b in range(4))
    embed_step(0, total)

    def lay(a):
        for t in range(2):
            line = jnp.concatenate([fg[(a * 4 + b) * 64 : (a * 4 + b + 1) * 64, t * 128 : (t + 1) * 128] for b in range(4)], axis=1)
            laid = nt(line, cU[...])
            for r in range(4):
                tall[:, 16 * t + 4 * r + a, :] = laid[:, r * 128 : (r + 1) * 128]

    sum_step(2, 1)
    sum_step(3, 1)
    sum_step(0, 2)
    sum_step(1, 2)
    sum_step(4, 1)
    lay(0)
    lay(1)
    embed_step(1)
    sum_step(2, 2)
    sum_step(3, 2)
    sum_step(0, 3)
    sum_step(1, 3)
    sum_step(4, 2)
    lay(2)
    lay(3)
    features_ref[...] = tall[...].astype(BF)
    sum_step(2, 3)
    sum_step(3, 3)
    sum_step(4, 3)
    embed_ref[...] = embed_step(2)
    for part in range(len(PARTS)):
        sum_step(part, 4)
    grads_ref[...] = whole[...]


WIDTHS = ((384, 1), (128, 1), (512, 1), (256, 1), (512, 1), (256, 2))


def run_net(counts, *args):
    syn, emb, k1, k2, *rest = args
    args = (syn, emb.T, k1, k2.transpose(0, 1, 3, 2), *rest)
    tables = [jnp.asarray(t, BF) for t in (np.eye(CELLS), PICK, PICK_FAR, SPREAD, SHIFT, SHIFT_FAR)]
    wide, own = (EXT,), (CELLS,)
    blocks = [(16 * 36,) + wide, (64 * 36,) + wide, (1024,) + own, (1024,) + wide, (1024,) + wide, (1024,) + wide]
    blocks += [(512,) + wide, (512,) + wide, (128 * 9,) + wide, (256,) + own, (256 * 9,) + wide, (512,) + wide, (128 * 16,) + wide]
    blocks += [(1024,) + wide, (1024,) + own, (64 * 36,) + wide, (128 * 16,) + wide, (256 * 9,) + wide, (128 * 16,) + wide]
    blocks += [(64 * 36,) + wide, (1024,) + own, (64,) + wide]
    weights = [(384, 96), (128, 768), (128, 768), (256, 768), (128, 1536), (256, 1152), (128, 2304), (512, 1024), (256, 2048), (256, 512), (128, 1024), (16, 256), (256, 16)]
    scratch = [pltpu.VMEM(s, BF) for s in blocks + weights]
    for width, depth in WIDTHS:
        scratch += [pltpu.VMEM((bounds(depth)[3] + 16, width), BF), pltpu.VMEM((128 * depth + 64, width), BF)]
    scratch += [pltpu.VMEM(SHIFT.shape, BF), pltpu.VMEM(SHIFT_FAR.shape, BF), pltpu.VMEM((256, 512), BF), pltpu.SemaphoreType.DMA((2,))]
    scratch += [pltpu.SemaphoreType.DMA((len(WIDTHS), 8)), pltpu.SemaphoreType.DMA((len(WIDTHS), 8))]
    scratch += [pltpu.VMEM((ROWS, 128), F32), pltpu.VMEM((ROWS, 128), BF), pltpu.VMEM((64, 32, 128), F32)]
    n_row, n_col = counts
    most = max(n_row, n_col)
    for _, size, first in PARTS:
        n1, n2 = (n_row, n_col) if first == "row" else (n_col, n_row)
        c1, c2 = size // n1, size // n1 // n2
        scratch += [
            pltpu.VMEM((size, 128), BF),
            pltpu.VMEM((n1 - 1, c1, 128), BF),
            pltpu.VMEM((c1, 128), F32),
            pltpu.VMEM((c1, 128), BF),
            pltpu.VMEM((n2 - 1, c2, 128), BF),
        ]
    scratch += [pltpu.SemaphoreType.DMA((len(PARTS), 4, most)), pltpu.SemaphoreType.DMA((len(PARTS), 4, most))]
    scratch += [pltpu.VMEM((n_row, 16, 64), F32), pltpu.VMEM((n_col, 16, 64), F32)]
    scratch += [pltpu.SemaphoreType.DMA((2, most)), pltpu.SemaphoreType.DMA((2, most))]
    vmem = pl.BlockSpec(memory_space=pltpu.VMEM)
    return pl.pallas_call(
        functools.partial(net_kernel, counts),
        out_shape=(
            jax.ShapeDtypeStruct((2, 32, 128), F32),
            jax.ShapeDtypeStruct((64, 32, 128), BF),
            jax.ShapeDtypeStruct((16, 64), F32),
            jax.ShapeDtypeStruct((ROWS, 128), BF),
        ),
        in_specs=[vmem] * 13 + [pl.BlockSpec(memory_space=pl.ANY)] * 2,
        out_specs=(vmem,) * 4,
        scratch_shapes=scratch,
        compiler_params=pltpu.CompilerParams(collective_id=1, has_side_effects=True, vmem_limit_bytes=56 * 2**20),
    )(*args, *tables)


def out_kernel(logits, features, embed, g, o_logits, o_features, o_embed, o_first, o_second, o_bottom, o_return, o_final, o_read):
    o_logits[...] = logits[...]
    o_features[...] = features[...]
    for t in range(9):
        ta, tb = t // 3, t % 3
        for half in range(2):
            start = AT_RETURN + (t * 2 + half) * 128
            o_return[ta, tb, :, half * 128 : (half + 1) * 128] = g[start : start + 128, :].astype(F32)
        o_final[ta, tb] = g[AT_FINAL + t * 64 : AT_FINAL + (t + 1) * 64, :].astype(F32)
        o_bottom[ta, tb] = g[AT_BOTTOM + t * 256 : AT_BOTTOM + (t + 1) * 256, :].astype(F32)
        o_second[ta, tb] = g[AT_SECOND + t * 64 : AT_SECOND + (t + 1) * 64, :].astype(F32)
        start, low = (AT_FIRST + ta * 64, tb * 64) if tb < 2 else (AT_FIRST + (192 if ta < 2 else 256), ta % 2 * 64)
        o_first[ta, tb] = g[start : start + 64, low : low + 64].astype(F32)
    o_embed[...] = embed[...]
    o_read[...] = g[AT_READ : AT_READ + 16, 0:64].astype(F32)[0:2]


def write_out(logits, features, embed, g):
    shapes = [(2, 32, 128), (64, 32, 128), (16, 64), (3, 3, 64, 64), (3, 3, 64, 128), (3, 3, 256, 128), (3, 3, 128, 256), (3, 3, 64, 128), (2, 64)]
    vmem = pl.BlockSpec(memory_space=pltpu.VMEM)
    outs = pl.pallas_call(
        out_kernel,
        out_shape=tuple(jax.ShapeDtypeStruct(s, BF if n == 1 else F32) for n, s in enumerate(shapes)),
        in_specs=[vmem] * 4,
        out_specs=(vmem,) * 9,
        compiler_params=pltpu.CompilerParams(vmem_limit_bytes=32 * 2**20),
    )(logits, features, embed, g)
    outs = list(outs)
    outs[2] = outs[2].T
    outs[4] = outs[4].transpose(0, 1, 3, 2)
    return tuple(outs)


def on_device(counts, *args):
    return write_out(*run_net(counts, *args))


def solution(mesh):
    counts = (mesh.shape["row"], mesh.shape["col"])
    cells = P(None, ("batch", "row"), "col")
    in_specs = (P(("batch", "row"), "col"),) + (P(),) * 7 + (cells,)
    out_specs = (cells, cells, P("batch", None)) + (P("batch", None, None, None),) * 5 + (P("batch", None),)
    return jax.shard_map(
        functools.partial(on_device, counts), mesh=mesh, in_specs=in_specs, out_specs=out_specs, check_vma=False
    )
```

time: 102 us -> 80.9 us (0.79)
  the two profiles are of different devices: /device:TPU:65 before, /device:TPU:1 now
where the time goes in v3:
time: 80.9 us; the launch traced here: 80.5 us
  Pallas kernels  76 us (94%)
  local copies, waits for them, and re-layouts  3.9 us (5%)
    pallas_call x1, Pallas kernels, run_net(): pl.pallas_call(functools.partial(net_kernel, counts), out_shape=(jax.Shap...  74.1 us
    unnamed x8, local copies, waits for them, and re-layouts  3.9 us
    pallas_call x1, Pallas kernels, write_out(): pl.pallas_call(out_kernel, out_shape=tuple((jax.ShapeDtypeStruct(s, BF if...  1.91 us

profile of v3, /device:TPU:1, one launch (start us, length us, event | category | flops | bytes accessed | tf_op | source)
XLA Modules:
  0.0 80.5 jit_solution(16097158083356978101)
XLA Ops:
  0.6 74.1 %shard_map.214 = (f32[2,32,128]{2,1,0:T(8,128)}, bf16[64,32,128]{2,1,0:T(8,128)(2,1)}, f32[16,64]{1,0:T(8,128)}, bf16[6144,128]{1,0:T(8,128)(2,1)}) custom-call(s32[32,128]{1,0:T(8,128)} %refs_0_.1, bf16[16,64]{1,0:T(8,128)(2,1)} %bitcast.5, bf16[3,3,64,64]{3,2,1,0:T(8,128)(2,1)} %refs_2_.1, bf16[3,3,64,128]{3,2,1,0:T(8,128)(2,1)} %bitcast.4, ...), custom_call_target="tpu_custom_call" | custom-call | tf_op jit(solution)/shard_map/pallas_call | solution.py:712
  74.7 0.0 copy-start
  74.7 1.4 %copy-done = bf16[6144,128]{1,0:T(8,128)(2,1)S(1)} copy-done((bf16[6144,128]{1,0:T(8,128)(2,1)S(1)}, bf16[6144,128]{1,0:T(8,128)(2,1)}, u32[]{:S(2)}) %copy-start) | copy-done | bytes 1572888
  76.1 0.0 copy-start.1
  76.1 1.0 %copy-done.1 = bf16[64,32,128]{2,1,0:T(8,128)(2,1)S(1)} copy-done((bf16[64,32,128]{2,1,0:T(8,128)(2,1)S(1)}, bf16[64,32,128]{2,1,0:T(8,128)(2,1)}, u32[]{:S(2)}) %copy-start.1) | copy-done | bytes 524312
  77.2 0.0 copy-start.2
  77.2 0.8 copy-done.2
  77.9 0.0 copy-start.3
  77.9 0.7 copy-done.3
  78.6 1.9 %shard_map.215 = (f32[2,32,128]{2,1,0:T(8,128)}, bf16[64,32,128]{2,1,0:T(8,128)(2,1)}, f32[16,64]{1,0:T(8,128)}, f32[3,3,64,64]{3,2,1,0:T(8,128)}, f32[3,3,64,12...) custom-call(f32[2,32,128]{2,1,0:T(8,128)S(1)} %copy-done.2, ...), custom_call_target="tpu_custom_call" | custom-call | tf_op jit(solution)/shard_map/pallas_call | solution.py:747
Async XLA Ops:
  74.7 1.4 %copy-start = (bf16[6144,128]{1,0:T(8,128)(2,1)S(1)}, bf16[6144,128]{1,0:T(8,128)(2,1)}, u32[]{:S(2)}) copy-start(bf16[6144,128]{1,0:T(8,128)(2,1)} %get-tuple-element.25.g) | copy-start | bytes 4718596
  76.1 1.0 %copy-start.1 = (bf16[64,32,128]{2,1,0:T(8,128)(2,1)S(1)}, bf16[64,32,128]{2,1,0:T(8,128)(2,1)}, u32[]{:S(2)}) copy-start(bf16[64,32,128]{2,1,0:T(8,128)(2,1)} %get-tuple-element.23.features) | copy-start | bytes 1572868
  77.2 0.8 copy-start.2
  77.9 0.7 copy-start.3

commit v4 on v3

--- a/solution.py
+++ b/solution.py
@@ -15,9 +15,9 @@
 CELLS = DEEP * WIDE
 EXT = CELLS + 128
 
-ROWS = 6144
-PARTS = ((0, 1024, "row"), (1024, 1024, "col"), (2048, 1024, "row"), (3072, 2048, "col"), (5120, 1024, "row"))
-AT_RETURN, AT_FINAL, AT_BOTTOM, AT_SECOND, AT_FIRST, AT_READ = 0, 2304, 2880, 5184, 5760, 6080
+ROWS = 6272
+PARTS = ((0, 1536, "row"), (1536, 1408, "col"), (2944, 1152, "row"), (4096, 1152, "col"), (5248, 640, "row"), (5888, 384, "col"))
+AT_RETURN, AT_FINAL, AT_BOTTOM, AT_SECOND, AT_FIRST, AT_READ = 0, 2304, 2944, 5248, 5888, 6208
 
 
 def ranged(values, start, size):
@@ -126,7 +126,7 @@
     )
 
 
-SIDES = ((-1, 0), (1, 0), (0, -1), (0, 1), (-1, -1), (-1, 1), (1, -1), (1, 1))
+SIDES = ((-1, -1), (-1, 1), (1, -1), (1, 1), (0, -1), (0, 1), (-1, 0), (1, 0))
 
 
 def net_kernel(counts, *refs):
@@ -135,15 +135,18 @@
     def take(n):
         return [next(it) for _ in range(n)]
 
-    syn, embt, k1, k2t, k3, k4, k5, rdo, cot, eye, cQ, cQ2, cU, cS_hbm, cF_hbm = take(15)
-    logits_ref, features_ref, embed_ref, grads_ref = take(4)
+    syn, embt, rdo, cot, eye, cQ, cU = take(7)
+    afar = take(8)
+    logits_out, features_out, embed_ref, grads_out = take(4)
     xb, e0, z0, z1, f1, e1, z2, f2, e2, z3, e3, z4, e4, z5, f5, t5, t4, t3, t2, t1, fg, cp = take(22)
     w0, w1, w1b, w2, w2b, w3, w3b, w4, w4b, w5, w5b, r4, r4t = take(13)
     halos = [take(2) for _ in WIDTHS]
-    cS, cF, far, loads = take(4)
+    near = take(8)
+    k1, cS, k2t, k3, k5, k4, cQ2, cF = near
+    far, loads, logits_ref, features_ref, stores = take(5)
     sends, recvs = take(2)
     g_ref, whole, tall = take(3)
-    stages = [take(5) for _ in PARTS]
+    stages = [take(3) for _ in PARTS]
     sum_sends, sum_recvs, embed_row, embed_col, embed_sends, embed_recvs = take(6)
 
     n_row, n_col = counts
@@ -161,12 +164,22 @@
     def place(dr, dc):
         return {"row": (row + dr + n_row) % n_row, "col": (col + dc + n_col) % n_col}
 
-    load_near = pltpu.make_async_copy(cS_hbm, cS, loads.at[0])
-    load_far = pltpu.make_async_copy(cF_hbm, cF, loads.at[1])
-    load_near.start()
-    load_far.start()
-
-    partners = [(d, 0) for d in range(1, n_row)] + [(0, d) for d in range(1, n_col)] + list(SIDES[4:])
+    loading = {}
+    for n, (source, target) in enumerate(zip(afar, near)):
+        loading[id(target)] = pltpu.make_async_copy(source, target, loads.at[n])
+        loading[id(target)].start()
+
+    def loaded(*targets):
+        for target in targets:
+            loading[id(target)].wait()
+
+    storing = []
+
+    def store(source, target):
+        storing.append(pltpu.make_async_copy(source, target, stores.at[len(storing)]))
+        storing[-1].start()
+
+    partners = [(d, 0) for d in range(1, n_row)] + [(0, d) for d in range(1, n_col)] + list(SIDES[:4])
     barrier = pltpu.get_barrier_semaphore()
     for partner in partners:
         pl.semaphore_signal(barrier, inc=1, device_id=place(*partner), device_id_type=MESH)
@@ -253,35 +266,31 @@
 
     def sum_step(part, step):
         start, size, first = PARTS[part]
-        s1, r1, h1, s2, r2 = stages[part]
+        s1, r1, r2 = stages[part]
         me1, n1, to1 = ways[first]
         me2, n2, to2 = ways["col" if first == "row" else "row"]
-        c1, c2 = size // n1, size // n1 // n2
+        c1 = size // n1
         for copy in flying.pop(part, ()):
             copy.wait()
-        if step == 4:
+        if step == 3:
+            store(whole.at[start : start + size], grads_out.at[start : start + size])
             return
+        own = pl.ds(pl.multiple_of(start + me1 * c1, 16), c1)
         if step == 0:
             s1[...] = g_ref[start : start + size, :].astype(BF)
         elif step == 1:
-            total = g_ref[pl.ds(pl.multiple_of(start + me1 * c1, 16), c1), :]
+            total = g_ref[own, :]
             for d in range(n1 - 1):
                 total = total + r1[d].astype(F32)
-            h1[...] = total
-            s2[...] = total.astype(BF)
-        elif step == 2:
-            total = h1[pl.ds(pl.multiple_of(me2 * c2, 16), c2), :]
-            for d in range(n2 - 1):
-                total = total + r2[d].astype(F32)
-            whole[pl.ds(pl.multiple_of(start + me1 * c1 + me2 * c2, 16), c2), :] = total.astype(BF)
+            r2[me2] = total.astype(BF)
+        else:
+            whole[own, :] = sum(r2[d].astype(F32) for d in range(n2)).astype(BF)
         copies = []
-        for d in range(1, n1 if step in (0, 3) else n2):
+        for d in range(1, n2 if step == 1 else n1):
             if step == 0:
                 src, dst, to = ranged(s1, (me1 + d) % n1 * c1, c1), r1.at[d - 1], to1
             elif step == 1:
-                src, dst, to = ranged(s2, (me2 + d) % n2 * c2, c2), r2.at[d - 1], to2
-            elif step == 2:
-                src = dst = ranged(whole, start + me1 * c1 + me2 * c2, c2)
+                src = dst = r2.at[me2]
                 to = to2
             else:
                 src = dst = ranged(whole, start + me1 * c1, c1)
@@ -405,9 +414,10 @@
         r4[...] = jnp.where(own, tiled, 0.0).astype(BF)
         r4t[...] = nt(eye[...], r4[...]).astype(BF)
 
+    loaded(k1)
     arrange_first()
     arrange_readout()
-    load_near.wait()
+    loaded(cS)
     end(0, 1, copies)
     (tile,) = ring(0, 1, 0, 256)
     for a in range(4):
@@ -439,6 +449,7 @@
             start = ((a + 1) * 4 + b + 1) * 64
             e1[start : start + 64, :] = pooled(f1, 4, 64, a, b, EXT)
     extend(2, 64, e1, CELLS)
+    loaded(k2t)
     arrange_second()
 
     for a in range(2):
@@ -447,6 +458,7 @@
     e2[4 * 128 : 5 * 128, 0:CELLS] = pooled(f2, 2, 128, 0, 0, CELLS)
     copies = begin(1, 1, [e2[4 * 128 : 5 * 128, 0:CELLS]])
     later = begin(2, 1, [z2[0:256, 0:CELLS], z2[256:512, 0:CELLS]])
+    loaded(k3, k5)
     arrange_bottom()
     arrange_final()
     end(1, 1, copies)
@@ -455,6 +467,7 @@
 
     z3[...], e3[4 * 256 : 5 * 256, 0:CELLS] = activated(mm(w3[...], e2[:, 0:CELLS]))
     copies = begin(3, 1, [e3[4 * 256 : 5 * 256, 0:CELLS]])
+    loaded(k4)
     arrange_return()
     end(2, 1, later)
     for a in range(2):
@@ -542,6 +555,7 @@
                         piece = value[:, half * 128 : (half + 1) * 128]
                         g_ref[start : start + 128, :] = piece if b == 0 else g_ref[start : start + 128, :] + piece
 
+    g_ref[AT_FINAL + 576 : AT_BOTTOM, :] = jnp.zeros((AT_BOTTOM - AT_FINAL - 576, 128), F32)
     sum_step(0, 0)
     sum_step(1, 0)
     total = jnp.zeros((16, 256), F32)
@@ -559,6 +573,7 @@
     extend(2, 128, t4, CELLS)
     v = sum(mm(w4b[:, m * 512 : (m + 1) * 512], t4[m * 512 : (m + 1) * 512, 0:CELLS]) for m in range(4))
     far[:, 0:CELLS] = sloped(v, z3[...])
+    loaded(cQ2)
     copies = begin(5, 2, [far[:, 0:CELLS]])
     for t in range(9):
         g_ref[AT_BOTTOM + t * 256 : AT_BOTTOM + (t + 1) * 256, :] = nt(far[:, 0:CELLS], e2[t * 128 : (t + 1) * 128, 0:CELLS])
@@ -581,7 +596,8 @@
             for r in range(4):
                 h = 16 * t + 4 * r + a
                 logits_ref[:, h : h + 1, :] = laid[(a * 2 + t) * 4 : (a * 2 + t) * 4 + 2, r * 128 : (r + 1) * 128].reshape(2, 1, 128)
-    load_far.wait()
+    store(logits_ref, logits_out)
+    loaded(cF)
     end(5, 2, copies)
     far[:, 256:384], far[:, 384:512] = ring(5, 2, 0, 256)
     for n in range(9):
@@ -594,14 +610,16 @@
             start = ((a + 1) * 4 + b + 1) * 128
             v = fenced(t4[start : start + 128, :].astype(F32) + through)
             t2[start : start + 128, :] = sloped(v, z2[n * 128 : (n + 1) * 128, :])
+    sum_step(0, 1)
+    sum_step(1, 1)
     for ta in range(3):
         product = 0.0
         for a in range(2):
             start = ((a + 1) * 4 + 1) * 128
             product = product + nt(e1[(a + ta) * 256 : (a + ta + 1) * 256, 0:CELLS], t2[start : start + 256, 0:CELLS])
         g_ref[AT_SECOND + ta * 192 : AT_SECOND + (ta + 1) * 192, :] = product[0:192, 0:128] + product[64:256, 128:256]
-    sum_step(0, 1)
-    sum_step(1, 1)
+    g_ref[AT_SECOND + 576 : AT_FIRST, :] = jnp.zeros((AT_FIRST - AT_SECOND - 576, 128), F32)
+    sum_step(4, 0)
     extend(2, 128, t2, EXT)
 
     for a in range(2):
@@ -613,6 +631,8 @@
                     start = ((fa + 1) * 6 + fb + 1) * 64
                     n = (fa * 4 + fb) * 64
                     t1[start : start + 64, :] = sloped(fenced(t5[start : start + 64, :].astype(F32) + v[b * 64 : (b + 1) * 64, :]), z1[n : n + 64, :])
+    sum_step(2, 1)
+    sum_step(3, 1)
     for ta in range(3):
         product = 0.0
         for a in range(4):
@@ -625,7 +645,7 @@
         start = AT_FIRST + (192 if ta < 2 else 256)
         g_ref[start : start + 64, ta % 2 * 64 : ta % 2 * 64 + 64] = value[:, 128:192]
     g_ref[AT_FIRST + 256 : AT_FIRST + 320, 64:128] = jnp.zeros((64, 64), F32)
-    sum_step(4, 0)
+    sum_step(5, 0)
     extend(4, 64, t1, CELLS)
 
     total = jnp.zeros((64, 256), F32)
@@ -649,29 +669,28 @@
             for r in range(4):
                 tall[:, 16 * t + 4 * r + a, :] = laid[:, r * 128 : (r + 1) * 128]
 
-    sum_step(2, 1)
-    sum_step(3, 1)
     sum_step(0, 2)
     sum_step(1, 2)
     sum_step(4, 1)
     lay(0)
     lay(1)
-    embed_step(1)
     sum_step(2, 2)
     sum_step(3, 2)
-    sum_step(0, 3)
-    sum_step(1, 3)
-    sum_step(4, 2)
+    embed_step(1)
+    sum_step(5, 1)
     lay(2)
     lay(3)
     features_ref[...] = tall[...].astype(BF)
-    sum_step(2, 3)
-    sum_step(3, 3)
-    sum_step(4, 3)
+    store(features_ref, features_out)
+    sum_step(4, 2)
+    sum_step(0, 3)
+    sum_step(1, 3)
+    sum_step(5, 2)
     embed_ref[...] = embed_step(2)
-    for part in range(len(PARTS)):
-        sum_step(part, 4)
-    grads_ref[...] = whole[...]
+    for part in (2, 3, 4, 5):
+        sum_step(part, 3)
+    for copy in storing:
+        copy.wait()
 
 
 WIDTHS = ((384, 1), (128, 1), (512, 1), (256, 1), (512, 1), (256, 2))
@@ -679,8 +698,9 @@
 
 def run_net(counts, *args):
     syn, emb, k1, k2, *rest = args
-    args = (syn, emb.T, k1, k2.transpose(0, 1, 3, 2), *rest)
-    tables = [jnp.asarray(t, BF) for t in (np.eye(CELLS), PICK, PICK_FAR, SPREAD, SHIFT, SHIFT_FAR)]
+    k3, k4, k5, rdo, cot = rest
+    eye, pick, pick_far, spread, near, far = [jnp.asarray(t, BF) for t in (np.eye(CELLS), PICK, PICK_FAR, SPREAD, SHIFT, SHIFT_FAR)]
+    afar = (k1, near, k2.transpose(0, 1, 3, 2), k3, k5, k4, pick_far, far)
     wide, own = (EXT,), (CELLS,)
     blocks = [(16 * 36,) + wide, (64 * 36,) + wide, (1024,) + own, (1024,) + wide, (1024,) + wide, (1024,) + wide]
     blocks += [(512,) + wide, (512,) + wide, (128 * 9,) + wide, (256,) + own, (256 * 9,) + wide, (512,) + wide, (128 * 16,) + wide]
@@ -690,25 +710,21 @@
     scratch = [pltpu.VMEM(s, BF) for s in blocks + weights]
     for width, depth in WIDTHS:
         scratch += [pltpu.VMEM((bounds(depth)[3] + 16, width), BF), pltpu.VMEM((128 * depth + 64, width), BF)]
-    scratch += [pltpu.VMEM(SHIFT.shape, BF), pltpu.VMEM(SHIFT_FAR.shape, BF), pltpu.VMEM((256, 512), BF), pltpu.SemaphoreType.DMA((2,))]
+    scratch += [pltpu.VMEM(x.shape, BF) for x in afar]
+    scratch += [pltpu.VMEM((256, 512), BF), pltpu.SemaphoreType.DMA((8,)), pltpu.VMEM((2, 32, 128), F32), pltpu.VMEM((64, 32, 128), BF)]
+    scratch += [pltpu.SemaphoreType.DMA((2 + len(PARTS),))]
     scratch += [pltpu.SemaphoreType.DMA((len(WIDTHS), 8)), pltpu.SemaphoreType.DMA((len(WIDTHS), 8))]
     scratch += [pltpu.VMEM((ROWS, 128), F32), pltpu.VMEM((ROWS, 128), BF), pltpu.VMEM((64, 32, 128), F32)]
     n_row, n_col = counts
     most = max(n_row, n_col)
     for _, size, first in PARTS:
         n1, n2 = (n_row, n_col) if first == "row" else (n_col, n_row)
-        c1, c2 = size // n1, size // n1 // n2
-        scratch += [
-            pltpu.VMEM((size, 128), BF),
-            pltpu.VMEM((n1 - 1, c1, 128), BF),
-            pltpu.VMEM((c1, 128), F32),
-            pltpu.VMEM((c1, 128), BF),
-            pltpu.VMEM((n2 - 1, c2, 128), BF),
-        ]
-    scratch += [pltpu.SemaphoreType.DMA((len(PARTS), 4, most)), pltpu.SemaphoreType.DMA((len(PARTS), 4, most))]
+        c1 = size // n1
+        scratch += [pltpu.VMEM((size, 128), BF), pltpu.VMEM((n1 - 1, c1, 128), BF), pltpu.VMEM((n2, c1, 128), BF)]
+    scratch += [pltpu.SemaphoreType.DMA((len(PARTS), 3, most)), pltpu.SemaphoreType.DMA((len(PARTS), 3, most))]
     scratch += [pltpu.VMEM((n_row, 16, 64), F32), pltpu.VMEM((n_col, 16, 64), F32)]
     scratch += [pltpu.SemaphoreType.DMA((2, most)), pltpu.SemaphoreType.DMA((2, most))]
-    vmem = pl.BlockSpec(memory_space=pltpu.VMEM)
+    vmem, hbm = pl.BlockSpec(memory_space=pltpu.VMEM), pl.BlockSpec(memory_space=pl.ANY)
     return pl.pallas_call(
         functools.partial(net_kernel, counts),
         out_shape=(
@@ -717,39 +733,67 @@
             jax.ShapeDtypeStruct((16, 64), F32),
             jax.ShapeDtypeStruct((ROWS, 128), BF),
         ),
-        in_specs=[vmem] * 13 + [pl.BlockSpec(memory_space=pl.ANY)] * 2,
-        out_specs=(vmem,) * 4,
+        in_specs=[vmem] * 7 + [hbm] * 8,
+        out_specs=(hbm, hbm, vmem, hbm),
         scratch_shapes=scratch,
         compiler_params=pltpu.CompilerParams(collective_id=1, has_side_effects=True, vmem_limit_bytes=56 * 2**20),
-    )(*args, *tables)
-
-
-def out_kernel(logits, features, embed, g, o_logits, o_features, o_embed, o_first, o_second, o_bottom, o_return, o_final, o_read):
-    o_logits[...] = logits[...]
-    o_features[...] = features[...]
+    )(syn, emb.T, rdo, cot, eye, pick, spread, *afar)
+
+
+def out_kernel(logits, features, embed, grads, *refs):
+    outs, (g, mids, loads, stores) = refs[:9], (refs[9], refs[10:16], refs[16], refs[17])
+    spans = ((0, AT_BOTTOM), (AT_BOTTOM, AT_SECOND), (AT_SECOND, ROWS))
+    pulls = [pltpu.make_async_copy(grads.at[a:b], g.at[a:b], loads.at[n]) for n, (a, b) in enumerate(spans)]
+    for copy in pulls:
+        copy.start()
+    pushes = [pltpu.make_async_copy(x, outs[n], stores.at[n]) for n, x in enumerate((logits, features, embed))]
+    for copy in pushes:
+        copy.start()
+
+    def push(n):
+        pushes.append(pltpu.make_async_copy(mids[n - 3], outs[n], stores.at[n]))
+        pushes[-1].start()
+
+    m_first, m_second, m_bottom, m_return, m_final, m_read = mids
+    pulls[0].wait()
     for t in range(9):
         ta, tb = t // 3, t % 3
         for half in range(2):
             start = AT_RETURN + (t * 2 + half) * 128
-            o_return[ta, tb, :, half * 128 : (half + 1) * 128] = g[start : start + 128, :].astype(F32)
-        o_final[ta, tb] = g[AT_FINAL + t * 64 : AT_FINAL + (t + 1) * 64, :].astype(F32)
-        o_bottom[ta, tb] = g[AT_BOTTOM + t * 256 : AT_BOTTOM + (t + 1) * 256, :].astype(F32)
-        o_second[ta, tb] = g[AT_SECOND + t * 64 : AT_SECOND + (t + 1) * 64, :].astype(F32)
+            m_return[ta, tb, :, half * 128 : (half + 1) * 128] = g[start : start + 128, :].astype(F32)
+        m_final[ta, tb] = g[AT_FINAL + t * 64 : AT_FINAL + (t + 1) * 64, :].astype(F32)
+    push(6)
+    push(7)
+    pulls[1].wait()
+    for t in range(9):
+        m_bottom[t // 3, t % 3] = g[AT_BOTTOM + t * 256 : AT_BOTTOM + (t + 1) * 256, :].astype(F32)
+    push(5)
+    pulls[2].wait()
+    for t in range(9):
+        ta, tb = t // 3, t % 3
+        m_second[ta, tb] = g[AT_SECOND + t * 64 : AT_SECOND + (t + 1) * 64, :].astype(F32)
         start, low = (AT_FIRST + ta * 64, tb * 64) if tb < 2 else (AT_FIRST + (192 if ta < 2 else 256), ta % 2 * 64)
-        o_first[ta, tb] = g[start : start + 64, low : low + 64].astype(F32)
-    o_embed[...] = embed[...]
-    o_read[...] = g[AT_READ : AT_READ + 16, 0:64].astype(F32)[0:2]
+        m_first[ta, tb] = g[start : start + 64, low : low + 64].astype(F32)
+    m_read[...] = g[AT_READ : AT_READ + 16, 0:64].astype(F32)[0:2]
+    push(3)
+    push(4)
+    push(8)
+    for copy in pushes:
+        copy.wait()
 
 
 def write_out(logits, features, embed, g):
     shapes = [(2, 32, 128), (64, 32, 128), (16, 64), (3, 3, 64, 64), (3, 3, 64, 128), (3, 3, 256, 128), (3, 3, 128, 256), (3, 3, 64, 128), (2, 64)]
-    vmem = pl.BlockSpec(memory_space=pltpu.VMEM)
+    hbm = pl.BlockSpec(memory_space=pl.ANY)
     outs = pl.pallas_call(
         out_kernel,
         out_shape=tuple(jax.ShapeDtypeStruct(s, BF if n == 1 else F32) for n, s in enumerate(shapes)),
-        in_specs=[vmem] * 4,
-        out_specs=(vmem,) * 9,
-        compiler_params=pltpu.CompilerParams(vmem_limit_bytes=32 * 2**20),
+        in_specs=[hbm] * 4,
+        out_specs=(hbm,) * 9,
+        scratch_shapes=[pltpu.VMEM((ROWS, 128), BF)]
+        + [pltpu.VMEM(s, F32) for s in shapes[3:]]
+        + [pltpu.SemaphoreType.DMA((3,)), pltpu.SemaphoreType.DMA((9,))],
+        compiler_params=pltpu.CompilerParams(vmem_limit_bytes=60 * 2**20),
     )(logits, features, embed, g)
     outs = list(outs)
     outs[2] = outs[2].T

time: 80.9 us -> 93.6 us (1.16)
  Pallas kernels: 76 us -> 92.6 us
  local copies, waits for them, and re-layouts: 3.9 us -> 0 us
    pallas_call x1, Pallas kernels: 1.91 us -> 18.3 us  [write_out(): pl.pallas_call(out_kernel, out_shape=tuple((jax.ShapeDtypeStruct(s, BF if...]
    unnamed x8 -> x0, local copies, waits for them, and re-layouts: 3.9 us -> none
where the time goes in v4:
time: 93.6 us; the launch traced here: 93.4 us
  Pallas kernels  92.6 us (99%)
    pallas_call x1, Pallas kernels, run_net(): pl.pallas_call(functools.partial(net_kernel, counts), out_shape=(jax.Shap...  74.3 us
    pallas_call x1, Pallas kernels, write_out(): pl.pallas_call(out_kernel, out_shape=tuple((jax.ShapeDtypeStruct(s, BF if...  18.3 us

profile of v4, /device:TPU:1, one launch (start us, length us, event | category | flops | bytes accessed | tf_op | source)
XLA Modules:
  0.0 93.4 jit_solution(6561340931397315753)
XLA Ops:
  0.6 74.3 %shard_map.214 = (f32[2,32,128]{2,1,0:T(8,128)}, bf16[64,32,128]{2,1,0:T(8,128)(2,1)}, f32[16,64]{1,0:T(8,128)}, bf16[6272,128]{1,0:T(8,128)(2,1)}) custom-call(s32[32,128]{1,0:T(8,128)} %refs_0_.1, bf16[16,64]{1,0:T(8,128)(2,1)} %bitcast.5, bf16[2,64]{1,0:T(2,128)(2,1)} %refs_2_.1, bf16[2,32,128]{2,1,0:T(8,128)(2,1)} %refs_3_.1, ...), custom_call_target="tpu_custom_call" | custom-call | tf_op jit(solution)/shard_map/pallas_call | solution.py:728
  74.9 18.3 %shard_map.215 = (f32[2,32,128]{2,1,0:T(8,128)}, bf16[64,32,128]{2,1,0:T(8,128)(2,1)}, f32[16,64]{1,0:T(8,128)}, f32[3,3,64,64]{3,2,1,0:T(8,128)}, f32[3,3,64,12...) custom-call(f32[2,32,128]{2,1,0:T(8,128)} %get-tuple-element.22.logi, ...), custom_call_target="tpu_custom_call" | custom-call | tf_op jit(solution)/shard_map/pallas_call | solution.py:788

commit v5 on v4

--- a/solution.py
+++ b/solution.py
@@ -16,7 +16,14 @@
 EXT = CELLS + 128
 
 ROWS = 6272
-PARTS = ((0, 1536, "row"), (1536, 1408, "col"), (2944, 1152, "row"), (4096, 1152, "col"), (5248, 640, "row"), (5888, 384, "col"))
+PARTS = (
+    (0, 1408, True, "x", "col"),
+    (1408, 1536, True, "col", "x"),
+    (2944, 1024, True, "x", "col"),
+    (3968, 1280, True, "col", "x"),
+    (5248, 640, False, "row", "col"),
+    (5888, 384, False, "col", "row"),
+)
 AT_RETURN, AT_FINAL, AT_BOTTOM, AT_SECOND, AT_FIRST, AT_READ = 0, 2304, 2944, 5248, 5888, 6208
 
 
@@ -143,10 +150,10 @@
     halos = [take(2) for _ in WIDTHS]
     near = take(8)
     k1, cS, k2t, k3, k5, k4, cQ2, cF = near
-    far, loads, logits_ref, features_ref, stores = take(5)
+    far, wide2, loads, logits_ref, features_ref, stores = take(6)
     sends, recvs = take(2)
     g_ref, whole, tall = take(3)
-    stages = [take(3) for _ in PARTS]
+    stages = [take(6) for _ in PARTS]
     sum_sends, sum_recvs, embed_row, embed_col, embed_sends, embed_recvs = take(6)
 
     n_row, n_col = counts
@@ -261,41 +268,55 @@
                 start = (ea * (p + 2) + eb) * width
                 ref[start : start + width, 0:size] = moved.astype(BF)
 
-    ways = {"row": (row, n_row, lambda d: place(d, 0)), "col": (col, n_col, lambda d: place(0, d))}
+    core, n_x = row % 2, n_row // 2
+    ways = {
+        "row": (row, n_row, lambda d: place(d, 0)),
+        "col": (col, n_col, lambda d: place(0, d)),
+        "x": (row // 2, n_x, lambda d: {"row": (row // 2 + d) % n_x * 2 + core}),
+    }
     flying = {}
 
     def sum_step(part, step):
-        start, size, first = PARTS[part]
-        s1, r1, r2 = stages[part]
+        start, size, paired, first, second = PARTS[part]
+        s0, r0, held, s1, r1, r2 = stages[part]
         me1, n1, to1 = ways[first]
-        me2, n2, to2 = ways["col" if first == "row" else "row"]
-        c1 = size // n1
+        me2, n2, to2 = ways[second]
         for copy in flying.pop(part, ()):
             copy.wait()
-        if step == 3:
+        if step == 5:
             store(whole.at[start : start + size], grads_out.at[start : start + size])
             return
-        own = pl.ds(pl.multiple_of(start + me1 * c1, 16), c1)
+        half = size // 2 if paired else size
+        base = start + core * half if paired else start
+        c1 = half // n1
+        own = pl.ds(pl.multiple_of(base + me1 * c1, 16), c1)
+        partner = {"row": row + 1 - 2 * core}
+        moves = []
         if step == 0:
-            s1[...] = g_ref[start : start + size, :].astype(BF)
+            s0[...] = g_ref[pl.ds(pl.multiple_of(start + (1 - core) * half, 16), half), :].astype(BF)
+            moves.append((s0, r0, partner))
         elif step == 1:
-            total = g_ref[own, :]
+            total = g_ref[pl.ds(pl.multiple_of(base, 16), half), :] if paired else g_ref[base : base + half, :]
+            if paired:
+                total = total + r0[...].astype(F32)
+            held[...] = total
+            s1[...] = total.astype(BF)
+            moves = [(ranged(s1, (me1 + d) % n1 * c1, c1), r1.at[d - 1], to1(d)) for d in range(1, n1)]
+        elif step == 2:
+            total = held[pl.ds(pl.multiple_of(me1 * c1, 16), c1), :]
             for d in range(n1 - 1):
                 total = total + r1[d].astype(F32)
             r2[me2] = total.astype(BF)
-        else:
+            moves = [(r2.at[me2], r2.at[me2], to2(d)) for d in range(1, n2)]
+        elif step == 3:
             whole[own, :] = sum(r2[d].astype(F32) for d in range(n2)).astype(BF)
-        copies = []
-        for d in range(1, n2 if step == 1 else n1):
-            if step == 0:
-                src, dst, to = ranged(s1, (me1 + d) % n1 * c1, c1), r1.at[d - 1], to1
-            elif step == 1:
-                src = dst = r2.at[me2]
-                to = to2
-            else:
-                src = dst = ranged(whole, start + me1 * c1, c1)
-                to = to1
-            copies.append(remote(src, dst, sum_sends.at[part, step, d], sum_recvs.at[part, step, d], to(d)))
+            moves = [(whole.at[own, :], whole.at[own, :], to1(d)) for d in range(1, n1)]
+        elif paired:
+            mine = ranged(whole, base, half)
+            moves.append((mine, mine, partner))
+        copies = [
+            remote(src, dst, sum_sends.at[part, step, k], sum_recvs.at[part, step, k], to) for k, (src, dst, to) in enumerate(moves)
+        ]
         for copy in copies:
             copy.start()
         flying[part] = copies
@@ -456,25 +477,27 @@
         v = sum(mm(w2[:, ta * 256 : (ta + 1) * 256], e1[(a + ta) * 256 : (a + ta + 1) * 256, 0:CELLS]) for ta in range(3))
         z2[a * 256 : (a + 1) * 256, 0:CELLS], f2[a * 256 : (a + 1) * 256, 0:CELLS] = activated(v)
     e2[4 * 128 : 5 * 128, 0:CELLS] = pooled(f2, 2, 128, 0, 0, CELLS)
-    copies = begin(1, 1, [e2[4 * 128 : 5 * 128, 0:CELLS]])
+    loaded(cQ2)
+    copies = begin(1, 2, [e2[4 * 128 : 5 * 128, 0:CELLS]])
     later = begin(2, 1, [z2[0:256, 0:CELLS], z2[256:512, 0:CELLS]])
     loaded(k3, k5)
     arrange_bottom()
     arrange_final()
-    end(1, 1, copies)
-    e2[4 * 128 : 5 * 128, CELLS:EXT] = ring(1, 1, 0, 128)[0]
-    extend(1, 128, e2, CELLS)
-
-    z3[...], e3[4 * 256 : 5 * 256, 0:CELLS] = activated(mm(w3[...], e2[:, 0:CELLS]))
-    copies = begin(3, 1, [e3[4 * 256 : 5 * 256, 0:CELLS]])
     loaded(k4)
     arrange_return()
+    loaded(cF)
+    end(1, 2, copies)
+    wide2[:, 0:CELLS] = e2[4 * 128 : 5 * 128, 0:CELLS]
+    wide2[:, 256:384], wide2[:, 384:512] = ring(1, 2, 0, 128)
+    for n in range(9):
+        e2[n * 128 : (n + 1) * 128, :] = mm(wide2[...], cF[n * 512 : (n + 1) * 512, :]).astype(BF)
+
+    stored, e3[4 * 256 : 5 * 256, :] = activated(fenced(mm(w3[...], e2[...])))
+    z3[...] = stored[:, 0:CELLS]
     end(2, 1, later)
     for a in range(2):
         z2[a * 256 : (a + 1) * 256, CELLS:EXT] = ring(2, 1, a * 256, 256)[0]
         f2[a * 256 : (a + 1) * 256, CELLS:EXT] = activated(z2[a * 256 : (a + 1) * 256, CELLS:EXT])[1]
-    end(3, 1, copies)
-    e3[4 * 256 : 5 * 256, CELLS:EXT] = ring(3, 1, 0, 256)[0]
     extend(1, 256, e3, EXT)
 
     for a in range(2):
@@ -515,7 +538,7 @@
             start = ((a + 1) * 4 + b + 1) * 128
             n = a * 2 + b
             t4[start : start + 128, 0:CELLS] = sloped(v, z4[n * 128 : (n + 1) * 128, 0:CELLS])
-    copies = begin(4, 1, [t4[((a + 1) * 4 + 1) * 128 : ((a + 1) * 4 + 3) * 128, 0:CELLS] for a in range(2)])
+    copies = begin(3, 1, [t4[((a + 1) * 4 + 1) * 128 : ((a + 1) * 4 + 3) * 128, 0:CELLS] for a in range(2)])
 
     sums = {}
     for a in range(4):
@@ -566,15 +589,16 @@
     g_ref[AT_READ:ROWS, :] = jnp.zeros((ROWS - AT_READ, 128), F32)
     g_ref[AT_READ : AT_READ + 4, 0:64] = total
 
-    end(4, 1, copies)
+    end(3, 1, copies)
+    sum_step(0, 1)
+    sum_step(1, 1)
     for a in range(2):
         start = ((a + 1) * 4 + 1) * 128
-        t4[start : start + 256, CELLS:EXT] = ring(4, 1, a * 256, 256)[0]
+        t4[start : start + 256, CELLS:EXT] = ring(3, 1, a * 256, 256)[0]
     extend(2, 128, t4, CELLS)
     v = sum(mm(w4b[:, m * 512 : (m + 1) * 512], t4[m * 512 : (m + 1) * 512, 0:CELLS]) for m in range(4))
     far[:, 0:CELLS] = sloped(v, z3[...])
-    loaded(cQ2)
-    copies = begin(5, 2, [far[:, 0:CELLS]])
+    copies = begin(4, 2, [far[:, 0:CELLS]])
     for t in range(9):
         g_ref[AT_BOTTOM + t * 256 : AT_BOTTOM + (t + 1) * 256, :] = nt(far[:, 0:CELLS], e2[t * 128 : (t + 1) * 128, 0:CELLS])
     sum_step(2, 0)
@@ -597,12 +621,15 @@
                 h = 16 * t + 4 * r + a
                 logits_ref[:, h : h + 1, :] = laid[(a * 2 + t) * 4 : (a * 2 + t) * 4 + 2, r * 128 : (r + 1) * 128].reshape(2, 1, 128)
     store(logits_ref, logits_out)
-    loaded(cF)
-    end(5, 2, copies)
-    far[:, 256:384], far[:, 384:512] = ring(5, 2, 0, 256)
+    sum_step(2, 1)
+    sum_step(3, 1)
+    end(4, 2, copies)
+    far[:, 256:384], far[:, 384:512] = ring(4, 2, 0, 256)
     for n in range(9):
         t3[n * 256 : (n + 1) * 256, :] = mm(far[...], cF[n * 512 : (n + 1) * 512, :]).astype(BF)
 
+    sum_step(0, 2)
+    sum_step(1, 2)
     through = mm(w3b[...], t3[...]) * 0.25
     for a in range(2):
         for b in range(2):
@@ -610,8 +637,6 @@
             start = ((a + 1) * 4 + b + 1) * 128
             v = fenced(t4[start : start + 128, :].astype(F32) + through)
             t2[start : start + 128, :] = sloped(v, z2[n * 128 : (n + 1) * 128, :])
-    sum_step(0, 1)
-    sum_step(1, 1)
     for ta in range(3):
         product = 0.0
         for a in range(2):
@@ -619,7 +644,7 @@
             product = product + nt(e1[(a + ta) * 256 : (a + ta + 1) * 256, 0:CELLS], t2[start : start + 256, 0:CELLS])
         g_ref[AT_SECOND + ta * 192 : AT_SECOND + (ta + 1) * 192, :] = product[0:192, 0:128] + product[64:256, 128:256]
     g_ref[AT_SECOND + 576 : AT_FIRST, :] = jnp.zeros((AT_FIRST - AT_SECOND - 576, 128), F32)
-    sum_step(4, 0)
+    sum_step(4, 1)
     extend(2, 128, t2, EXT)
 
     for a in range(2):
@@ -631,8 +656,8 @@
                     start = ((fa + 1) * 6 + fb + 1) * 64
                     n = (fa * 4 + fb) * 64
                     t1[start : start + 64, :] = sloped(fenced(t5[start : start + 64, :].astype(F32) + v[b * 64 : (b + 1) * 64, :]), z1[n : n + 64, :])
-    sum_step(2, 1)
-    sum_step(3, 1)
+    sum_step(2, 2)
+    sum_step(3, 2)
     for ta in range(3):
         product = 0.0
         for a in range(4):
@@ -645,7 +670,9 @@
         start = AT_FIRST + (192 if ta < 2 else 256)
         g_ref[start : start + 64, ta % 2 * 64 : ta % 2 * 64 + 64] = value[:, 128:192]
     g_ref[AT_FIRST + 256 : AT_FIRST + 320, 64:128] = jnp.zeros((64, 64), F32)
-    sum_step(5, 0)
+    sum_step(5, 1)
+    sum_step(0, 3)
+    sum_step(1, 3)
     extend(4, 64, t1, CELLS)
 
     total = jnp.zeros((64, 256), F32)
@@ -669,31 +696,31 @@
             for r in range(4):
                 tall[:, 16 * t + 4 * r + a, :] = laid[:, r * 128 : (r + 1) * 128]
 
-    sum_step(0, 2)
-    sum_step(1, 2)
-    sum_step(4, 1)
+    sum_step(4, 2)
     lay(0)
     lay(1)
-    sum_step(2, 2)
-    sum_step(3, 2)
-    embed_step(1)
-    sum_step(5, 1)
+    sum_step(5, 2)
+    sum_step(2, 3)
+    sum_step(3, 3)
+    sum_step(0, 4)
+    sum_step(1, 4)
     lay(2)
     lay(3)
+    embed_step(1)
     features_ref[...] = tall[...].astype(BF)
     store(features_ref, features_out)
-    sum_step(4, 2)
-    sum_step(0, 3)
-    sum_step(1, 3)
-    sum_step(5, 2)
+    sum_step(4, 3)
+    sum_step(5, 3)
+    sum_step(2, 4)
+    sum_step(3, 4)
     embed_ref[...] = embed_step(2)
-    for part in (2, 3, 4, 5):
-        sum_step(part, 3)
+    for part in (0, 1, 4, 2, 3, 5):
+        sum_step(part, 5)
     for copy in storing:
         copy.wait()
 
 
-WIDTHS = ((384, 1), (128, 1), (512, 1), (256, 1), (512, 1), (256, 2))
+WIDTHS = ((384, 1), (128, 2), (512, 1), (512, 1), (256, 2))
 
 
 def run_net(counts, *args):
@@ -711,17 +738,26 @@
     for width, depth in WIDTHS:
         scratch += [pltpu.VMEM((bounds(depth)[3] + 16, width), BF), pltpu.VMEM((128 * depth + 64, width), BF)]
     scratch += [pltpu.VMEM(x.shape, BF) for x in afar]
-    scratch += [pltpu.VMEM((256, 512), BF), pltpu.SemaphoreType.DMA((8,)), pltpu.VMEM((2, 32, 128), F32), pltpu.VMEM((64, 32, 128), BF)]
+    scratch += [pltpu.VMEM((256, 512), BF), pltpu.VMEM((128, 512), BF), pltpu.SemaphoreType.DMA((8,)), pltpu.VMEM((2, 32, 128), F32), pltpu.VMEM((64, 32, 128), BF)]
     scratch += [pltpu.SemaphoreType.DMA((2 + len(PARTS),))]
     scratch += [pltpu.SemaphoreType.DMA((len(WIDTHS), 8)), pltpu.SemaphoreType.DMA((len(WIDTHS), 8))]
     scratch += [pltpu.VMEM((ROWS, 128), F32), pltpu.VMEM((ROWS, 128), BF), pltpu.VMEM((64, 32, 128), F32)]
     n_row, n_col = counts
     most = max(n_row, n_col)
-    for _, size, first in PARTS:
-        n1, n2 = (n_row, n_col) if first == "row" else (n_col, n_row)
-        c1 = size // n1
-        scratch += [pltpu.VMEM((size, 128), BF), pltpu.VMEM((n1 - 1, c1, 128), BF), pltpu.VMEM((n2, c1, 128), BF)]
-    scratch += [pltpu.SemaphoreType.DMA((len(PARTS), 3, most)), pltpu.SemaphoreType.DMA((len(PARTS), 3, most))]
+    along = {"row": n_row, "col": n_col, "x": n_row // 2}
+    for _, size, paired, first, second in PARTS:
+        half = size // 2 if paired else size
+        n1, n2 = along[first], along[second]
+        c1, pair = half // n1, half if paired else 16
+        scratch += [
+            pltpu.VMEM((pair, 128), BF),
+            pltpu.VMEM((pair, 128), BF),
+            pltpu.VMEM((half, 128), F32),
+            pltpu.VMEM((half, 128), BF),
+            pltpu.VMEM((n1 - 1, c1, 128), BF),
+            pltpu.VMEM((n2, c1, 128), BF),
+        ]
+    scratch += [pltpu.SemaphoreType.DMA((len(PARTS), 5, most)), pltpu.SemaphoreType.DMA((len(PARTS), 5, most))]
     scratch += [pltpu.VMEM((n_row, 16, 64), F32), pltpu.VMEM((n_col, 16, 64), F32)]
     scratch += [pltpu.SemaphoreType.DMA((2, most)), pltpu.SemaphoreType.DMA((2, most))]
     vmem, hbm = pl.BlockSpec(memory_space=pltpu.VMEM), pl.BlockSpec(memory_space=pl.ANY)
@@ -741,14 +777,15 @@
 
 
 def out_kernel(logits, features, embed, grads, *refs):
-    outs, (g, mids, loads, stores) = refs[:9], (refs[9], refs[10:16], refs[16], refs[17])
+    outs, (g, passed, mids, loads, stores) = refs[:9], (refs[9], refs[10:13], refs[13:19], refs[19], refs[20])
     spans = ((0, AT_BOTTOM), (AT_BOTTOM, AT_SECOND), (AT_SECOND, ROWS))
     pulls = [pltpu.make_async_copy(grads.at[a:b], g.at[a:b], loads.at[n]) for n, (a, b) in enumerate(spans)]
     for copy in pulls:
         copy.start()
-    pushes = [pltpu.make_async_copy(x, outs[n], stores.at[n]) for n, x in enumerate((logits, features, embed))]
-    for copy in pushes:
+    through = [pltpu.make_async_copy(x, passed[n], loads.at[3 + n]) for n, x in enumerate((logits, features, embed))]
+    for copy in through:
         copy.start()
+    pushes = [pltpu.make_async_copy(passed[n], outs[n], stores.at[n]) for n in range(3)]
 
     def push(n):
         pushes.append(pltpu.make_async_copy(mids[n - 3], outs[n], stores.at[n]))
@@ -764,6 +801,9 @@
         m_final[ta, tb] = g[AT_FINAL + t * 64 : AT_FINAL + (t + 1) * 64, :].astype(F32)
     push(6)
     push(7)
+    for pull, copy in zip(through, pushes):
+        pull.wait()
+        copy.start()
     pulls[1].wait()
     for t in range(9):
         m_bottom[t // 3, t % 3] = g[AT_BOTTOM + t * 256 : AT_BOTTOM + (t + 1) * 256, :].astype(F32)
@@ -791,8 +831,8 @@
         in_specs=[hbm] * 4,
         out_specs=(hbm,) * 9,
         scratch_shapes=[pltpu.VMEM((ROWS, 128), BF)]
-        + [pltpu.VMEM(s, F32) for s in shapes[3:]]
-        + [pltpu.SemaphoreType.DMA((3,)), pltpu.SemaphoreType.DMA((9,))],
+        + [pltpu.VMEM(s, BF if n == 1 else F32) for n, s in enumerate(shapes)]
+        + [pltpu.SemaphoreType.DMA((6,)), pltpu.SemaphoreType.DMA((9,))],
         compiler_params=pltpu.CompilerParams(vmem_limit_bytes=60 * 2**20),
     )(logits, features, embed, g)
     outs = list(outs)

time: 93.6 us -> 68.6 us (0.73)
  Pallas kernels: 92.6 us -> 67.6 us
    pallas_call x1, Pallas kernels: 18.3 us -> 3.21 us  [write_out(): pl.pallas_call(out_kernel, out_shape=tuple((jax.ShapeDtypeStruct(s, BF if...]
    pallas_call x1, Pallas kernels: 74.3 us -> 64.4 us  [run_net(): pl.pallas_call(functools.partial(net_kernel, counts), out_shape=(jax.Shap...]
where the time goes in v5:
time: 68.6 us; the launch traced here: 68.4 us
  Pallas kernels  67.6 us (99%)
  between operations  0.81 us (1%)
    pallas_call x1, Pallas kernels, run_net(): pl.pallas_call(functools.partial(net_kernel, counts), out_shape=(jax.Shap...  64.4 us
    pallas_call x1, Pallas kernels, write_out(): pl.pallas_call(out_kernel, out_shape=tuple((jax.ShapeDtypeStruct(s, BF if...  3.21 us

profile of v5, /device:TPU:1, one launch (start us, length us, event | category | flops | bytes accessed | tf_op | source)
XLA Modules:
  0.0 68.4 jit_solution(10635635049668291985)
XLA Ops:
  0.6 64.4 %shard_map.214 = (f32[2,32,128]{2,1,0:T(8,128)}, bf16[64,32,128]{2,1,0:T(8,128)(2,1)}, f32[16,64]{1,0:T(8,128)}, bf16[6272,128]{1,0:T(8,128)(2,1)}) custom-call(s32[32,128]{1,0:T(8,128)} %refs_0_.1, bf16[16,64]{1,0:T(8,128)(2,1)} %bitcast.5, bf16[2,64]{1,0:T(2,128)(2,1)} %refs_2_.1, bf16[2,32,128]{2,1,0:T(8,128)(2,1)} %refs_3_.1, ...), custom_call_target="tpu_custom_call" | custom-call | tf_op jit(solution)/shard_map/pallas_call | solution.py:764
  65.0 3.2 %shard_map.215 = (f32[2,32,128]{2,1,0:T(8,128)}, bf16[64,32,128]{2,1,0:T(8,128)(2,1)}, f32[16,64]{1,0:T(8,128)}, f32[3,3,64,64]{3,2,1,0:T(8,128)}, f32[3,3,64,12...) custom-call(f32[2,32,128]{2,1,0:T(8,128)} %get-tuple-element.22.logi, ...), custom_call_target="tpu_custom_call" | custom-call | tf_op jit(solution)/shard_map/pallas_call | solution.py:828

commit v6 on v5

--- a/solution.py
+++ b/solution.py
@@ -142,14 +142,13 @@
     def take(n):
         return [next(it) for _ in range(n)]
 
-    syn, embt, rdo, cot, eye, cQ, cU = take(7)
-    afar = take(8)
+    afar = take(15)
     logits_out, features_out, embed_ref, grads_out = take(4)
     xb, e0, z0, z1, f1, e1, z2, f2, e2, z3, e3, z4, e4, z5, f5, t5, t4, t3, t2, t1, fg, cp = take(22)
     w0, w1, w1b, w2, w2b, w3, w3b, w4, w4b, w5, w5b, r4, r4t = take(13)
     halos = [take(2) for _ in WIDTHS]
-    near = take(8)
-    k1, cS, k2t, k3, k5, k4, cQ2, cF = near
+    near = take(15)
+    syn, cU, cot, cQ, eye, embt, rdo, k1, cS, k2t, k3, k5, k4, cQ2, cF = near
     far, wide2, loads, logits_ref, features_ref, stores = take(6)
     sends, recvs = take(2)
     g_ref, whole, tall = take(3)
@@ -171,6 +170,17 @@
     def place(dr, dc):
         return {"row": (row + dr + n_row) % n_row, "col": (col + dc + n_col) % n_col}
 
+    storing = []
+
+    def store(source, target):
+        storing.append(pltpu.make_async_copy(source, target, stores.at[len(storing)]))
+        storing[-1].start()
+
+    partners = [(d, 0) for d in range(1, n_row)] + [(0, d) for d in range(1, n_col)] + list(SIDES[:4])
+    barrier = pltpu.get_barrier_semaphore()
+    for partner in partners:
+        pl.semaphore_signal(barrier, inc=1, device_id=place(*partner), device_id_type=MESH)
+
     loading = {}
     for n, (source, target) in enumerate(zip(afar, near)):
         loading[id(target)] = pltpu.make_async_copy(source, target, loads.at[n])
@@ -179,17 +189,6 @@
     def loaded(*targets):
         for target in targets:
             loading[id(target)].wait()
-
-    storing = []
-
-    def store(source, target):
-        storing.append(pltpu.make_async_copy(source, target, stores.at[len(storing)]))
-        storing[-1].start()
-
-    partners = [(d, 0) for d in range(1, n_row)] + [(0, d) for d in range(1, n_col)] + list(SIDES[:4])
-    barrier = pltpu.get_barrier_semaphore()
-    for partner in partners:
-        pl.semaphore_signal(barrier, inc=1, device_id=place(*partner), device_id_type=MESH)
 
     lane = lax.broadcasted_iota(jnp.int32, (1, 128), 1)
     sixteen = lax.broadcasted_iota(jnp.int32, (16, 1), 0)
@@ -257,16 +256,27 @@
         return tiles
 
     def extend(p, width, ref, size):
+        sides = {}
         for ea in range(p + 2):
             for eb in range(p + 2):
-                dr, dc = (ea > p) - (ea < 1), (eb > p) - (eb < 1)
-                if (dr, dc) == (0, 0):
-                    continue
-                start = (((ea - 1) % p + 1) * (p + 2) + (eb - 1) % p + 1) * width
-                at = (dr * 3 + dc + 4) * EXT
-                moved = mm(ref[start : start + width, :], cS[at : at + EXT, 0:size])
-                start = (ea * (p + 2) + eb) * width
-                ref[start : start + width, 0:size] = moved.astype(BF)
+                way = (ea > p) - (ea < 1), (eb > p) - (eb < 1)
+                if way != (0, 0):
+                    source = (((ea - 1) % p + 1) * (p + 2) + (eb - 1) % p + 1) * width
+                    sides.setdefault(way, []).append((source, (ea * (p + 2) + eb) * width))
+        for (dr, dc), spots in sides.items():
+            at = (dr * 3 + dc + 4) * EXT
+            many = len(spots) * width
+            first, target = spots[0]
+            if dc == 0:
+                held = ref[first : first + many, :]
+            else:
+                held = jnp.concatenate([ref[i : i + width, :] for i, _ in spots], axis=0)
+            moved = mm(held, cS[at : at + EXT, 0:size]).astype(BF)
+            if dc == 0:
+                ref[target : target + many, 0:size] = moved
+            else:
+                for n, (_, target) in enumerate(spots):
+                    ref[target : target + width, 0:size] = moved[n * width : (n + 1) * width, :]
 
     core, n_x = row % 2, n_row // 2
     ways = {
@@ -338,6 +348,7 @@
             copy.start()
         flying["embed"] = copies
 
+    loaded(syn, cU)
     bit = lax.broadcasted_iota(jnp.int32, (16, 1), 0)
     groups = []
     for a in range(4):
@@ -351,6 +362,7 @@
             for b in range(4):
                 start = ((a + 1) * 6 + b + 1) * 16
                 xb[start : start + 16, t * 128 : (t + 1) * 128] = phased[(a * 2 + t) * 16 : (a * 2 + t + 1) * 16, b * 128 : (b + 1) * 128]
+    loaded(cot)
     wide = cot[...].astype(F32)
     groups = []
     for a in range(4):
@@ -364,6 +376,7 @@
             pieces = [phased[start : start + 4, b * 128 : (b + 1) * 128] for b in range(4)]
             cp[a * 16 : (a + 1) * 16, t * 128 : (t + 1) * 128] = jnp.concatenate(pieces, axis=0).astype(BF)
 
+    loaded(cQ)
     inner = [((a + 1) * 6 + 1) * 16 for a in range(4)]
     pieces = [jnp.concatenate([xb[i : i + 64, 0:CELLS] for i in inner], axis=0), cp[:, 0:CELLS]]
     copies = begin(0, 1, pieces, lambda: pl.semaphore_wait(barrier, len(partners)))
@@ -435,7 +448,7 @@
         r4[...] = jnp.where(own, tiled, 0.0).astype(BF)
         r4t[...] = nt(eye[...], r4[...]).astype(BF)
 
-    loaded(k1)
+    loaded(eye, embt, rdo, k1)
     arrange_first()
     arrange_readout()
     loaded(cS)
@@ -727,7 +740,7 @@
     syn, emb, k1, k2, *rest = args
     k3, k4, k5, rdo, cot = rest
     eye, pick, pick_far, spread, near, far = [jnp.asarray(t, BF) for t in (np.eye(CELLS), PICK, PICK_FAR, SPREAD, SHIFT, SHIFT_FAR)]
-    afar = (k1, near, k2.transpose(0, 1, 3, 2), k3, k5, k4, pick_far, far)
+    afar = (syn, spread, cot, pick, eye, emb.T, rdo, k1, near, k2.transpose(0, 1, 3, 2), k3, k5, k4, pick_far, far)
     wide, own = (EXT,), (CELLS,)
     blocks = [(16 * 36,) + wide, (64 * 36,) + wide, (1024,) + own, (1024,) + wide, (1024,) + wide, (1024,) + wide]
     blocks += [(512,) + wide, (512,) + wide, (128 * 9,) + wide, (256,) + own, (256 * 9,) + wide, (512,) + wide, (128 * 16,) + wide]
@@ -737,8 +750,8 @@
     scratch = [pltpu.VMEM(s, BF) for s in blocks + weights]
     for width, depth in WIDTHS:
         scratch += [pltpu.VMEM((bounds(depth)[3] + 16, width), BF), pltpu.VMEM((128 * depth + 64, width), BF)]
-    scratch += [pltpu.VMEM(x.shape, BF) for x in afar]
-    scratch += [pltpu.VMEM((256, 512), BF), pltpu.VMEM((128, 512), BF), pltpu.SemaphoreType.DMA((8,)), pltpu.VMEM((2, 32, 128), F32), pltpu.VMEM((64, 32, 128), BF)]
+    scratch += [pltpu.VMEM(x.shape, x.dtype) for x in afar]
+    scratch += [pltpu.VMEM((256, 512), BF), pltpu.VMEM((128, 512), BF), pltpu.SemaphoreType.DMA((15,)), pltpu.VMEM((2, 32, 128), F32), pltpu.VMEM((64, 32, 128), BF)]
     scratch += [pltpu.SemaphoreType.DMA((2 + len(PARTS),))]
     scratch += [pltpu.SemaphoreType.DMA((len(WIDTHS), 8)), pltpu.SemaphoreType.DMA((len(WIDTHS), 8))]
     scratch += [pltpu.VMEM((ROWS, 128), F32), pltpu.VMEM((ROWS, 128), BF), pltpu.VMEM((64, 32, 128), F32)]
@@ -769,55 +782,63 @@
             jax.ShapeDtypeStruct((16, 64), F32),
             jax.ShapeDtypeStruct((ROWS, 128), BF),
         ),
-        in_specs=[vmem] * 7 + [hbm] * 8,
+        in_specs=[hbm] * 15,
         out_specs=(hbm, hbm, vmem, hbm),
         scratch_shapes=scratch,
         compiler_params=pltpu.CompilerParams(collective_id=1, has_side_effects=True, vmem_limit_bytes=56 * 2**20),
-    )(syn, emb.T, rdo, cot, eye, pick, spread, *afar)
+    )(*afar)
 
 
 def out_kernel(logits, features, embed, grads, *refs):
     outs, (g, passed, mids, loads, stores) = refs[:9], (refs[9], refs[10:13], refs[13:19], refs[19], refs[20])
-    spans = ((0, AT_BOTTOM), (AT_BOTTOM, AT_SECOND), (AT_SECOND, ROWS))
-    pulls = [pltpu.make_async_copy(grads.at[a:b], g.at[a:b], loads.at[n]) for n, (a, b) in enumerate(spans)]
-    for copy in pulls:
-        copy.start()
-    through = [pltpu.make_async_copy(x, passed[n], loads.at[3 + n]) for n, x in enumerate((logits, features, embed))]
-    for copy in through:
-        copy.start()
-    pushes = [pltpu.make_async_copy(passed[n], outs[n], stores.at[n]) for n in range(3)]
-
-    def push(n):
-        pushes.append(pltpu.make_async_copy(mids[n - 3], outs[n], stores.at[n]))
+    pulls, pushes = [], []
+
+    def pull(source, target):
+        pulls.append(pltpu.make_async_copy(source, target, loads.at[len(pulls)]))
+        pulls[-1].start()
+        return pulls[-1]
+
+    def push(source, target):
+        pushes.append(pltpu.make_async_copy(source, target, stores.at[len(pushes)]))
         pushes[-1].start()
 
     m_first, m_second, m_bottom, m_return, m_final, m_read = mids
-    pulls[0].wait()
+    o_first, o_second, o_bottom, o_return, o_final, o_read = outs[3:]
+    by_return = [pull(grads.at[n * 768 : (n + 1) * 768], g.at[n * 768 : (n + 1) * 768]) for n in range(3)]
+    spots = [AT_BOTTOM + n * 768 for n in range(3)]
+    by_bottom = [pull(grads.at[i : i + 768], g.at[i : i + 768]) for i in spots]
+    through = [pull(features.at[n * 16 : (n + 1) * 16], passed[1].at[n * 16 : (n + 1) * 16]) for n in range(4)]
+    tail = [pull(grads.at[AT_FINAL:AT_BOTTOM], g.at[AT_FINAL:AT_BOTTOM]), pull(grads.at[AT_SECOND:ROWS], g.at[AT_SECOND:ROWS])]
+    small = [pull(logits, passed[0]), pull(embed, passed[2])]
+    for ta in range(3):
+        by_return[ta].wait()
+        for tb in range(3):
+            for half in range(2):
+                start = AT_RETURN + ((ta * 3 + tb) * 2 + half) * 128
+                m_return[ta, tb, :, half * 128 : (half + 1) * 128] = g[start : start + 128, :].astype(F32)
+        push(m_return.at[ta], o_return.at[ta])
+    for ta in range(3):
+        by_bottom[ta].wait()
+        for tb in range(3):
+            start = AT_BOTTOM + (ta * 3 + tb) * 256
+            m_bottom[ta, tb] = g[start : start + 256, :].astype(F32)
+        push(m_bottom.at[ta], o_bottom.at[ta])
+    for n in range(4):
+        through[n].wait()
+        push(passed[1].at[n * 16 : (n + 1) * 16], outs[1].at[n * 16 : (n + 1) * 16])
+    for copy in tail:
+        copy.wait()
     for t in range(9):
         ta, tb = t // 3, t % 3
-        for half in range(2):
-            start = AT_RETURN + (t * 2 + half) * 128
-            m_return[ta, tb, :, half * 128 : (half + 1) * 128] = g[start : start + 128, :].astype(F32)
         m_final[ta, tb] = g[AT_FINAL + t * 64 : AT_FINAL + (t + 1) * 64, :].astype(F32)
-    push(6)
-    push(7)
-    for pull, copy in zip(through, pushes):
-        pull.wait()
-        copy.start()
-    pulls[1].wait()
-    for t in range(9):
-        m_bottom[t // 3, t % 3] = g[AT_BOTTOM + t * 256 : AT_BOTTOM + (t + 1) * 256, :].astype(F32)
-    push(5)
-    pulls[2].wait()
-    for t in range(9):
-        ta, tb = t // 3, t % 3
         m_second[ta, tb] = g[AT_SECOND + t * 64 : AT_SECOND + (t + 1) * 64, :].astype(F32)
         start, low = (AT_FIRST + ta * 64, tb * 64) if tb < 2 else (AT_FIRST + (192 if ta < 2 else 256), ta % 2 * 64)
         m_first[ta, tb] = g[start : start + 64, low : low + 64].astype(F32)
     m_read[...] = g[AT_READ : AT_READ + 16, 0:64].astype(F32)[0:2]
-    push(3)
-    push(4)
-    push(8)
+    for copy in small:
+        copy.wait()
+    for source, target in ((m_final, o_final), (m_second, o_second), (m_first, o_first), (m_read, o_read), (passed[0], outs[0]), (passed[2], outs[2])):
+        push(source, target)
     for copy in pushes:
         copy.wait()
 
@@ -832,7 +853,7 @@
         out_specs=(hbm,) * 9,
         scratch_shapes=[pltpu.VMEM((ROWS, 128), BF)]
         + [pltpu.VMEM(s, BF if n == 1 else F32) for n, s in enumerate(shapes)]
-        + [pltpu.SemaphoreType.DMA((6,)), pltpu.SemaphoreType.DMA((9,))],
+        + [pltpu.SemaphoreType.DMA((14,)), pltpu.SemaphoreType.DMA((16,))],
         compiler_params=pltpu.CompilerParams(vmem_limit_bytes=60 * 2**20),
     )(logits, features, embed, g)
     outs = list(outs)

time: 68.6 us -> 66.7 us (0.972)
  Pallas kernels: 67.6 us -> 65.7 us
    pallas_call x1, Pallas kernels: 64.4 us -> 62.7 us  [run_net(): pl.pallas_call(functools.partial(net_kernel, counts), out_shape=(jax.Shap...]
where the time goes in v6:
time: 66.7 us; the launch traced here: 66.6 us
  Pallas kernels  65.7 us (99%)
  between operations  0.81 us (1%)
    pallas_call x1, Pallas kernels, run_net(): pl.pallas_call(functools.partial(net_kernel, counts), out_shape=(jax.Shap...  62.7 us
    pallas_call x1, Pallas kernels, write_out(): pl.pallas_call(out_kernel, out_shape=tuple((jax.ShapeDtypeStruct(s, BF if...  3.08 us

profile of v6, /device:TPU:1, one launch (start us, length us, event | category | flops | bytes accessed | tf_op | source)
XLA Modules:
  0.0 66.6 jit_solution(4574116560737583623)
XLA Ops:
  0.6 62.7 %shard_map.214 = (f32[2,32,128]{2,1,0:T(8,128)}, bf16[64,32,128]{2,1,0:T(8,128)(2,1)}, f32[16,64]{1,0:T(8,128)}, bf16[6272,128]{1,0:T(8,128)(2,1)}) custom-call(s32[32,128]{1,0:T(8,128)} %refs_0_.1, bf16[512,512]{1,0:T(8,128)(2,1)} %constant.15.clone.refs_1_, bf16[2,32,128]{2,1,0:T(8,128)(2,1)} %refs_2_.1, bf16[112,256]{1,0:T(8,128)(2,1)} %constant.13.clone.refs_3_, ...), custom_call_target="tpu_custom_call" | custom-call | tf_op jit(solution)/shard_map/pallas_call | solution.py:777
  63.3 3.1 %shard_map.215 = (f32[2,32,128]{2,1,0:T(8,128)}, bf16[64,32,128]{2,1,0:T(8,128)(2,1)}, f32[16,64]{1,0:T(8,128)}, f32[3,3,64,64]{3,2,1,0:T(8,128)}, f32[3,3,64,12...) custom-call(f32[2,32,128]{2,1,0:T(8,128)} %get-tuple-element.22.logi, ...), custom_call_target="tpu_custom_call" | custom-call | tf_op jit(solution)/shard_map/pallas_call | solution.py:849

commit v7 on v6

--- a/solution.py
+++ b/solution.py
@@ -451,6 +451,8 @@
     loaded(eye, embt, rdo, k1)
     arrange_first()
     arrange_readout()
+    loaded(k2t)
+    arrange_second()
     loaded(cS)
     end(0, 1, copies)
     (tile,) = ring(0, 1, 0, 256)
@@ -483,8 +485,6 @@
             start = ((a + 1) * 4 + b + 1) * 64
             e1[start : start + 64, :] = pooled(f1, 4, 64, a, b, EXT)
     extend(2, 64, e1, CELLS)
-    loaded(k2t)
-    arrange_second()
 
     for a in range(2):
         v = sum(mm(w2[:, ta * 256 : (ta + 1) * 256], e1[(a + ta) * 256 : (a + ta + 1) * 256, 0:CELLS]) for ta in range(3))
@@ -602,9 +602,9 @@
     g_ref[AT_READ:ROWS, :] = jnp.zeros((ROWS - AT_READ, 128), F32)
     g_ref[AT_READ : AT_READ + 4, 0:64] = total
 
-    end(3, 1, copies)
     sum_step(0, 1)
     sum_step(1, 1)
+    end(3, 1, copies)
     for a in range(2):
         start = ((a + 1) * 4 + 1) * 128
         t4[start : start + 256, CELLS:EXT] = ring(3, 1, a * 256, 256)[0]
@@ -712,20 +712,20 @@
     sum_step(4, 2)
     lay(0)
     lay(1)
-    sum_step(5, 2)
     sum_step(2, 3)
     sum_step(3, 3)
+    sum_step(5, 2)
+    lay(2)
+    lay(3)
     sum_step(0, 4)
     sum_step(1, 4)
-    lay(2)
-    lay(3)
     embed_step(1)
     features_ref[...] = tall[...].astype(BF)
     store(features_ref, features_out)
     sum_step(4, 3)
-    sum_step(5, 3)
     sum_step(2, 4)
     sum_step(3, 4)
+    sum_step(5, 3)
     embed_ref[...] = embed_step(2)
     for part in (0, 1, 4, 2, 3, 5):
         sum_step(part, 5)

time: 66.7 us -> 66.9 us (level); the launches traced: 66.6 us -> 65.7 us
  Pallas kernels: 65.7 us -> 64.8 us
    pallas_call x1, Pallas kernels: 62.7 us -> 61.8 us  [run_net(): pl.pallas_call(functools.partial(net_kernel, counts), out_shape=(jax.Shap...]
where the time goes in v7:
time: 66.9 us; the launch traced here: 65.7 us
  Pallas kernels  64.8 us (97%)
  between operations  0.81 us (1%)
    pallas_call x1, Pallas kernels, run_net(): pl.pallas_call(functools.partial(net_kernel, counts), out_shape=(jax.Shap...  61.8 us
    pallas_call x1, Pallas kernels, write_out(): pl.pallas_call(out_kernel, out_shape=tuple((jax.ShapeDtypeStruct(s, BF if...  3.08 us

profile of v7, /device:TPU:1, one launch (start us, length us, event | category | flops | bytes accessed | tf_op | source)
XLA Modules:
  0.0 65.7 jit_solution(14091206299729783823)
XLA Ops:
  0.6 61.8 %shard_map.214 = (f32[2,32,128]{2,1,0:T(8,128)}, bf16[64,32,128]{2,1,0:T(8,128)(2,1)}, f32[16,64]{1,0:T(8,128)}, bf16[6272,128]{1,0:T(8,128)(2,1)}) custom-call(s32[32,128]{1,0:T(8,128)} %refs_0_.1, bf16[512,512]{1,0:T(8,128)(2,1)} %constant.15.clone.refs_1_, bf16[2,32,128]{2,1,0:T(8,128)(2,1)} %refs_2_.1, bf16[112,256]{1,0:T(8,128)(2,1)} %constant.13.clone.refs_3_, ...), custom_call_target="tpu_custom_call" | custom-call | tf_op jit(solution)/shard_map/pallas_call | solution.py:777
  62.4 3.1 %shard_map.215 = (f32[2,32,128]{2,1,0:T(8,128)}, bf16[64,32,128]{2,1,0:T(8,128)(2,1)}, f32[16,64]{1,0:T(8,128)}, f32[3,3,64,64]{3,2,1,0:T(8,128)}, f32[3,3,64,12...) custom-call(f32[2,32,128]{2,1,0:T(8,128)} %get-tuple-element.22.logi, ...), custom_call_target="tpu_custom_call" | custom-call | tf_op jit(solution)/shard_map/pallas_call | solution.py:849

commit v8 on v7

--- a/solution.py
+++ b/solution.py
@@ -669,8 +669,6 @@
                     start = ((fa + 1) * 6 + fb + 1) * 64
                     n = (fa * 4 + fb) * 64
                     t1[start : start + 64, :] = sloped(fenced(t5[start : start + 64, :].astype(F32) + v[b * 64 : (b + 1) * 64, :]), z1[n : n + 64, :])
-    sum_step(2, 2)
-    sum_step(3, 2)
     for ta in range(3):
         product = 0.0
         for a in range(4):
@@ -684,6 +682,8 @@
         g_ref[start : start + 64, ta % 2 * 64 : ta % 2 * 64 + 64] = value[:, 128:192]
     g_ref[AT_FIRST + 256 : AT_FIRST + 320, 64:128] = jnp.zeros((64, 64), F32)
     sum_step(5, 1)
+    sum_step(2, 2)
+    sum_step(3, 2)
     sum_step(0, 3)
     sum_step(1, 3)
     extend(4, 64, t1, CELLS)

time: 66.9 us -> 67.1 us (level); the launches traced: 65.7 us -> 66.5 us
  Pallas kernels: 64.8 us -> 65.7 us
    pallas_call x1, Pallas kernels: 61.8 us -> 62.6 us  [run_net(): pl.pallas_call(functools.partial(net_kernel, counts), out_shape=(jax.Shap...]
where the time goes in v8:
time: 67.1 us; the launch traced here: 66.5 us
  Pallas kernels  65.7 us (98%)
  between operations  0.81 us (1%)
    pallas_call x1, Pallas kernels, run_net(): pl.pallas_call(functools.partial(net_kernel, counts), out_shape=(jax.Shap...  62.6 us
    pallas_call x1, Pallas kernels, write_out(): pl.pallas_call(out_kernel, out_shape=tuple((jax.ShapeDtypeStruct(s, BF if...  3.08 us

profile of v8, /device:TPU:1, one launch (start us, length us, event | category | flops | bytes accessed | tf_op | source)
XLA Modules:
  0.0 66.5 jit_solution(8687185796123308553)
XLA Ops:
  0.6 62.6 %shard_map.214 = (f32[2,32,128]{2,1,0:T(8,128)}, bf16[64,32,128]{2,1,0:T(8,128)(2,1)}, f32[16,64]{1,0:T(8,128)}, bf16[6272,128]{1,0:T(8,128)(2,1)}) custom-call(s32[32,128]{1,0:T(8,128)} %refs_0_.1, bf16[512,512]{1,0:T(8,128)(2,1)} %constant.15.clone.refs_1_, bf16[2,32,128]{2,1,0:T(8,128)(2,1)} %refs_2_.1, bf16[112,256]{1,0:T(8,128)(2,1)} %constant.13.clone.refs_3_, ...), custom_call_target="tpu_custom_call" | custom-call | tf_op jit(solution)/shard_map/pallas_call | solution.py:777
  63.3 3.1 %shard_map.215 = (f32[2,32,128]{2,1,0:T(8,128)}, bf16[64,32,128]{2,1,0:T(8,128)(2,1)}, f32[16,64]{1,0:T(8,128)}, f32[3,3,64,64]{3,2,1,0:T(8,128)}, f32[3,3,64,12...) custom-call(f32[2,32,128]{2,1,0:T(8,128)} %get-tuple-element.22.logi, ...), custom_call_target="tpu_custom_call" | custom-call | tf_op jit(solution)/shard_map/pallas_call | solution.py:849
